TPU v7x, 32 devices: a whole 2x2x4 slice. The times are simulated.
32 devices in a mesh: groups: 2 (over y), rep: 4 (over z), fsdp: 2 (over x), tp: 2 (over core).
Axes of the slice: x: 2, y: 2, z: 4, core: 2. Of those that a mesh axis runs over, the one named last changes fastest.
Arguments:
- tokens: bfloat16 [10240, 5120], P(('groups', 'rep', 'fsdp'), 'tp'), parts along dimension 0, may hold values from -6 to 6
- norm_gain: bfloat16 [5120], replicated, may hold values from 0.099609375 to 1.8984375
- key_weight: bfloat16 [5120, 512], P('fsdp', 'tp'), may hold values from -0.078125 to 0.078125
- value_weight: bfloat16 [5120, 512], P('fsdp', 'tp'), may hold values from -0.078125 to 0.078125
- key_bias: bfloat16 [512], P('tp'), may hold values from -3 to 3
- value_bias: bfloat16 [512], P('tp'), may hold values from -3 to 3
- block_counts: int32 [16], P('groups'), parts along dimension 0, may hold values from 1 to 5, as said below
- positions: int32 [10240], P(('groups', 'rep', 'fsdp')), parts along dimension 0, may hold values from 0 to 32767
- dest_slots: int32 [10240], P(('groups', 'rep', 'fsdp')), parts along dimension 0, may hold values from -1 to 2047, as said below
Outputs:
- cache_keys: bfloat16 [4096, 512], P(('groups', 'rep', 'fsdp'), 'tp'), parts along dimension 0
- cache_values: bfloat16 [4096, 512], P(('groups', 'rep', 'fsdp'), 'tp'), parts along dimension 0
There are 2 independent parts, one for each index of `groups`. A program takes and returns all parts, laid end to end along the dimension named above; an argument that names none is the same for every part. Nothing has to cross between parts.
Inputs may be any that keep to these rules, and one draw needn't show every extreme that they name: `block_counts`: valid rows come first on each device. One device has 5 blocks, three have 1, all others 2. `dest_slots`: valid rows name distinct cache rows and every cache row is named once; cache rows k * 256 to (k + 1) * 256 - 1 belong to device k of the group; the rows of one device name at most 96 cache rows of one owner, and some device reaches it; padding rows hold -1.
All inputs are finite; a program needn't handle non-finite values.
Results may differ from a plain program's by a relative error of at most 0.0046.
Values may be sent and summed in bfloat16 or wider, within the bound.
No kernel may reach another device: no remote copies, remote signals or barrier semaphores. Data moves between devices by JAX's collectives and lax.ppermute only.
A program may use at most 64 MiB of HBM per device.

v0:
```python
import jax
import jax.numpy as jnp
from jax import lax
from jax.sharding import PartitionSpec as P

HEAD_DIM = 128
BLOCK = 128
HOT_BLOCKS = 5
OWN_DEV = 256


epsilon = 1e-05
rope_base = 1000000.0


def rotate(key_rows, positions, head_dim):
    row_count = key_rows.shape[0]
    head_view = key_rows.reshape(row_count, -1, head_dim)
    half_rot = head_dim // 4
    freq_index = jnp.arange(half_rot, dtype=jnp.float32)
    inverse = rope_base ** (-freq_index / half_rot)
    angles = positions.astype(jnp.float32)[:, None] * inverse[None, :]
    cosine = jnp.cos(angles)[:, None, :]
    sine_part = jnp.sin(angles)[:, None, :]
    first_half = head_view[..., :half_rot]
    second = head_view[..., half_rot : 2 * half_rot]
    tail_dims = head_view[..., 2 * half_rot :]
    turned = jnp.concatenate(
        [
            first_half * cosine - second * sine_part,
            second * cosine + first_half * sine_part,
            tail_dims,
        ],
        axis=-1,
    )
    return turned.reshape(row_count, -1)


def accumulate_with(normed, pieces):
    return (
        jnp.dot(normed, pieces[0], preferred_element_type=jnp.float32),
        jnp.dot(normed, pieces[1], preferred_element_type=jnp.float32),
    )


def project(half_rows, positions, norm_gain, key_weight, value_weight, key_bias, value_bias):
    whole = lax.all_gather(half_rows, "tp", axis=1, tiled=True)
    float_rows = whole.astype(jnp.float32)
    mean_square = jnp.mean(float_rows * float_rows, axis=-1, keepdims=True)
    normed = (float_rows * lax.rsqrt(mean_square + epsilon) * norm_gain.astype(jnp.float32)).astype(
        jnp.bfloat16
    )
    key_rows, values = accumulate_with(
        normed,
        (
            lax.all_gather(key_weight, "fsdp", axis=0, tiled=True),
            lax.all_gather(value_weight, "fsdp", axis=0, tiled=True),
        ),
    )
    key_rows = rotate(key_rows + key_bias.astype(jnp.float32), positions, HEAD_DIM)
    values = values + value_bias.astype(jnp.float32)
    return (key_rows, values)


def local(
    tokens,
    norm_gain,
    key_weight,
    value_weight,
    key_bias,
    value_bias,
    block_counts,
    positions,
    dest_slots,
):
    devices = lax.axis_size(("rep", "fsdp"))
    most_rows = (HOT_BLOCKS + 1) * (BLOCK // devices)
    owner_rows = OWN_DEV
    my_index = lax.axis_index(("rep", "fsdp"))
    local_index = jnp.arange(tokens.shape[0], dtype=jnp.int32)
    is_valid = (local_index < BLOCK * block_counts[my_index]) & (dest_slots >= 0)
    owner_index = jnp.where(is_valid, dest_slots // owner_rows, -1)
    slot_local = jnp.where(is_valid, dest_slots % owner_rows, -1)
    onehot = (owner_index[:, None] == jnp.arange(devices, dtype=jnp.int32)[None, :]).astype(
        jnp.int32
    )
    rank_in_slot = jnp.sum((jnp.cumsum(onehot, axis=0) - 1) * onehot, axis=1)
    capacity = devices * most_rows
    target = jnp.where(is_valid, owner_index * most_rows + rank_in_slot, capacity)
    marker = slot_local.astype(jnp.bfloat16)
    column_count = key_weight.shape[1]
    key_rows, values = project(
        tokens, positions, norm_gain, key_weight, value_weight, key_bias, value_bias
    )
    send_keys = (
        jnp.zeros((capacity, column_count), jnp.bfloat16)
        .at[target]
        .set(key_rows.astype(jnp.bfloat16), mode="drop")
    )
    send_values = (
        jnp.zeros((capacity, column_count), jnp.bfloat16)
        .at[target]
        .set(values.astype(jnp.bfloat16), mode="drop")
    )
    send_marks = jnp.full((capacity,), -1.0, jnp.bfloat16).at[target].set(marker, mode="drop")
    got_keys, got_values, got_marks = (
        lax.all_to_all(send_keys, ("rep", "fsdp"), split_axis=0, concat_axis=0, tiled=True),
        lax.all_to_all(send_values, ("rep", "fsdp"), split_axis=0, concat_axis=0, tiled=True),
        lax.all_to_all(send_marks, ("rep", "fsdp"), split_axis=0, concat_axis=0, tiled=True),
    )
    placement = jnp.where(got_marks >= 0, got_marks.astype(jnp.int32), owner_rows)
    cache_keys = (
        jnp.zeros((owner_rows, column_count), jnp.bfloat16).at[placement].set(got_keys, mode="drop")
    )
    cache_values = (
        jnp.zeros((owner_rows, column_count), jnp.bfloat16)
        .at[placement]
        .set(got_values, mode="drop")
    )
    return (cache_keys, cache_values)


def solution(mesh):
    return jax.shard_map(
        local,
        mesh=mesh,
        in_specs=(
            P(("groups", "rep", "fsdp"), "tp"),
            P(),
            P("fsdp", "tp"),
            P("fsdp", "tp"),
            P("tp"),
            P("tp"),
            P("groups"),
            P(("groups", "rep", "fsdp")),
            P(("groups", "rep", "fsdp")),
        ),
        out_specs=(P(("groups", "rep", "fsdp"), "tp"), P(("groups", "rep", "fsdp"), "tp")),
        check_vma=False,
    )
```

profile of v0, /device:TPU:0, one launch (start us, length us, event | category | flops | bytes accessed | tf_op | source)
XLA Modules:
  0.0 156.4 jit_solution(10783711096227529081)
XLA Ops:
  7.2 0.0 all-gather.4.cloned.1.call-start
  7.2 0.7 all-gather.4.cloned.1.call-update
  7.9 0.0 all-gather.6.cloned.1.call-start
  7.9 0.7 all-gather.6.cloned.1.call-update
  8.6 0.0 all-gather.8.cloned.1.call-start
  8.7 0.7 all-gather.8.cloned.1.call-update
  9.4 1.2 dynamic_slice.3
  11.3 0.7 fusion.28
  12.0 1.4 reduce-window.6
  13.4 0.1 slice.21
  13.5 0.1 copy.16
  13.6 0.2 reduce-window.9
  13.8 0.1 copy.17
  13.9 0.1 fusion.24
  14.0 0.7 compare_select_fusion.2
  14.7 8.6 %scatter_custom_fusion = bf16[768]{0:T(1024)(128)(2,1)S(1)} fusion(s32[640]{0:T(1024)S(1)} %compare_select_fusion.2, bf16[640]{0:T(1024)(128)(2,1)S(1)} %get-tuple-element.6, bf16[]{:T(256)} %constant.30.clone.1), kind=kCustom, calls=%fused_computation.53 | custom fusion | bytes 1538 | tf_op jit(solution)/shard_map/scatter | solution.py:105
  23.3 0.7 all_to_all.30
  24.0 7.3 %all-to-all-start = ((bf16[8,96,1]{1,2,0:T(2,128)(2,1)}), bf16[8,96,1]{1,2,0:T(2,128)(2,1)S(1)}, u32[]{:S(2)}, u32[]{:S(2)}) async-start(bf16[8,96,1]{1,2,0:T(2,128)(2,1)} %all_to_all.30), calls=%async_computation | async-start | bytes 8192 | tf_op jit(solution)/shard_map/all_to_all | solution.py:109
  31.2 0.7 convert_element_type.48
  31.9 0.7 convert_element_type.50
  32.6 0.7 convert_element_type.51
  33.3 0.7 convert_element_type.53
  34.0 0.4 multiply_cosine_fusion
  34.3 0.0 all-gather.4.cloned.1.call-done
  34.4 4.2 %fusion = f32[640]{0:T(1024)S(1)} fusion(bf16[640,5120]{1,0:T(8,128)(2,1)} %all-gather.4.cloned.1.call-done), kind=kLoop, calls=%fused_computation.7 | loop fusion | flops 9829760 | bytes 6556160 | tf_op jit(solution)/shard_map/reduce_sum | solution.py:49
  38.6 32.6 %all-gather.6.cloned.1.call-done = bf16[5120,256]{1,0:T(8,128)(2,1)} async-done(((bf16[2560,256]{1,0:T(8,128)(2,1)}), bf16[5120,256]{1,0:T(8,128)(2,1)}) %all-gather.6.cloned.1.call-update) | async-done | bytes 2621456 | tf_op jit(solution)/shard_map/all_gather | solution.py:56
  71.2 6.1 %fusion.7 = f32[640,256]{0,1:T(8,128)S(1)} fusion(bf16[5120,256]{1,0:T(8,128)(2,1)} %all-gather.6.cloned.1.call-done, bf16[640,5120]{1,0:T(8,128)(2,1)} %all-gather.4.cloned.1.call-done, f32[5120]{0:T(1024)S(1)} %convert_element_type.48, f32[640]{0:T(1024)S(1)} %add_rsqrt_fusion, f32[256]{0:T(256)S(1)} %convert_element_type.50), kind=kOutput, calls=%fused_computation.12 | convolution fusion | flops 1690992640 | bytes 9854464 | tf_op jit(solution)/shard_map/dot_general | solution.py:41
  77.4 0.2 copy.20
  77.6 6.1 %scatter_custom_fusion.1 = bf16[768,256]{1,0:T(8,128)(2,1)} fusion(s32[640]{0:T(1024)S(1)} %compare_select_fusion.2, bf16[640,256]{1,0:T(8,128)(2,1)S(1)} %copy.20, bf16[]{:T(256)} %constant.29.clone.1), kind=kCustom, calls=%fused_computation.19 | custom fusion | bytes 393218 | tf_op jit(solution)/shard_map/scatter | solution.py:98
  83.7 0.0 all-to-all-done
  83.7 4.6 %all-to-all-start.1 = ((bf16[8,96,256]{2,1,0:T(8,128)(2,1)}), bf16[8,96,256]{2,1,0:T(8,128)(2,1)S(1)}, u32[]{:S(2)}, u32[]{:S(2)}) async-start(bf16[8,96,256]{2,1,0:T(8,128)(2,1)} %bitcast.7), calls=%async_computation.1 | async-start | bytes 786432 | tf_op jit(solution)/shard_map/all_to_all | solution.py:107
  88.3 27.7 %all-gather.8.cloned.1.call-done = bf16[5120,256]{1,0:T(8,128)(2,1)} async-done(((bf16[2560,256]{1,0:T(8,128)(2,1)}), bf16[5120,256]{1,0:T(8,128)(2,1)}) %all-gather.8.cloned.1.call-update) | async-done | bytes 2621456 | tf_op jit(solution)/shard_map/all_gather | solution.py:57
  116.0 5.5 %fusion.13 = bf16[640,256]{1,0:T(8,128)(2,1)S(1)} fusion(bf16[5120,256]{1,0:T(8,128)(2,1)} %all-gather.8.cloned.1.call-done, bf16[640,5120]{1,0:T(8,128)(2,1)} %all-gather.4.cloned.1.call-done, f32[5120]{0:T(1024)S(1)} %convert_element_type.48, f32[640]{0:T(1024)S(1)} %add_rsqrt_fusion, f32[256]{0:T(256)S(1)} %convert_element_type.53), kind=kOutput, calls=%fused_computation.14 | convolution fusion | flops 1691156480 | bytes 9526784 | tf_op jit(solution)/shard_map/dot_general | solution.py:42
  121.6 6.1 %scatter_custom_fusion.3 = bf16[768,256]{1,0:T(8,128)(2,1)} fusion(s32[640]{0:T(1024)S(1)} %compare_select_fusion.2, bf16[640,256]{1,0:T(8,128)(2,1)S(1)} %fusion.13, bf16[]{:T(256)} %constant.29.clone.1), kind=kCustom, calls=%fused_computation.17 | custom fusion | bytes 393218 | tf_op jit(solution)/shard_map/scatter | solution.py:103
  127.7 0.0 all-to-all-done.1
  127.7 4.6 %all-to-all-start.2 = ((bf16[8,96,256]{2,1,0:T(8,128)(2,1)}), bf16[8,96,256]{2,1,0:T(8,128)(2,1)S(1)}, u32[]{:S(2)}, u32[]{:S(2)}) async-start(bf16[8,96,256]{2,1,0:T(8,128)(2,1)} %bitcast.9), calls=%async_computation.2 | async-start | bytes 786432 | tf_op jit(solution)/shard_map/all_to_all | solution.py:108
  132.3 0.1 select_n.63
  132.4 5.9 %scatter_custom_fusion.2 = bf16[256,256]{1,0:T(8,128)(2,1)} fusion(s32[768]{0:T(1024)S(1)} %fusion.32, bf16[768,256]{1,0:T(8,128)(2,1)S(1)} %bitcast.20, bf16[]{:T(256)} %constant.29.clone.1), kind=kCustom, calls=%fused_computation.27 | custom fusion | bytes 131074 | tf_op jit(solution)/shard_map/scatter | solution.py:113
  138.3 5.6 %all-to-all-done.2 = bf16[8,96,256]{2,1,0:T(8,128)(2,1)S(1)} async-done(((bf16[8,96,256]{2,1,0:T(8,128)(2,1)}), bf16[8,96,256]{2,1,0:T(8,128)(2,1)S(1)}, u32[]{:S(2)}, u32[]{:S(2)}) %all-to-all-start.2) | async-done | bytes 393248 | tf_op jit(solution)/shard_map/all_to_all | solution.py:108
  144.0 5.9 %scatter_custom_fusion.4 = bf16[256,256]{1,0:T(8,128)(2,1)} fusion(s32[768]{0:T(1024)S(1)} %fusion.32, bf16[768,256]{1,0:T(8,128)(2,1)S(1)} %bitcast.21, bf16[]{:T(256)} %constant.29.clone.1), kind=kCustom, calls=%fused_computation.25 | custom fusion | bytes 131074 | tf_op jit(solution)/shard_map/scatter | solution.py:118
  (8 shorter events, 0.2 us)
Async XLA Ops:
  7.2 27.2 %all-gather.4.cloned.1.call-start = ((), (), s32[]{:S(2)}) async-start(), calls=%async_computation.3 | async-start | bytes 9830400 | tf_op jit(solution)/shard_map/all_gather | solution.py:47
  7.9 63.3 %all-gather.6.cloned.1.call-start = ((), (), s32[]{:S(2)}) async-start(), calls=%async_computation.4 | async-start | bytes 3932160 | tf_op jit(solution)/shard_map/all_gather | solution.py:56
  8.6 107.4 %all-gather.8.cloned.1.call-start = ((), (), s32[]{:S(2)}) async-start(), calls=%async_computation.5 | async-start | bytes 3932160 | tf_op jit(solution)/shard_map/all_gather | solution.py:57
  24.0 59.8 %all-to-all-start = ((bf16[8,96,1]{1,2,0:T(2,128)(2,1)}), bf16[8,96,1]{1,2,0:T(2,128)(2,1)S(1)}, u32[]{:S(2)}, u32[]{:S(2)}) async-start(bf16[8,96,1]{1,2,0:T(2,128)(2,1)} %all_to_all.30), calls=%async_computation | async-start | bytes 8192 | tf_op jit(solution)/shard_map/all_to_all | solution.py:109
  83.7 43.9 %all-to-all-start.1 = ((bf16[8,96,256]{2,1,0:T(8,128)(2,1)}), bf16[8,96,256]{2,1,0:T(8,128)(2,1)S(1)}, u32[]{:S(2)}, u32[]{:S(2)}) async-start(bf16[8,96,256]{2,1,0:T(8,128)(2,1)} %bitcast.7), calls=%async_computation.1 | async-start | bytes 786432 | tf_op jit(solution)/shard_map/all_to_all | solution.py:107
  127.7 16.3 %all-to-all-start.2 = ((bf16[8,96,256]{2,1,0:T(8,128)(2,1)}), bf16[8,96,256]{2,1,0:T(8,128)(2,1)S(1)}, u32[]{:S(2)}, u32[]{:S(2)}) async-start(bf16[8,96,256]{2,1,0:T(8,128)(2,1)} %bitcast.9), calls=%async_computation.2 | async-start | bytes 786432 | tf_op jit(solution)/shard_map/all_to_all | solution.py:108
Sparse Core Ops, SparseCore 0:
  9.5 19.8 all-gather.3
  31.0 40.1 all-gather.5
  72.7 43.2 all-gather.7
where the time goes:
time: 157 us; the launch traced here: 156 us
  waiting for transfers between devices  68 us (43%)
  local copies, waits for them, and re-layouts  35.2 us (22%)
  starting transfers between devices  16.6 us (11%)
  between operations  14.5 us (9%)
  matrix products  11.6 us (7%)
  other arithmetic  10.5 us (7%)
    all_gather x1, waiting for transfers between devices, project(): lax.all_gather(key_weight, 'fsdp', axis=0, tiled=True)  32.6 us
    all_gather x1, waiting for transfers between devices, project(): lax.all_gather(value_weight, 'fsdp', axis=0, tiled=True)  27.7 us
    scatter x1, local copies, waits for them, and re-layouts, local(): jnp.full((capacity,), -1.0, jnp.bfloat16).at[target]  8.61 us
    all_to_all x1, starting transfers between devices, local(): lax.all_to_all(send_marks, ('rep', 'fsdp'), split_axis=0, concat_axis=0,...  7.25 us
    scatter x1, local copies, waits for them, and re-layouts, local(): send_keys = jnp.zeros((capacity, column_count), jnp.bfloat16).at[target]....  6.13 us
    dot_general x1, matrix products, accumulate_with(): jnp.dot(normed, pieces[0], preferred_element_type=jnp.float32)  6.09 us
    scatter x1, local copies, waits for them, and re-layouts, local(): send_values = jnp.zeros((capacity, column_count), jnp.bfloat16).at[target...  6.09 us
    scatter x1, local copies, waits for them, and re-layouts, local(): jnp.zeros((owner_rows, column_count), jnp.bfloat16).at[placement]  5.95 us
  transfers between devices with their start and end apart: 6, of which 3 were waited for; matrix products, arithmetic and copies ran while one was open for 32% of the time, Pallas kernels for 0%

commit v1 on v0

v1 whole, which is shorter than its diff:
```python
import functools

import jax
import jax.numpy as jnp
from jax import lax
from jax.experimental import pallas as pl
from jax.experimental.pallas import tpu as pltpu
from jax.sharding import PartitionSpec as P

HEAD_DIM = 128
BLOCK = 128
HOT_BLOCKS = 5
OWN_DEV = 256


epsilon = 1e-05
rope_base = 1000000.0
VMEM_BYTES = 48 * 1024 * 1024


def rotary_tables(positions):
    half_rot = HEAD_DIM // 4
    freq_index = jnp.arange(half_rot, dtype=jnp.float32)
    inverse = rope_base ** (-freq_index / half_rot)
    angles = positions.astype(jnp.float32)[:, None] * inverse[None, :]
    cosine = jnp.cos(angles)
    sine = jnp.sin(angles)
    rest = jnp.zeros((positions.shape[0], HEAD_DIM - 2 * half_rot), jnp.float32)
    straight = jnp.concatenate([cosine, cosine, rest + 1.0], axis=1)
    crossed = jnp.concatenate([-sine, sine, rest], axis=1)
    return straight, crossed


def norm_kernel(half_ref, own_ref, got_ref, gain_ref, out_ref):
    half = half_ref[0]
    width = own_ref.shape[1]
    own = own_ref[...].astype(jnp.float32)
    got = got_ref[...].astype(jnp.float32)
    total = jnp.sum(own * own, axis=1, keepdims=True) + jnp.sum(got * got, axis=1, keepdims=True)
    scale = lax.rsqrt(total / (2 * width) + epsilon)
    out_ref[:, :width] = (own * scale * gain_ref[half].astype(jnp.float32)).astype(jnp.bfloat16)
    out_ref[:, width:] = (got * scale * gain_ref[1 - half].astype(jnp.float32)).astype(jnp.bfloat16)


def normalize(half, own, got, norm_gain):
    rows, width = own.shape
    step = 128
    return pl.pallas_call(
        norm_kernel,
        out_shape=jax.ShapeDtypeStruct((rows, 2 * width), jnp.bfloat16),
        grid_spec=pltpu.PrefetchScalarGridSpec(
            num_scalar_prefetch=1,
            grid=(rows // step,),
            in_specs=[
                pl.BlockSpec((step, width), lambda i, half: (i, 0)),
                pl.BlockSpec((step, width), lambda i, half: (i, 0)),
                pl.BlockSpec((2, 1, width), lambda i, half: (0, 0, 0)),
            ],
            out_specs=pl.BlockSpec((step, 2 * width), lambda i, half: (i, 0)),
        ),
        compiler_params=pltpu.CompilerParams(vmem_limit_bytes=VMEM_BYTES),
        name="normalize",
    )(half.reshape(1), own, got, norm_gain.reshape(2, 1, width))


def near_kernel(place_ref, normed_ref, key_ref, value_ref, bias_ref, keys_ref, values_ref):
    rows = normed_ref[...]
    keys_ref[...] = (
        jnp.dot(rows, key_ref[...], preferred_element_type=jnp.float32) + bias_ref[0:1, :]
    )
    values_ref[...] = (
        jnp.dot(rows, value_ref[...], preferred_element_type=jnp.float32) + bias_ref[1:2, :]
    )


def near_part(place, normed, key_weight, value_weight, key_bias, value_bias):
    rows = normed.shape[0]
    depth, columns = key_weight.shape
    step = 128
    bias = jnp.stack([key_bias, value_bias]).astype(jnp.float32)
    out = jax.ShapeDtypeStruct((rows, columns), jnp.float32)
    return pl.pallas_call(
        near_kernel,
        out_shape=(out, out),
        grid_spec=pltpu.PrefetchScalarGridSpec(
            num_scalar_prefetch=1,
            grid=(rows // step,),
            in_specs=[
                pl.BlockSpec((step, depth), lambda i, place: (i, place[0])),
                pl.BlockSpec((depth, columns), lambda i, place: (0, 0)),
                pl.BlockSpec((depth, columns), lambda i, place: (0, 0)),
                pl.BlockSpec((2, columns), lambda i, place: (0, 0)),
            ],
            out_specs=(
                pl.BlockSpec((step, columns), lambda i, place: (i, 0)),
                pl.BlockSpec((step, columns), lambda i, place: (i, 0)),
            ),
        ),
        compiler_params=pltpu.CompilerParams(vmem_limit_bytes=VMEM_BYTES),
        name="near_part",
    )(place.reshape(1), normed, key_weight, value_weight, bias)


def far_kernel(turn, count, places_ref, normed_ref, near_ref, *refs):
    pieces = refs[:count]
    if turn:
        straight_ref, crossed_ref, pick_ref, out_ref = refs[count:]
    else:
        pick_ref, out_ref = refs[count:]
    total = near_ref[...]
    for index, piece in enumerate(pieces):
        depth = piece.shape[0]
        start = pl.multiple_of(places_ref[index] * depth, depth)
        total += jnp.dot(
            normed_ref[:, pl.ds(start, depth)], piece[...], preferred_element_type=jnp.float32
        )
    if turn:
        half_rot = HEAD_DIM // 4
        straight = straight_ref[...]
        crossed = crossed_ref[...]
        lane = lax.broadcasted_iota(jnp.int32, straight.shape, 1)
        heads = []
        for head in range(total.shape[1] // HEAD_DIM):
            part = total[:, head * HEAD_DIM : (head + 1) * HEAD_DIM]
            partner = jnp.where(
                lane < half_rot,
                pltpu.roll(part, HEAD_DIM - half_rot, 1),
                pltpu.roll(part, half_rot, 1),
            )
            heads.append(part * straight + partner * crossed)
        total = jnp.concatenate(heads, axis=1)
    rows = total.astype(jnp.bfloat16)
    out_ref[...] = jnp.dot(pick_ref[...], rows, preferred_element_type=jnp.float32).astype(
        jnp.bfloat16
    )


def far_part(places, normed, near, pieces, tables, pick):
    columns = near.shape[1]
    vmem = pl.BlockSpec(memory_space=pltpu.VMEM)
    operands = (normed, near, *pieces, *tables, pick)
    return pl.pallas_call(
        functools.partial(far_kernel, bool(tables), len(pieces)),
        out_shape=jax.ShapeDtypeStruct((pick.shape[0], columns), jnp.bfloat16),
        in_specs=[pl.BlockSpec(memory_space=pltpu.SMEM)] + [vmem] * len(operands),
        out_specs=vmem,
        compiler_params=pltpu.CompilerParams(vmem_limit_bytes=VMEM_BYTES),
        name="far_part",
    )(places, *operands)


def local(
    tokens,
    norm_gain,
    key_weight,
    value_weight,
    key_bias,
    value_bias,
    block_counts,
    positions,
    dest_slots,
):
    axes = ("rep", "fsdp")
    devices = lax.axis_size(axes)
    most_rows = (HOT_BLOCKS + 1) * (BLOCK // devices)
    capacity = devices * most_rows
    my_index = lax.axis_index(axes)
    rows, width = tokens.shape
    depth = key_weight.shape[0]
    shards = lax.axis_size("fsdp")
    half = lax.axis_index("tp")
    shard = lax.axis_index("fsdp")

    def place_of(first, size):
        which = first // width
        return (jnp.where(which == half, 0, width) + first % width) // size

    got = lax.ppermute(tokens, "tp", [(0, 1), (1, 0)])

    quarter = depth // 4
    relayed = (
        shards == 2
        and lax.axis_size("groups") == 2
        and lax.axis_size("rep") % 2 == 0
        and depth % 4 == 0
        and quarter % 128 == 0
    )
    if relayed:
        group = lax.axis_index("groups")
        odd = lax.axis_index("rep") % 2
        swap = [(0, 1), (1, 0)]
        across = [(i, i ^ 1) for i in range(lax.axis_size("rep"))]
        mine = 2 * group + odd
        last = 3 - mine
        far_first = (1 - shard) * depth

        def pieces_of(weight):
            own = lax.ppermute(
                lax.dynamic_slice_in_dim(weight, mine * quarter, quarter), "fsdp", swap
            )
            opposite = lax.ppermute(
                lax.dynamic_slice_in_dim(weight, last * quarter, quarter), "fsdp", swap
            )
            by_group = lax.ppermute(own, "groups", swap)
            by_rep = lax.ppermute(own, "rep", across)
            return own, by_group, by_rep, opposite

        numbers = (mine, 2 * (1 - group) + odd, 2 * group + 1 - odd, last)
        places = jnp.stack([place_of(far_first + n * quarter, quarter) for n in numbers])
        key_pieces = pieces_of(key_weight)
        value_pieces = pieces_of(value_weight)
    else:
        steps = range(1, shards)

        def pieces_of(weight):
            return tuple(
                lax.ppermute(weight, "fsdp", [(i, (i + k) % shards) for i in range(shards)])
                for k in steps
            )

        places = jnp.stack([place_of(((shard - k) % shards) * depth, depth) for k in steps])
        key_pieces = pieces_of(key_weight)
        value_pieces = pieces_of(value_weight)

    local_index = jnp.arange(rows, dtype=jnp.int32)
    is_valid = (local_index < BLOCK * block_counts[my_index]) & (dest_slots >= 0)
    owner_index = jnp.where(is_valid, dest_slots // OWN_DEV, -1)
    slot_local = jnp.where(is_valid, dest_slots % OWN_DEV, -1)
    onehot = (owner_index[:, None] == jnp.arange(devices, dtype=jnp.int32)[None, :]).astype(
        jnp.int32
    )
    rank_in_slot = jnp.sum((jnp.cumsum(onehot, axis=0) - 1) * onehot, axis=1)
    target = jnp.where(is_valid, owner_index * most_rows + rank_in_slot, capacity)
    hit = jnp.arange(capacity, dtype=jnp.int32)[:, None] == target[None, :]
    pick = hit.astype(jnp.bfloat16)
    marks = jnp.max(jnp.where(hit, slot_local[None, :], -1), axis=1).astype(jnp.bfloat16)
    got_marks = lax.all_to_all(marks, axes, split_axis=0, concat_axis=0, tiled=True)
    put = (
        jnp.arange(OWN_DEV, dtype=jnp.int32)[:, None] == got_marks.astype(jnp.int32)[None, :]
    ).astype(jnp.bfloat16)
    tables = rotary_tables(positions)

    normed = normalize(half, tokens, got, norm_gain)
    near_keys, near_values = near_part(
        place_of(shard * depth, depth), normed, key_weight, value_weight, key_bias, value_bias
    )
    outs = []
    for near, pieces, turn in (
        (near_keys, key_pieces, tables),
        (near_values, value_pieces, ()),
    ):
        send = far_part(places, normed, near, pieces, turn, pick)
        came = lax.all_to_all(send, axes, split_axis=0, concat_axis=0, tiled=True)
        outs.append(
            jnp.dot(put, came, preferred_element_type=jnp.float32).astype(jnp.bfloat16)
        )
    return tuple(outs)


def solution(mesh):
    return jax.shard_map(
        local,
        mesh=mesh,
        in_specs=(
            P(("groups", "rep", "fsdp"), "tp"),
            P(),
            P("fsdp", "tp"),
            P("fsdp", "tp"),
            P("tp"),
            P("tp"),
            P("groups"),
            P(("groups", "rep", "fsdp")),
            P(("groups", "rep", "fsdp")),
        ),
        out_specs=(P(("groups", "rep", "fsdp"), "tp"), P(("groups", "rep", "fsdp"), "tp")),
        check_vma=False,
    )
```

time: 157 us -> 94.6 us (0.60)
  waiting for transfers between devices: 68 us -> 24.3 us
  local copies, waits for them, and re-layouts: 35.2 us -> 8.46 us
  Pallas kernels: 0 us -> 24.3 us
  between operations: 14.5 us -> 1.42 us
  starting transfers between devices: 16.6 us -> 26.4 us
  matrix products: 11.6 us -> 2.86 us
  other arithmetic: 10.5 us -> 6.01 us
    all_gather x3 -> x0, waiting for transfers between devices: 60.3 us -> none  [the longest x1 32.6 us: project(): lax.all_gather(key_weight, 'fsdp', axis=0, tiled=True)]
    scatter x5 -> x0, local copies, waits for them, and re-layouts: 32.7 us -> none  [the longest x1 8.61 us: local(): jnp.full((capacity,), -1.0, jnp.bfloat16).at[target]]
    pallas_call x0 -> x4, Pallas kernels: none -> 24.3 us  [the longest x2 11.8 us: far_part(): pl.pallas_call(functools.partial(far_kernel, bool(tables), len(pieces)),...]
    ppermute x0 -> x9, waiting for transfers between devices: none -> 17.1 us  [the longest x2 11.9 us: pieces_of(): lax.ppermute(lax.dynamic_slice_in_dim(weight, mine * quarter, quarter), '...]
    ppermute x0 -> x9, starting transfers between devices: none -> 11.2 us  [the longest x2 4.63 us: pieces_of(): lax.ppermute(lax.dynamic_slice_in_dim(weight, mine * quarter, quarter), '...]
    dot_general x2, matrix products: 11.6 us -> 2.86 us  [local(): jnp.dot(put, came, preferred_element_type=jnp.float32).astype(jnp.bfloat16)]
    reduce_sum x1 -> x0, other arithmetic: 4.21 us -> none  [project(): mean_square = jnp.mean(float_rows * float_rows, axis=-1, keepdims=True)]
    unnamed x0 -> x12, local copies, waits for them, and re-layouts: none -> 2.79 us
  transfers between devices with their start and end apart: 6 -> 12, of which waited for: 3 -> 5; matrix products, arithmetic and copies ran while one was open for 32% -> 15% of each run, Pallas kernels for 0% -> 26%
where the time goes in v1:
time: 94.6 us; the launch traced here: 93.8 us
  starting transfers between devices  26.4 us (28%)
  waiting for transfers between devices  24.3 us (26%)
  Pallas kernels  24.3 us (26%)
  local copies, waits for them, and re-layouts  8.46 us (9%)
  other arithmetic  6.01 us (6%)
  matrix products  2.86 us (3%)
  between operations  1.42 us (2%)
    ppermute x2, waiting for transfers between devices, pieces_of(): lax.ppermute(lax.dynamic_slice_in_dim(weight, mine * quarter, quarter), '...  11.9 us
    pallas_call x2, Pallas kernels, far_part(): pl.pallas_call(functools.partial(far_kernel, bool(tables), len(pieces)),...  11.8 us
    all_to_all x2, starting transfers between devices, local(): came = lax.all_to_all(send, axes, split_axis=0, concat_axis=0, tiled=True)  8.85 us
    pallas_call x1, Pallas kernels, normalize(): pl.pallas_call(norm_kernel, out_shape=jax.ShapeDtypeStruct((rows, 2 * wid...  7.6 us
    all_to_all x2, waiting for transfers between devices, local(): came = lax.all_to_all(send, axes, split_axis=0, concat_axis=0, tiled=True)  7.17 us
    all_to_all x1, starting transfers between devices, local(): lax.all_to_all(marks, axes, split_axis=0, concat_axis=0, tiled=True)  6.31 us
    pallas_call x1, Pallas kernels, near_part(): pl.pallas_call(near_kernel, out_shape=(out, out), grid_spec=pltpu.Prefetc...  4.89 us
    ppermute x2, starting transfers between devices, pieces_of(): lax.ppermute(lax.dynamic_slice_in_dim(weight, mine * quarter, quarter), '...  4.63 us
  transfers between devices with their start and end apart: 12, of which 5 were waited for; matrix products, arithmetic and copies ran while one was open for 15% of the time, Pallas kernels for 26%

profile of v1, /device:TPU:0, one launch (start us, length us, event | category | flops | bytes accessed | tf_op | source)
XLA Modules:
  0.0 93.8 jit_solution(3991799368082032888)
XLA Ops:
  0.6 0.5 collective-permute-start
  1.1 1.9 %constant_dynamic-slice_fusion.2 = (bf16[640,256]{1,0:T(8,128)(2,1)}, bf16[640,256]{1,0:T(8,128)(2,1)S(1)}) fusion(bf16[2560,256]{1,0:T(8,128)(2,1)} %key_ref.1, s32[]{:T(128)S(6)} %select_n.139, s32[]{:T(128)S(6)} %select_n.138), kind=kLoop, calls=%fused_computation.35 | loop fusion | bytes 1310728 | tf_op jit(solution)/shard_map/dynamic_slice | solution.py:202
  3.0 2.5 %collective-permute-start.1 = (bf16[640,256]{1,0:T(8,128)(2,1)S(1)}, bf16[640,256]{1,0:T(8,128)(2,1)S(1)}, u32[]{:S(2)}, u32[]{:S(2)}) collective-permute-start(bf16[640,256]{1,0:T(8,128)(2,1)S(1)} %get-tuple-element.9), channel_id=1, source_target_pairs={{0,2},{2,0},{1,3},{3,1},{4,6},{6,4},{5,7},{7,5},{8,10},{10,8},{9,1... | collective-permute-start | bytes 983048 | tf_op jit(solution)/shard_map/ppermute | solution.py:198
  5.6 0.0 collective-permute-start.4
  5.6 1.2 %dynamic_slice.15 = s32[1]{0:T(128)} dynamic-slice(s32[8]{0:T(128)} %param.15, s32[]{:T(128)S(6)} %select_n.110), dynamic_slice_sizes={1} | dynamic-slice | bytes 12 | tf_op jit(solution)/shard_map/dynamic_slice | solution.py:226
  7.5 0.7 fusion.7
  8.2 1.4 %reduce-window.6 = s32[8,5,128]{2,0,1:T(8,128)S(1)} reduce-window(s32[8,5,128]{2,0,1:T(8,128)S(1)} %fusion.5, s32[]{:T(128)} %constant.118.clone.1), window={size=1x1x128 pad=0_0x0_0x127_0}, to_apply=%region_0.1 | reduce-window | flops 650240 | bytes 40964 | tf_op jit(solution)/shard_map/reduce-window
  9.6 0.1 slice.8
  9.7 0.1 copy.20
  9.8 0.2 reduce-window.9
  10.0 0.1 copy.21
  10.1 0.1 fusion.4
  10.2 0.7 add_select_fusion.2
  10.9 0.0 copy-start.5
  10.9 0.3 select_reduce_fusion
  11.2 0.7 convert_element_type.55
  11.9 6.3 %all-to-all-start = ((bf16[8,96,1]{1,2,0:T(2,128)(2,1)}), bf16[8,96,1]{1,2,0:T(2,128)(2,1)S(1)}, u32[]{:S(2)}, u32[]{:S(2)}) async-start(bf16[8,96,1]{1,2,0:T(2,128)(2,1)} %convert_element_type.55), calls=%async_computation | async-start | bytes 8192 | tf_op jit(solution)/shard_map/all_to_all | solution.py:237
  18.2 0.7 stack.30
  18.9 0.7 stack.29
  19.5 0.7 convert_element_type.50
  20.2 0.1 pad.5.clone
  20.3 0.1 pad.2.clone
  20.4 0.3 fusion.refs_6_.refs_4_
  20.7 1.2 %fusion.3 = (f32[640,32]{1,0:T(8,128)S(1)}, f32[640,32]{1,0:T(8,128)S(1)}, f32[640,32]{1,0:T(8,128)S(1)}) fusion(f32[32]{0:T(128)S(1)} %multiply_power_fusion, f32[640]{0:T(1024)S(1)} %convert_element_type.50), kind=kLoop, calls=%fused_computation.12 | loop fusion | flops 40960 | bytes 248448 | tf_op jit(solution)/shard_map/neg | solution.py:30
  21.9 0.0 collective-permute-done.1.refs_0_
  22.0 1.6 %collective-permute-start.2 = (bf16[640,256]{1,0:T(8,128)(2,1)S(1)}, bf16[640,256]{1,0:T(8,128)(2,1)}, u32[]{:S(2)}, u32[]{:S(2)}) collective-permute-start(bf16[640,256]{1,0:T(8,128)(2,1)S(1)} %collective-permute-done.1.refs_0_), channel_id=1, source_target_pairs={{0,16},{16,0},{1,17},{17,1},{2,18},{18,2},{3,19},{19,3},{4,20},{20... | collective-permute-start | bytes 983048 | tf_op jit(solution)/shard_map/ppermute | solution.py:204
  23.5 2.0 %collective-permute-start.3 = (bf16[640,256]{1,0:T(8,128)(2,1)S(1)}, bf16[640,256]{1,0:T(8,128)(2,1)}, u32[]{:S(2)}, u32[]{:S(2)}) collective-permute-start(bf16[640,256]{1,0:T(8,128)(2,1)S(1)} %collective-permute-done.1.refs_0_), channel_id=1, source_target_pairs={{0,4},{4,0},{8,12},{12,8},{1,5},{5,1},{9,13},{13,9},{2,6},{6,2},{1... | collective-permute-start | bytes 983048 | tf_op jit(solution)/shard_map/ppermute | solution.py:205
  25.6 0.2 maximum_maximum_fusion
  25.8 0.1 pad_add_fusion.places_ref
  25.9 0.0 copy-done.5
  25.9 0.0 collective-permute-done.got_ref
  25.9 0.0 copy-start
  25.9 1.9 %copy-done = bf16[640,2560]{1,0:T(8,128)(2,1)S(1)} copy-done((bf16[640,2560]{1,0:T(8,128)(2,1)S(1)}, bf16[640,2560]{1,0:T(8,128)(2,1)}, u32[]{:S(2)}) %copy-start) | copy-done | bytes 3276824
  27.9 0.0 copy-start.1
  27.9 0.0 copy-start.2
  27.9 7.6 %normalize.1.normed_ref = bf16[640,5120]{1,0:T(8,128)(2,1)} custom-call(s32[1]{0:T(128)} %bitcast.9.half_ref, bf16[640,2560]{1,0:T(8,128)(2,1)S(1)} %copy-done, bf16[640,2560]{1,0:T(8,128)(2,1)} %collective-permute-done.got_ref, bf16[2,1,2560]{2,1,0:T(2,128)(2,1)S(1)} %reshape.71.gain_ref), custom_call_target="tpu_custom_call" | custom-call | tf_op jit(solution)/shard_map/normalize/pallas_call | solution.py:48
  35.5 0.0 copy-done.1
  35.5 0.0 copy-done.2
  35.5 4.9 %near_part.1 = (f32[640,256]{1,0:T(8,128)S(1)}, f32[640,256]{1,0:T(8,128)S(1)}) custom-call(s32[1]{0:T(128)} %bitcast.10.place_ref, bf16[640,5120]{1,0:T(8,128)(2,1)} %normalize.1.normed_ref, bf16[2560,256]{1,0:T(8,128)(2,1)S(1)} %copy-done.1, bf16[2560,256]{1,0:T(8,128)(2,1)S(1)} %copy-done.2, f32[2,256]{1,0:T(2,128)S(1)} %maximum_convert_fusion.bias_ref), custom_call_target="tpu_custom_call" | custom-call | tf_op jit(solution)/shard_map/near_part/pallas_call | solution.py:82
  40.4 0.0 copy-start.3
  40.4 0.8 copy-done.3
  41.2 0.0 collective-permute-done.4.refs_3_
  41.2 0.0 collective-permute-done.2.refs_1_
  41.2 0.0 collective-permute-done.3.refs_2_
  41.2 6.1 %far_part.2 = bf16[768,256]{1,0:T(8,128)(2,1)} custom-call(s32[4]{0:T(128)S(1)} %pad_add_fusion.places_ref, bf16[640,5120]{1,0:T(8,128)(2,1)} %normalize.1.normed_ref, f32[640,256]{1,0:T(8,128)S(1)} %get-tuple-element.4.near_ref, bf16[640,256]{1,0:T(8,128)(2,1)S(1)} %collective-permute-done.1.refs_0_, bf16[640,256]{1,0:T(8,128)(2,1)} %collective-permute-done.2.refs_1_, ...), custom_call_target="tpu_custom_call" | custom-call | tf_op jit(solution)/shard_map/far_part/pallas_call | solution.py:142
  47.3 0.0 copy-start.4
  47.3 0.0 all-to-all-done
  47.3 4.7 %all-to-all-start.1 = ((bf16[8,96,256]{2,1,0:T(8,128)(2,1)}), bf16[8,96,256]{2,1,0:T(8,128)(2,1)}, u32[]{:S(2)}, u32[]{:S(2)}) async-start(bf16[8,96,256]{2,1,0:T(8,128)(2,1)} %bitcast.11), calls=%async_computation.1 | async-start | bytes 786432 | tf_op jit(solution)/shard_map/all_to_all | solution.py:253
  52.0 2.1 %collective-permute-start.5 = (bf16[640,256]{1,0:T(8,128)(2,1)S(1)}, bf16[640,256]{1,0:T(8,128)(2,1)S(1)}, u32[]{:S(2)}, u32[]{:S(2)}) collective-permute-start(bf16[640,256]{1,0:T(8,128)(2,1)S(1)} %get-tuple-element.7), channel_id=1, source_target_pairs={{0,2},{2,0},{1,3},{3,1},{4,6},{6,4},{5,7},{7,5},{8,10},{10,8},{9,1... | collective-permute-start | bytes 983048 | tf_op jit(solution)/shard_map/ppermute | solution.py:198
  54.1 0.1 collective-permute-start.8
  54.2 11.9 %collective-permute-done.5.refs_0_ = bf16[640,256]{1,0:T(8,128)(2,1)S(1)} collective-permute-done((bf16[640,256]{1,0:T(8,128)(2,1)S(1)}, bf16[640,256]{1,0:T(8,128)(2,1)S(1)}, u32[]{:S(2)}, u32[]{:S(2)}) %collective-permute-start.5) | collective-permute-done | bytes 327712 | tf_op jit(solution)/shard_map/ppermute | solution.py:198
  66.1 0.5 collective-permute-start.6
  66.6 1.9 %collective-permute-start.7 = (bf16[640,256]{1,0:T(8,128)(2,1)S(1)}, bf16[640,256]{1,0:T(8,128)(2,1)S(1)}, u32[]{:S(2)}, u32[]{:S(2)}) collective-permute-start(bf16[640,256]{1,0:T(8,128)(2,1)S(1)} %collective-permute-done.5.refs_0_), channel_id=1, source_target_pairs={{0,4},{4,0},{8,12},{12,8},{1,5},{5,1},{9,13},{13,9},{2,6},{6,2},{1... | collective-permute-start | bytes 983048 | tf_op jit(solution)/shard_map/ppermute | solution.py:205
  68.5 3.0 %collective-permute-done.8.refs_3_ = bf16[640,256]{1,0:T(8,128)(2,1)S(1)} collective-permute-done((bf16[640,256]{1,0:T(8,128)(2,1)S(1)}, bf16[640,256]{1,0:T(8,128)(2,1)S(1)}, u32[]{:S(2)}, u32[]{:S(2)}) %collective-permute-start.8) | collective-permute-done | bytes 327712 | tf_op jit(solution)/shard_map/ppermute | solution.py:201
  71.5 1.6 %collective-permute-done.6.refs_1_ = bf16[640,256]{1,0:T(8,128)(2,1)S(1)} collective-permute-done((bf16[640,256]{1,0:T(8,128)(2,1)S(1)}, bf16[640,256]{1,0:T(8,128)(2,1)S(1)}, u32[]{:S(2)}, u32[]{:S(2)}) %collective-permute-start.6) | collective-permute-done | bytes 327712 | tf_op jit(solution)/shard_map/ppermute | solution.py:204
  73.2 0.5 collective-permute-done.7.refs_2_
  73.7 0.0 copy-done.4
  73.7 5.8 %far_part.3 = bf16[768,256]{1,0:T(8,128)(2,1)} custom-call(s32[4]{0:T(128)S(1)} %pad_add_fusion.places_ref, bf16[640,5120]{1,0:T(8,128)(2,1)} %normalize.1.normed_ref, f32[640,256]{1,0:T(8,128)S(1)} %copy-done.4, bf16[640,256]{1,0:T(8,128)(2,1)S(1)} %collective-permute-done.5.refs_0_, bf16[640,256]{1,0:T(8,128)(2,1)S(1)} %collective-permute-done.6.refs_1_, ...), custom_call_target="tpu_custom_call" | custom-call | tf_op jit(solution)/shard_map/far_part/pallas_call | solution.py:142
  79.5 0.0 all-to-all-done.1
  79.5 4.2 %all-to-all-start.2 = ((bf16[8,96,256]{2,1,0:T(8,128)(2,1)}), bf16[8,96,256]{2,1,0:T(8,128)(2,1)S(1)}, u32[]{:S(2)}, u32[]{:S(2)}) async-start(bf16[8,96,256]{2,1,0:T(8,128)(2,1)} %bitcast.13), calls=%async_computation.2 | async-start | bytes 786432 | tf_op jit(solution)/shard_map/all_to_all | solution.py:253
  83.7 0.1 reshape.70
  83.7 1.9 %convolution_convert_fusion.1 = bf16[256,256]{1,0:T(8,128)(2,1)} fusion(bf16[768,256]{1,0:T(8,128)(2,1)} %bitcast.12, s32[768]{0:T(1024)S(1)} %reshape.70), kind=kOutput, calls=%fused_computation.4 | convolution fusion | flops 100925440 | bytes 527360 | tf_op jit(solution)/shard_map/dot_general | solution.py:255
  85.7 7.2 %all-to-all-done.2 = bf16[8,96,256]{2,1,0:T(8,128)(2,1)S(1)} async-done(((bf16[8,96,256]{2,1,0:T(8,128)(2,1)}), bf16[8,96,256]{2,1,0:T(8,128)(2,1)S(1)}, u32[]{:S(2)}, u32[]{:S(2)}) %all-to-all-start.2) | async-done | bytes 393248 | tf_op jit(solution)/shard_map/all_to_all | solution.py:253
  92.9 0.9 convolution_convert_fusion
  (9 shorter events, 0.1 us)
Async XLA Ops:
  0.6 25.3 %collective-permute-start = (bf16[640,2560]{1,0:T(8,128)(2,1)}, bf16[640,2560]{1,0:T(8,128)(2,1)}, u32[]{:S(2)}, u32[]{:S(2)}) collective-permute-start(bf16[640,2560]{1,0:T(8,128)(2,1)} %own_ref.1), channel_id=1, source_target_pairs={{0,1},{1,0},{2,3},{3,2},{4,5},{5,4},{6,7},{7,6},{8,9},{9,8},{10,11... | collective-permute-start | bytes 9830408 | tf_op jit(solution)/shard_map/ppermute | solution.py:178
  3.0 18.9 %collective-permute-start.1 = (bf16[640,256]{1,0:T(8,128)(2,1)S(1)}, bf16[640,256]{1,0:T(8,128)(2,1)S(1)}, u32[]{:S(2)}, u32[]{:S(2)}) collective-permute-start(bf16[640,256]{1,0:T(8,128)(2,1)S(1)} %get-tuple-element.9), channel_id=1, source_target_pairs={{0,2},{2,0},{1,3},{3,1},{4,6},{6,4},{5,7},{7,5},{8,10},{10,8},{9,1... | collective-permute-start | bytes 983048 | tf_op jit(solution)/shard_map/ppermute | solution.py:198
  5.6 35.7 %collective-permute-start.4 = (bf16[640,256]{1,0:T(8,128)(2,1)}, bf16[640,256]{1,0:T(8,128)(2,1)}, u32[]{:S(2)}, u32[]{:S(2)}) collective-permute-start(bf16[640,256]{1,0:T(8,128)(2,1)} %get-tuple-element.8), channel_id=1, source_target_pairs={{0,2},{2,0},{1,3},{3,1},{4,6},{6,4},{5,7},{7,5},{8,10},{10,8},{9,1... | collective-permute-start | bytes 983048 | tf_op jit(solution)/shard_map/ppermute | solution.py:201
  10.9 15.0 %copy-start.5 = (bf16[5120]{0:T(1024)(128)(2,1)S(1)}, bf16[5120]{0:T(1024)(128)(2,1)}, u32[]{:S(2)}) copy-start(bf16[5120]{0:T(1024)(128)(2,1)} %param.10) | copy-start | bytes 30724
  11.9 35.4 %all-to-all-start = ((bf16[8,96,1]{1,2,0:T(2,128)(2,1)}), bf16[8,96,1]{1,2,0:T(2,128)(2,1)S(1)}, u32[]{:S(2)}, u32[]{:S(2)}) async-start(bf16[8,96,1]{1,2,0:T(2,128)(2,1)} %convert_element_type.55), calls=%async_computation | async-start | bytes 8192 | tf_op jit(solution)/shard_map/all_to_all | solution.py:237
  22.0 19.3 %collective-permute-start.2 = (bf16[640,256]{1,0:T(8,128)(2,1)S(1)}, bf16[640,256]{1,0:T(8,128)(2,1)}, u32[]{:S(2)}, u32[]{:S(2)}) collective-permute-start(bf16[640,256]{1,0:T(8,128)(2,1)S(1)} %collective-permute-done.1.refs_0_), channel_id=1, source_target_pairs={{0,16},{16,0},{1,17},{17,1},{2,18},{18,2},{3,19},{19,3},{4,20},{20... | collective-permute-start | bytes 983048 | tf_op jit(solution)/shard_map/ppermute | solution.py:204
  23.5 17.7 %collective-permute-start.3 = (bf16[640,256]{1,0:T(8,128)(2,1)S(1)}, bf16[640,256]{1,0:T(8,128)(2,1)}, u32[]{:S(2)}, u32[]{:S(2)}) collective-permute-start(bf16[640,256]{1,0:T(8,128)(2,1)S(1)} %collective-permute-done.1.refs_0_), channel_id=1, source_target_pairs={{0,4},{4,0},{8,12},{12,8},{1,5},{5,1},{9,13},{13,9},{2,6},{6,2},{1... | collective-permute-start | bytes 983048 | tf_op jit(solution)/shard_map/ppermute | solution.py:205
  25.9 1.9 %copy-start = (bf16[640,2560]{1,0:T(8,128)(2,1)S(1)}, bf16[640,2560]{1,0:T(8,128)(2,1)}, u32[]{:S(2)}) copy-start(bf16[640,2560]{1,0:T(8,128)(2,1)} %own_ref.1) | copy-start | bytes 9830404
  27.9 7.6 %copy-start.1 = (bf16[2560,256]{1,0:T(8,128)(2,1)S(1)}, bf16[2560,256]{1,0:T(8,128)(2,1)}, u32[]{:S(2)}) copy-start(bf16[2560,256]{1,0:T(8,128)(2,1)} %key_ref.1) | copy-start | bytes 3932164
  27.9 7.6 %copy-start.2 = (bf16[2560,256]{1,0:T(8,128)(2,1)S(1)}, bf16[2560,256]{1,0:T(8,128)(2,1)}, u32[]{:S(2)}) copy-start(bf16[2560,256]{1,0:T(8,128)(2,1)} %value_ref.1) | copy-start | bytes 3932164
  40.4 0.9 copy-start.3
  47.3 26.4 %copy-start.4 = (f32[640,256]{1,0:T(8,128)S(1)}, f32[640,256]{1,0:T(8,128)}, u32[]{:S(2)}) copy-start(f32[640,256]{1,0:T(8,128)} %copy-done.3) | copy-start | bytes 1966084
  47.3 32.2 %all-to-all-start.1 = ((bf16[8,96,256]{2,1,0:T(8,128)(2,1)}), bf16[8,96,256]{2,1,0:T(8,128)(2,1)}, u32[]{:S(2)}, u32[]{:S(2)}) async-start(bf16[8,96,256]{2,1,0:T(8,128)(2,1)} %bitcast.11), calls=%async_computation.1 | async-start | bytes 786432 | tf_op jit(solution)/shard_map/all_to_all | solution.py:253
  52.0 14.1 %collective-permute-start.5 = (bf16[640,256]{1,0:T(8,128)(2,1)S(1)}, bf16[640,256]{1,0:T(8,128)(2,1)S(1)}, u32[]{:S(2)}, u32[]{:S(2)}) collective-permute-start(bf16[640,256]{1,0:T(8,128)(2,1)S(1)} %get-tuple-element.7), channel_id=1, source_target_pairs={{0,2},{2,0},{1,3},{3,1},{4,6},{6,4},{5,7},{7,5},{8,10},{10,8},{9,1... | collective-permute-start | bytes 983048 | tf_op jit(solution)/shard_map/ppermute | solution.py:198
  54.1 17.4 %collective-permute-start.8 = (bf16[640,256]{1,0:T(8,128)(2,1)S(1)}, bf16[640,256]{1,0:T(8,128)(2,1)S(1)}, u32[]{:S(2)}, u32[]{:S(2)}) collective-permute-start(bf16[640,256]{1,0:T(8,128)(2,1)S(1)} %get-tuple-element.6), channel_id=1, source_target_pairs={{0,2},{2,0},{1,3},{3,1},{4,6},{6,4},{5,7},{7,5},{8,10},{10,8},{9,1... | collective-permute-start | bytes 983048 | tf_op jit(solution)/shard_map/ppermute | solution.py:201
  66.1 7.1 %collective-permute-start.6 = (bf16[640,256]{1,0:T(8,128)(2,1)S(1)}, bf16[640,256]{1,0:T(8,128)(2,1)S(1)}, u32[]{:S(2)}, u32[]{:S(2)}) collective-permute-start(bf16[640,256]{1,0:T(8,128)(2,1)S(1)} %collective-permute-done.5.refs_0_), channel_id=1, source_target_pairs={{0,16},{16,0},{1,17},{17,1},{2,18},{18,2},{3,19},{19,3},{4,20},{20... | collective-permute-start | bytes 983048 | tf_op jit(solution)/shard_map/ppermute | solution.py:204
  66.6 7.1 %collective-permute-start.7 = (bf16[640,256]{1,0:T(8,128)(2,1)S(1)}, bf16[640,256]{1,0:T(8,128)(2,1)S(1)}, u32[]{:S(2)}, u32[]{:S(2)}) collective-permute-start(bf16[640,256]{1,0:T(8,128)(2,1)S(1)} %collective-permute-done.5.refs_0_), channel_id=1, source_target_pairs={{0,4},{4,0},{8,12},{12,8},{1,5},{5,1},{9,13},{13,9},{2,6},{6,2},{1... | collective-permute-start | bytes 983048 | tf_op jit(solution)/shard_map/ppermute | solution.py:205
  79.5 13.4 %all-to-all-start.2 = ((bf16[8,96,256]{2,1,0:T(8,128)(2,1)}), bf16[8,96,256]{2,1,0:T(8,128)(2,1)S(1)}, u32[]{:S(2)}, u32[]{:S(2)}) async-start(bf16[8,96,256]{2,1,0:T(8,128)(2,1)} %bitcast.13), calls=%async_computation.2 | async-start | bytes 786432 | tf_op jit(solution)/shard_map/all_to_all | solution.py:253

commit v2 on v0

v2 whole, which is shorter than its diff:
```python
import functools

import jax
import jax.numpy as jnp
from jax import lax
from jax.experimental import pallas as pl
from jax.experimental.pallas import tpu as pltpu
from jax.sharding import PartitionSpec as P

HEAD_DIM = 128
BLOCK = 128
HOT_BLOCKS = 5
OWN_DEV = 256


epsilon = 1e-05
rope_base = 1000000.0
VMEM_BYTES = 58 * 1024 * 1024
NEAR_STEP = 128
NEAR_CUTS = 4
NEAR_COST = 20_000_000_000
FAR_COST = 20_000_000_000


def ordered(*values):
    return lax.optimization_barrier(values)


def place_of(first, width):
    return jnp.where(first // width == lax.axis_index("tp"), 0, width) + first % width


def quarter_numbers():
    group = lax.axis_index("groups")
    odd = lax.rem(lax.axis_index("rep"), 2)
    return (2 * group + odd, 2 * (1 - group) + odd, 2 * group + 1 - odd, 3 - 2 * group - odd)


def far_places(relayed, depth, width):
    if relayed:
        return [number * (depth // 4) for number in quarter_numbers()]
    shards = lax.axis_size("fsdp")
    shard = lax.axis_index("fsdp")
    others = [lax.rem(shard + shards - k, shards) * depth for k in range(1, shards)]
    return [place_of(first, width) if depth != width else 0 for first in others]


def rotary_angles(positions):
    half_rot = HEAD_DIM // 4
    freq_index = jnp.arange(half_rot, dtype=jnp.float32)
    inverse = rope_base ** (-freq_index / half_rot)
    angles = inverse[:, None] * positions.astype(jnp.float32)[None, :]
    return jnp.cos(angles), jnp.sin(angles)


def cut_kernel(key_ref, value_ref, *refs):
    outs, sems = refs[:4], refs[4]
    quarter = outs[0].shape[0]
    mine = 2 * lax.axis_index("groups") + lax.rem(lax.axis_index("rep"), 2)
    copies = []
    for index, (source, which) in enumerate(
        ((key_ref, mine), (value_ref, mine), (key_ref, 3 - mine), (value_ref, 3 - mine))
    ):
        start = pl.multiple_of(which * quarter, quarter)
        copy = pltpu.make_async_copy(
            source.at[pl.ds(start, quarter), :], outs[index], sems.at[index]
        )
        copy.start()
        copies.append(copy)
    for copy in copies:
        copy.wait()


def cut_quarters(key_weight, value_weight):
    depth, columns = key_weight.shape
    piece = jax.ShapeDtypeStruct((depth // 4, columns), key_weight.dtype)
    return pl.pallas_call(
        cut_kernel,
        out_shape=(piece,) * 4,
        in_specs=[pl.BlockSpec(memory_space=pl.ANY)] * 2,
        out_specs=(pl.BlockSpec(memory_space=pltpu.VMEM),) * 4,
        scratch_shapes=[pltpu.SemaphoreType.DMA((4,))],
        compiler_params=pltpu.CompilerParams(vmem_limit_bytes=VMEM_BYTES),
        name="cut_quarters",
    )(key_weight, value_weight)


def near_kernel(whole, cuts, *refs):
    own_refs, got_refs = refs[:cuts], refs[cuts : 2 * cuts]
    gain_ref = refs[2 * cuts]
    key_refs, value_refs = refs[2 * cuts + 1 : 3 * cuts + 1], refs[3 * cuts + 1 : 4 * cuts + 1]
    key_bias_ref, value_bias_ref, keys_ref, values_ref, far_ref, normed_ref = refs[4 * cuts + 1 :]
    size, part_width = own_refs[0].shape
    width = cuts * part_width
    part_depth = key_refs[0].shape[0]
    depth = cuts * part_depth
    half = lax.axis_index("tp")
    lanes = 128
    squares = jnp.zeros((size, lanes), jnp.float32)
    for source in own_refs + got_refs:
        for first in range(0, part_width, lanes):
            part = source[:, first : first + lanes].astype(jnp.float32)
            squares += part * part
    total = jnp.sum(squares, axis=1, keepdims=True)
    scale = jnp.broadcast_to(lax.rsqrt(total / (2 * width) + epsilon), (size, lanes))
    for sources, side, which in ((own_refs, 0, half), (got_refs, width, 1 - half)):
        gain = gain_ref[pl.ds(pl.multiple_of(which * width, width), width)].astype(jnp.float32)
        gain = gain.reshape(1, width)
        for first in range(0, width, lanes):
            inner = first % part_width
            part = sources[first // part_width][:, inner : inner + lanes].astype(jnp.float32)
            normed_ref[:, side + first : side + first + lanes] = (
                part * scale * gain[:, first : first + lanes]
            ).astype(jnp.bfloat16)
    near_first = pl.multiple_of(place_of(lax.axis_index("fsdp") * depth, width), depth)
    for pieces, bias_ref, out_ref in (
        (key_refs, key_bias_ref, keys_ref),
        (value_refs, value_bias_ref, values_ref),
    ):
        sums = jnp.broadcast_to(
            bias_ref[...].astype(jnp.float32).reshape(1, out_ref.shape[1]), out_ref.shape
        )
        for index, piece in enumerate(pieces):
            start = pl.multiple_of(near_first + index * part_depth, part_depth)
            sums += jnp.dot(
                normed_ref[:, pl.ds(start, part_depth)],
                piece[...],
                preferred_element_type=jnp.float32,
            )
        out_ref[...] = sums
    if whole:
        far_ref[...] = normed_ref[...]
    else:
        far_ref[...] = normed_ref[:, pl.ds(pl.multiple_of(width - near_first, width), width)]


def near_part(own, got, norm_gain, key_weight, value_weight, key_bias, value_bias):
    rows, width = own.shape
    depth, columns = key_weight.shape
    whole = depth != width
    kept = 2 * width if whole else width
    cuts = NEAR_CUTS if depth % (128 * NEAR_CUTS) == 0 else 1
    step = NEAR_STEP
    sums = jax.ShapeDtypeStruct((rows, columns), jnp.float32)
    row_blocks = [
        pl.BlockSpec((step, width // cuts), lambda i, c=c: (i, c)) for c in range(cuts)
    ]
    weight_blocks = [
        pl.BlockSpec((depth // cuts, columns), lambda i, c=c: (c, 0)) for c in range(cuts)
    ]
    return pl.pallas_call(
        functools.partial(near_kernel, whole, cuts),
        out_shape=(sums, sums, jax.ShapeDtypeStruct((rows, kept), jnp.bfloat16)),
        grid=(rows // step,),
        in_specs=[
            *row_blocks,
            *row_blocks,
            pl.BlockSpec((2 * width,), lambda i: (0,)),
            *weight_blocks,
            *weight_blocks,
            pl.BlockSpec((columns,), lambda i: (0,)),
            pl.BlockSpec((columns,), lambda i: (0,)),
        ],
        out_specs=(
            pl.BlockSpec((step, columns), lambda i: (i, 0)),
            pl.BlockSpec((step, columns), lambda i: (i, 0)),
            pl.BlockSpec((step, kept), lambda i: (i, 0)),
        ),
        scratch_shapes=[pltpu.VMEM((step, 2 * width), jnp.bfloat16)],
        compiler_params=pltpu.CompilerParams(vmem_limit_bytes=VMEM_BYTES),
        cost_estimate=pl.CostEstimate(
            flops=NEAR_COST,
            bytes_accessed=6 * rows * width + 4 * depth * columns,
            transcendentals=0,
        ),
        name="near_part",
    )(
        *[own] * cuts,
        *[got] * cuts,
        norm_gain,
        *[key_weight] * cuts,
        *[value_weight] * cuts,
        key_bias,
        value_bias,
    )


def turned(total, straight, crossed):
    half_rot = HEAD_DIM // 4
    lane = lax.broadcasted_iota(jnp.int32, straight.shape, 1)
    heads = []
    for head in range(total.shape[1] // HEAD_DIM):
        part = total[:, head * HEAD_DIM : (head + 1) * HEAD_DIM]
        partner = jnp.where(
            lane < half_rot,
            pltpu.roll(part, HEAD_DIM - half_rot, 1),
            pltpu.roll(part, half_rot, 1),
        )
        heads.append(part * straight + partner * crossed)
    return jnp.concatenate(heads, axis=1)


def far_kernel(relayed, half_width, turn, extra, count, *refs):
    normed_ref, near_ref = refs[:2]
    pieces = refs[2 : 2 + count]
    rest = list(refs[2 + count :])
    rows_ref = rest.pop()
    out_ref = rest.pop()
    rest.pop()
    if turn:
        straight_ref, crossed_ref = rest.pop(0), rest.pop(0)
    pick_ref = rest.pop(0)
    step, total_steps = pl.program_id(0), pl.num_programs(0)
    size = near_ref.shape[0]
    total = near_ref[...]
    depth = pieces[0].shape[0]
    places = far_places(relayed, depth * 4 if relayed else depth, half_width)
    for piece, start in zip(pieces, places):
        start = pl.multiple_of(start, depth)
        total += jnp.dot(
            normed_ref[:, pl.ds(start, depth)], piece[...], preferred_element_type=jnp.float32
        )
    if turn:
        total = turned(total, straight_ref[...], crossed_ref[...])
    rows_ref[pl.ds(pl.multiple_of(step * size, size), size), :] = total.astype(jnp.bfloat16)

    @pl.when(step == total_steps - 1)
    def _():
        laid = jnp.dot(pick_ref[...], rows_ref[...], preferred_element_type=jnp.float32).astype(
            jnp.bfloat16
        )
        if extra:
            extra_ref = rest.pop(0)
            owners, tall, columns = out_ref.shape
            most_rows = tall - extra
            out_ref[:, :most_rows, :] = laid.reshape(owners, most_rows, columns)
            out_ref[:, most_rows:, :] = extra_ref[...]
        else:
            out_ref[...] = laid


def far_part(relayed, width, normed, near, pieces, tables, pick, extra, after):
    rows, columns = near.shape
    step = 320
    operands = [normed, near, *pieces, *tables, pick]
    specs = [
        pl.BlockSpec((step, normed.shape[1]), lambda i: (i, 0)),
        pl.BlockSpec((step, columns), lambda i: (i, 0)),
        *[pl.BlockSpec(piece.shape, lambda i: (0, 0)) for piece in pieces],
        *[pl.BlockSpec((step, HEAD_DIM), lambda i: (i, 0)) for _ in tables],
        pl.BlockSpec(pick.shape, lambda i: (0, 0)),
    ]
    tall = 0
    if extra is None:
        shape = (pick.shape[0], columns)
    else:
        owners, tall, _ = extra.shape
        shape = (owners, pick.shape[0] // owners + tall, columns)
        operands.append(extra)
        specs.append(pl.BlockSpec(extra.shape, lambda i: (0, 0, 0)))
    operands.append(after)
    specs.append(pl.BlockSpec(memory_space=pl.ANY))
    return pl.pallas_call(
        functools.partial(far_kernel, relayed, width, bool(tables), tall, len(pieces)),
        out_shape=jax.ShapeDtypeStruct(shape, jnp.bfloat16),
        grid=(rows // step,),
        in_specs=specs,
        out_specs=pl.BlockSpec(shape, lambda i: (0,) * len(shape)),
        scratch_shapes=[pltpu.VMEM((rows, columns), jnp.bfloat16)],
        compiler_params=pltpu.CompilerParams(vmem_limit_bytes=VMEM_BYTES),
        cost_estimate=pl.CostEstimate(
            flops=FAR_COST,
            bytes_accessed=2 * rows * normed.shape[1] + 6 * rows * columns,
            transcendentals=0,
        ),
        name="far_part",
    )(*operands)


def route_kernel(most_rows, counts_ref, dest_ref, cosine_ref, sine_ref, *refs):
    pick_ref, marks_ref, straight_ref, crossed_ref = refs[1:]
    me = lax.axis_index("rep") * lax.axis_size("fsdp") + lax.axis_index("fsdp")
    devices = marks_ref.shape[0]
    rows = dest_ref.shape[0]
    dest = dest_ref[...].reshape(1, rows)
    row = lax.broadcasted_iota(jnp.int32, (1, rows), 1)
    valid = (row < BLOCK * counts_ref[me]) & (dest >= 0)
    owner = jnp.where(valid, lax.div(dest, OWN_DEV), -1)
    slot = jnp.where(valid, lax.rem(dest, OWN_DEV), -1)
    tall = -(-devices // 16) * 16
    to_owner = lax.broadcasted_iota(jnp.int32, (tall, rows), 0) == owner
    ones = jnp.where(to_owner, 1.0, 0.0)
    earlier = jnp.where(
        lax.broadcasted_iota(jnp.int32, (rows, rows), 0)
        < lax.broadcasted_iota(jnp.int32, (rows, rows), 1),
        1.0,
        0.0,
    ).astype(jnp.bfloat16)
    before = jnp.dot(ones.astype(jnp.bfloat16), earlier, preferred_element_type=jnp.float32)
    rank = jnp.sum(ones * before, axis=0, keepdims=True).astype(jnp.int32)
    capacity = pick_ref.shape[0]
    target = jnp.where(valid, owner * most_rows + rank, capacity)
    pick_ref[...] = jnp.where(
        lax.broadcasted_iota(jnp.int32, (capacity, rows), 0) == target, 1.0, 0.0
    ).astype(jnp.bfloat16)
    at_rank = jnp.where(
        (lax.broadcasted_iota(jnp.int32, (marks_ref.shape[2], rows), 0) == rank) & valid, 1.0, 0.0
    ).astype(jnp.bfloat16)
    slots = jnp.where(to_owner, (slot + 1).astype(jnp.float32), 0.0).astype(jnp.bfloat16)
    marks = lax.dot_general(
        slots, at_rank, (((1,), (1,)), ((), ())), preferred_element_type=jnp.float32
    )
    marks = marks[:devices] - 1.0
    marks_ref[...] = jnp.broadcast_to(marks[:, None, :], marks_ref.shape).astype(jnp.bfloat16)
    cosine, sine = cosine_ref[...], sine_ref[...]
    rest = jnp.zeros((HEAD_DIM - 2 * cosine.shape[0], rows), jnp.float32)
    straight_ref[...] = jnp.concatenate([cosine, cosine, rest + 1.0], axis=0).T
    crossed_ref[...] = jnp.concatenate([-sine, sine, rest], axis=0).T


def route(block_counts, dest_slots, angles, devices, most_rows, columns, after):
    rows = dest_slots.shape[0]
    vmem = pl.BlockSpec(memory_space=pltpu.VMEM)
    return pl.pallas_call(
        functools.partial(route_kernel, most_rows),
        out_shape=(
            jax.ShapeDtypeStruct((devices * most_rows, rows), jnp.bfloat16),
            jax.ShapeDtypeStruct((devices, 16, columns), jnp.bfloat16),
            jax.ShapeDtypeStruct((rows, HEAD_DIM), jnp.float32),
            jax.ShapeDtypeStruct((rows, HEAD_DIM), jnp.float32),
        ),
        in_specs=[
            pl.BlockSpec(memory_space=pltpu.SMEM),
            vmem,
            vmem,
            vmem,
            pl.BlockSpec(memory_space=pl.ANY),
        ],
        out_specs=(vmem,) * 4,
        compiler_params=pltpu.CompilerParams(vmem_limit_bytes=VMEM_BYTES),
        name="route",
    )(block_counts, dest_slots, *angles, after)


def local(
    tokens,
    norm_gain,
    key_weight,
    value_weight,
    key_bias,
    value_bias,
    block_counts,
    positions,
    dest_slots,
):
    axes = ("rep", "fsdp")
    devices = lax.axis_size(axes)
    most_rows = (HOT_BLOCKS + 1) * (BLOCK // devices)
    capacity = devices * most_rows
    rows, width = tokens.shape
    depth = key_weight.shape[0]
    shards = lax.axis_size("fsdp")

    def exchange(rows_by_owner):
        return lax.all_to_all(rows_by_owner, axes, split_axis=0, concat_axis=0, tiled=True)

    got = lax.ppermute(tokens, "tp", [(0, 1), (1, 0)])

    near_keys, near_values, normed = near_part(
        tokens,
        got,
        norm_gain,
        key_weight,
        value_weight,
        key_bias,
        value_bias,
    )
    quarter = depth // 4
    relayed = (
        shards == 2
        and lax.axis_size("groups") == 2
        and lax.axis_size("rep") % 2 == 0
        and depth % 4 == 0
        and quarter % 128 == 0
    )
    if relayed:
        swap = [(0, 1), (1, 0)]
        across = [(i, i ^ 1) for i in range(lax.axis_size("rep"))]
        key_own, value_own, key_last, value_last = (
            lax.ppermute(piece, "fsdp", swap) for piece in cut_quarters(key_weight, value_weight)
        )

        key_own, near_values = ordered(key_own, near_values)

        def pieces_of(own, opposite):
            by_group = lax.ppermute(own, "groups", swap)
            by_rep = lax.ppermute(own, "rep", across)
            return own, by_group, by_rep, opposite

        key_pieces = pieces_of(key_own, key_last)
        value_pieces = pieces_of(value_own, value_last)
    else:
        steps = range(1, shards)

        def pieces_of(weight):
            return tuple(
                lax.ppermute(weight, "fsdp", [(i, (i + k) % shards) for i in range(shards)])
                for k in steps
            )

        key_pieces = pieces_of(key_weight)
        value_pieces = pieces_of(value_weight)

    columns = key_weight.shape[1]
    inline = most_rows % 16 == 0 and most_rows <= columns
    pick, marks, *tables = route(
        block_counts,
        dest_slots,
        rotary_angles(positions),
        devices,
        most_rows,
        columns,
        near_values,
    )
    if not inline:
        got_marks = exchange(marks[:, 0, :most_rows].reshape(capacity))
    send_keys = far_part(
        relayed,
        width,
        normed,
        near_keys,
        key_pieces,
        tables,
        pick,
        marks if inline else None,
        value_pieces[0],
    )
    came_keys = exchange(send_keys)
    send_values = far_part(
        relayed, width, normed, near_values, value_pieces, (), pick, None, send_keys
    )
    came_values = exchange(send_values)
    if inline:
        got_marks = came_keys[:, most_rows, :most_rows].reshape(capacity)
        came_keys = came_keys[:, :most_rows].reshape(capacity, columns)
    put = (
        jnp.arange(OWN_DEV, dtype=jnp.int32)[:, None] == got_marks.astype(jnp.int32)[None, :]
    ).astype(jnp.bfloat16)
    return tuple(
        jnp.dot(put, came, preferred_element_type=jnp.float32).astype(jnp.bfloat16)
        for came in (came_keys, came_values)
    )


def solution(mesh):
    return jax.shard_map(
        local,
        mesh=mesh,
        in_specs=(
            P(("groups", "rep", "fsdp"), "tp"),
            P(),
            P("fsdp", "tp"),
            P("fsdp", "tp"),
            P("tp"),
            P("tp"),
            P("groups"),
            P(("groups", "rep", "fsdp")),
            P(("groups", "rep", "fsdp")),
        ),
        out_specs=(P(("groups", "rep", "fsdp"), "tp"), P(("groups", "rep", "fsdp"), "tp")),
        check_vma=False,
    )
```

time: 157 us -> 74.6 us (0.48)
  waiting for transfers between devices: 68 us -> 18.4 us
  local copies, waits for them, and re-layouts: 35.2 us -> 4.24 us
  Pallas kernels: 0 us -> 26.1 us
  between operations: 14.5 us -> 0.75 us
  matrix products: 11.6 us -> 1.86 us
  other arithmetic: 10.5 us -> 1.76 us
  starting transfers between devices: 16.6 us -> 20.9 us
    all_gather x3 -> x0, waiting for transfers between devices: 60.3 us -> none  [the longest x1 32.6 us: project(): lax.all_gather(key_weight, 'fsdp', axis=0, tiled=True)]
    scatter x5 -> x0, local copies, waits for them, and re-layouts: 32.7 us -> none  [the longest x1 8.61 us: local(): jnp.full((capacity,), -1.0, jnp.bfloat16).at[target]]
    pallas_call x0 -> x5, Pallas kernels: none -> 26.1 us  [the longest x1 10.7 us: near_part(): pl.pallas_call(functools.partial(near_kernel, whole, cuts), out_shape=(su...]
    ppermute x0 -> x9, starting transfers between devices: none -> 12.4 us  [the longest x4 4.69 us: local(): lax.ppermute(piece, 'fsdp', swap)]
    all_to_all x3 -> x2, waiting for transfers between devices: 5.62 us -> 15.6 us  [exchange(): lax.all_to_all(rows_by_owner, axes, split_axis=0, concat_axis=0, tiled=True)]
    dot_general x2, matrix products: 11.6 us -> 1.86 us  [local(): jnp.dot(put, came, preferred_element_type=jnp.float32).astype(jnp.bfloat16)]
    all_to_all x3 -> x2, starting transfers between devices: 16.5 us -> 8.48 us  [exchange(): lax.all_to_all(rows_by_owner, axes, split_axis=0, concat_axis=0, tiled=True)]
    reduce_sum x2 -> x0, other arithmetic: 4.29 us -> none  [the longest x1 4.21 us: project(): mean_square = jnp.mean(float_rows * float_rows, axis=-1, keepdims=True)]
  transfers between devices with their start and end apart: 6 -> 11, of which waited for: 3 -> 3; matrix products, arithmetic and copies ran while one was open for 32% -> 4% of each run, Pallas kernels for 0% -> 35%
where the time goes in v2:
time: 74.6 us; the launch traced here: 74.1 us
  Pallas kernels  26.1 us (35%)
  starting transfers between devices  20.9 us (28%)
  waiting for transfers between devices  18.4 us (25%)
  local copies, waits for them, and re-layouts  4.24 us (6%)
  matrix products  1.86 us (2%)
  other arithmetic  1.76 us (2%)
  between operations  0.75 us (1%)
    all_to_all x2, waiting for transfers between devices, exchange(): lax.all_to_all(rows_by_owner, axes, split_axis=0, concat_axis=0, tiled=True)  15.6 us
    pallas_call x1, Pallas kernels, near_part(): pl.pallas_call(functools.partial(near_kernel, whole, cuts), out_shape=(su...  10.7 us
    pallas_call x2, Pallas kernels, far_part(): pl.pallas_call(functools.partial(far_kernel, relayed, width, bool(tables)...  10.2 us
    all_to_all x2, starting transfers between devices, exchange(): lax.all_to_all(rows_by_owner, axes, split_axis=0, concat_axis=0, tiled=True)  8.48 us
    ppermute x4, starting transfers between devices, local(): lax.ppermute(piece, 'fsdp', swap)  4.69 us
    unnamed x18, local copies, waits for them, and re-layouts  4.14 us
    ppermute x2, starting transfers between devices, pieces_of(): by_group = lax.ppermute(own, 'groups', swap)  4.02 us
    ppermute x2, starting transfers between devices, pieces_of(): by_rep = lax.ppermute(own, 'rep', across)  3.22 us
  transfers between devices with their start and end apart: 11, of which 3 were waited for; matrix products, arithmetic and copies ran while one was open for 4% of the time, Pallas kernels for 35%

profile of v2, /device:TPU:0, one launch (start us, length us, event | category | flops | bytes accessed | tf_op | source)
XLA Modules:
  0.0 74.1 jit_solution(2719085085256821881)
XLA Ops:
  0.6 0.5 collective-permute-start
  1.1 2.4 %cut_quarters.1 = (bf16[640,256]{1,0:T(8,128)(2,1)}, bf16[640,256]{1,0:T(8,128)(2,1)}, bf16[640,256]{1,0:T(8,128)(2,1)}, bf16[640,256]{1,0:T(8,128)(2,1)}) custom-call(bf16[2560,256]{1,0:T(8,128)(2,1)} %key_ref.1, bf16[2560,256]{1,0:T(8,128)(2,1)} %value_ref.1), custom_call_target="tpu_custom_call" | custom-call | tf_op jit(solution)/shard_map/cut_quarters/pallas_call | solution.py:77
  3.6 2.6 %collective-permute-start.1 = (bf16[640,256]{1,0:T(8,128)(2,1)}, bf16[640,256]{1,0:T(8,128)(2,1)S(1)}, u32[]{:S(2)}, u32[]{:S(2)}) collective-permute-start(bf16[640,256]{1,0:T(8,128)(2,1)} %get-tuple-element.17), channel_id=1, source_target_pairs={{0,2},{2,0},{1,3},{3,1},{4,6},{6,4},{5,7},{7,5},{8,10},{10,8},{9,1... | collective-permute-start | bytes 983048 | tf_op jit(solution)/shard_map/ppermute | solution.py:390
  6.2 0.1 collective-permute-start.4
  6.2 1.9 %collective-permute-start.5 = (bf16[640,256]{1,0:T(8,128)(2,1)}, bf16[640,256]{1,0:T(8,128)(2,1)S(1)}, u32[]{:S(2)}, u32[]{:S(2)}) collective-permute-start(bf16[640,256]{1,0:T(8,128)(2,1)} %get-tuple-element.26), channel_id=1, source_target_pairs={{0,2},{2,0},{1,3},{3,1},{4,6},{6,4},{5,7},{7,5},{8,10},{10,8},{9,1... | collective-permute-start | bytes 983048 | tf_op jit(solution)/shard_map/ppermute | solution.py:390
  8.2 0.1 collective-permute-start.8
  8.3 0.7 convert_element_type.20
  9.0 0.0 collective-permute-done.refs_4_.refs_5_.refs_6_.refs_7_
  9.0 0.0 copy-start
  9.0 1.7 %copy-done = bf16[640,2560]{1,0:T(8,128)(2,1)} copy-done((bf16[640,2560]{1,0:T(8,128)(2,1)}, bf16[640,2560]{1,0:T(8,128)(2,1)S(1)}, u32[]{:S(2)}) %copy-start) | copy-done | bytes 3276824
  10.7 10.7 %near_part.1 = (f32[640,256]{1,0:T(8,128)}, f32[640,256]{1,0:T(8,128)}, bf16[640,2560]{1,0:T(8,128)(2,1)}) custom-call(bf16[640,2560]{1,0:T(8,128)(2,1)} %refs_3_.1, bf16[640,2560]{1,0:T(8,128)(2,1)} %refs_3_.1, bf16[640,2560]{1,0:T(8,128)(2,1)} %refs_3_.1, bf16[640,2560]{1,0:T(8,128)(2,1)} %refs_3_.1, bf16[640,2560]{1,0:T(8,128)(2,1)} %copy-done, ...), custom_call_target="tpu_custom_call" | custom-call | flops 20000000000 | bytes 12451840 | tf_op jit(solution)/shard_map/near_part/pallas_call | solution.py:151
  21.5 0.0 collective-permute-done.1.refs_2_
  21.5 0.0 copy-start.3
  21.5 2.0 %collective-permute-start.2 = (bf16[640,256]{1,0:T(8,128)(2,1)S(1)}, bf16[640,256]{1,0:T(8,128)(2,1)S(1)}, u32[]{:S(2)}, u32[]{:S(2)}) collective-permute-start(bf16[640,256]{1,0:T(8,128)(2,1)S(1)} %collective-permute-done.1.refs_2_), channel_id=1, source_target_pairs={{0,16},{16,0},{1,17},{17,1},{2,18},{18,2},{3,19},{19,3},{4,20},{20... | collective-permute-start | bytes 983048 | tf_op jit(solution)/shard_map/ppermute | solution.py:396
  23.5 1.6 %collective-permute-start.3 = (bf16[640,256]{1,0:T(8,128)(2,1)S(1)}, bf16[640,256]{1,0:T(8,128)(2,1)S(1)}, u32[]{:S(2)}, u32[]{:S(2)}) collective-permute-start(bf16[640,256]{1,0:T(8,128)(2,1)S(1)} %collective-permute-done.1.refs_2_), channel_id=1, source_target_pairs={{0,4},{4,0},{8,12},{12,8},{1,5},{5,1},{9,13},{13,9},{2,6},{6,2},{1... | collective-permute-start | bytes 983048 | tf_op jit(solution)/shard_map/ppermute | solution.py:397
  25.1 1.0 %multiply_sine_fusion = (f32[32,640]{1,0:T(8,128)}, f32[32,640]{1,0:T(8,128)}) fusion(f32[640]{0:T(1024)S(1)} %convert_element_type.20, f32[32]{0:T(128)S(1)} %multiply_power_fusion), kind=kLoop, calls=%fused_computation.5 | loop fusion | flops 20480 | bytes 166528 | tf_op jit(solution)/shard_map/sin | solution.py:53
  26.1 2.8 %collective-permute-done.5.refs_10_.refs_2_ = bf16[640,256]{1,0:T(8,128)(2,1)S(1)} collective-permute-done((bf16[640,256]{1,0:T(8,128)(2,1)}, bf16[640,256]{1,0:T(8,128)(2,1)S(1)}, u32[]{:S(2)}, u32[]{:S(2)}) %collective-permute-start.5) | collective-permute-done | bytes 327712 | tf_op jit(solution)/shard_map/ppermute | solution.py:390
  29.0 0.0 copy-start.1
  29.0 2.0 %collective-permute-start.6 = (bf16[640,256]{1,0:T(8,128)(2,1)S(1)}, bf16[640,256]{1,0:T(8,128)(2,1)S(1)}, u32[]{:S(2)}, u32[]{:S(2)}) collective-permute-start(bf16[640,256]{1,0:T(8,128)(2,1)S(1)} %collective-permute-done.5.refs_10_.refs_2_), channel_id=1, source_target_pairs={{0,16},{16,0},{1,17},{17,1},{2,18},{18,2},{3,19},{19,3},{4,20},{20... | collective-permute-start | bytes 983048 | tf_op jit(solution)/shard_map/ppermute | solution.py:396
  31.0 2.8 %route.1 = (bf16[768,640]{1,0:T(8,128)(2,1)}, bf16[8,16,256]{2,1,0:T(8,128)(2,1)}, f32[640,128]{1,0:T(8,128)}, f32[640,128]{1,0:T(8,128)}) custom-call(s32[8]{0:T(128)} %counts_ref.1, s32[640]{0:T(1024)} %dest_ref.1, f32[32,640]{1,0:T(8,128)} %get-tuple-element.29.cosine_ref, f32[32,640]{1,0:T(8,128)} %get-tuple-element.28.sine_ref, ...), custom_call_target="tpu_custom_call" | custom-call | tf_op jit(solution)/shard_map/route/pallas_call | solution.py:324
  33.8 0.0 collective-permute-done.4.refs_5_
  33.8 0.0 copy-start.4
  33.8 1.6 %collective-permute-start.7 = (bf16[640,256]{1,0:T(8,128)(2,1)S(1)}, bf16[640,256]{1,0:T(8,128)(2,1)S(1)}, u32[]{:S(2)}, u32[]{:S(2)}) collective-permute-start(bf16[640,256]{1,0:T(8,128)(2,1)S(1)} %collective-permute-done.5.refs_10_.refs_2_), channel_id=1, source_target_pairs={{0,4},{4,0},{8,12},{12,8},{1,5},{5,1},{9,13},{13,9},{2,6},{6,2},{1... | collective-permute-start | bytes 983048 | tf_op jit(solution)/shard_map/ppermute | solution.py:397
  35.4 0.0 collective-permute-done.2.refs_3_
  35.4 0.0 copy-start.6
  35.4 0.0 collective-permute-done.3.refs_4_
  35.4 0.0 copy-start.7
  35.4 0.0 copy-done.3
  35.4 0.0 copy-done.1
  35.5 0.0 copy-done.4
  35.5 0.7 copy-done.6
  36.1 0.2 copy-done.7
  36.3 5.4 %far_part.2.refs_7_ = bf16[8,112,256]{2,1,0:T(8,128)(2,1)} custom-call(bf16[640,2560]{1,0:T(8,128)(2,1)} %get-tuple-element.15.refs_0_, f32[640,256]{1,0:T(8,128)} %get-tuple-element.16.refs_1_, bf16[640,256]{1,0:T(8,128)(2,1)} %copy-done.3, bf16[640,256]{1,0:T(8,128)(2,1)} %copy-done.6, bf16[640,256]{1,0:T(8,128)(2,1)} %copy-done.7, ...), custom_call_target="tpu_custom_call" | custom-call | flops 20000000000 | bytes 4259840 | tf_op jit(solution)/shard_map/far_part/pallas_call | solution.py:263
  41.7 4.8 %all-to-all-start = ((bf16[8,112,256]{2,1,0:T(8,128)(2,1)}), bf16[8,112,256]{2,1,0:T(8,128)(2,1)S(1)}, u32[]{:S(2)}, u32[]{:S(2)}) async-start(bf16[8,112,256]{2,1,0:T(8,128)(2,1)} %far_part.2.refs_7_), calls=%async_computation | async-start | bytes 917504 | tf_op jit(solution)/shard_map/all_to_all | solution.py:365
  46.5 0.0 collective-permute-done.8.refs_5_
  46.5 0.0 copy-start.2
  46.5 0.0 collective-permute-done.6.refs_3_
  46.5 0.0 copy-start.5
  46.5 0.0 collective-permute-done.7.refs_4_
  46.6 0.7 copy-done.2
  47.2 0.1 copy-done.5
  47.4 0.0 copy-start.8
  47.4 0.7 copy-done.8
  48.1 4.8 %far_part.3 = bf16[768,256]{1,0:T(8,128)(2,1)} custom-call(bf16[640,2560]{1,0:T(8,128)(2,1)} %get-tuple-element.15.refs_0_, f32[640,256]{1,0:T(8,128)} %get-tuple-element.21.refs_0_.refs_1_, bf16[640,256]{1,0:T(8,128)(2,1)} %copy-done.1, bf16[640,256]{1,0:T(8,128)(2,1)} %copy-done.5, bf16[640,256]{1,0:T(8,128)(2,1)} %copy-done.8, ...), custom_call_target="tpu_custom_call" | custom-call | flops 20000000000 | bytes 4259840 | tf_op jit(solution)/shard_map/far_part/pallas_call | solution.py:263
  52.9 5.6 %all-to-all-done = bf16[8,112,256]{2,1,0:T(8,128)(2,1)S(1)} async-done(((bf16[8,112,256]{2,1,0:T(8,128)(2,1)}), bf16[8,112,256]{2,1,0:T(8,128)(2,1)S(1)}, u32[]{:S(2)}, u32[]{:S(2)}) %all-to-all-start) | async-done | bytes 458784 | tf_op jit(solution)/shard_map/all_to_all | solution.py:365
  58.5 3.7 %all-to-all-start.1 = ((bf16[8,96,256]{2,1,0:T(8,128)(2,1)}), bf16[8,96,256]{2,1,0:T(8,128)(2,1)S(1)}, u32[]{:S(2)}, u32[]{:S(2)}) async-start(bf16[8,96,256]{2,1,0:T(8,128)(2,1)} %bitcast.5), calls=%async_computation.1 | async-start | bytes 786432 | tf_op jit(solution)/shard_map/all_to_all | solution.py:365
  62.2 0.1 reshape.24
  62.3 0.9 %convolution_convert_fusion.1 = bf16[256,256]{1,0:T(8,128)(2,1)} fusion(bf16[768,256]{1,0:T(8,128)(2,1)S(1)} %bitcast.7, s32[768]{0:T(1024)S(1)} %reshape.24), kind=kOutput, calls=%fused_computation.1 | convolution fusion | flops 100925440 | bytes 527360 | tf_op jit(solution)/shard_map/dot_general | solution.py:450
  63.2 10.0 %all-to-all-done.1 = bf16[8,96,256]{2,1,0:T(8,128)(2,1)S(1)} async-done(((bf16[8,96,256]{2,1,0:T(8,128)(2,1)}), bf16[8,96,256]{2,1,0:T(8,128)(2,1)S(1)}, u32[]{:S(2)}, u32[]{:S(2)}) %all-to-all-start.1) | async-done | bytes 393248 | tf_op jit(solution)/shard_map/all_to_all | solution.py:365
  73.2 0.9 %convolution_convert_fusion = bf16[256,256]{1,0:T(8,128)(2,1)} fusion(bf16[768,256]{1,0:T(8,128)(2,1)S(1)} %bitcast.6, s32[768]{0:T(1024)S(1)} %reshape.24), kind=kOutput, calls=%fused_computation | convolution fusion | flops 100925440 | bytes 527360 | tf_op jit(solution)/shard_map/dot_general | solution.py:450
  (3 shorter events, 0.1 us)
Async XLA Ops:
  0.6 8.3 %collective-permute-start = (bf16[640,2560]{1,0:T(8,128)(2,1)}, bf16[640,2560]{1,0:T(8,128)(2,1)S(1)}, u32[]{:S(2)}, u32[]{:S(2)}) collective-permute-start(bf16[640,2560]{1,0:T(8,128)(2,1)} %refs_3_.1), channel_id=1, source_target_pairs={{0,1},{1,0},{2,3},{3,2},{4,5},{5,4},{6,7},{7,6},{8,9},{9,8},{10,11... | collective-permute-start | bytes 9830408 | tf_op jit(solution)/shard_map/ppermute | solution.py:367
  3.6 17.9 %collective-permute-start.1 = (bf16[640,256]{1,0:T(8,128)(2,1)}, bf16[640,256]{1,0:T(8,128)(2,1)S(1)}, u32[]{:S(2)}, u32[]{:S(2)}) collective-permute-start(bf16[640,256]{1,0:T(8,128)(2,1)} %get-tuple-element.17), channel_id=1, source_target_pairs={{0,2},{2,0},{1,3},{3,1},{4,6},{6,4},{5,7},{7,5},{8,10},{10,8},{9,1... | collective-permute-start | bytes 983048 | tf_op jit(solution)/shard_map/ppermute | solution.py:390
  6.2 27.6 %collective-permute-start.4 = (bf16[640,256]{1,0:T(8,128)(2,1)}, bf16[640,256]{1,0:T(8,128)(2,1)S(1)}, u32[]{:S(2)}, u32[]{:S(2)}) collective-permute-start(bf16[640,256]{1,0:T(8,128)(2,1)} %get-tuple-element.20), channel_id=1, source_target_pairs={{0,2},{2,0},{1,3},{3,1},{4,6},{6,4},{5,7},{7,5},{8,10},{10,8},{9,1... | collective-permute-start | bytes 983048 | tf_op jit(solution)/shard_map/ppermute | solution.py:390
  6.2 22.7 %collective-permute-start.5 = (bf16[640,256]{1,0:T(8,128)(2,1)}, bf16[640,256]{1,0:T(8,128)(2,1)S(1)}, u32[]{:S(2)}, u32[]{:S(2)}) collective-permute-start(bf16[640,256]{1,0:T(8,128)(2,1)} %get-tuple-element.26), channel_id=1, source_target_pairs={{0,2},{2,0},{1,3},{3,1},{4,6},{6,4},{5,7},{7,5},{8,10},{10,8},{9,1... | collective-permute-start | bytes 983048 | tf_op jit(solution)/shard_map/ppermute | solution.py:390
  8.2 38.3 %collective-permute-start.8 = (bf16[640,256]{1,0:T(8,128)(2,1)}, bf16[640,256]{1,0:T(8,128)(2,1)S(1)}, u32[]{:S(2)}, u32[]{:S(2)}) collective-permute-start(bf16[640,256]{1,0:T(8,128)(2,1)} %get-tuple-element.27), channel_id=1, source_target_pairs={{0,2},{2,0},{1,3},{3,1},{4,6},{6,4},{5,7},{7,5},{8,10},{10,8},{9,1... | collective-permute-start | bytes 983048 | tf_op jit(solution)/shard_map/ppermute | solution.py:390
  9.0 1.7 %copy-start = (bf16[640,2560]{1,0:T(8,128)(2,1)}, bf16[640,2560]{1,0:T(8,128)(2,1)S(1)}, u32[]{:S(2)}) copy-start(bf16[640,2560]{1,0:T(8,128)(2,1)S(1)} %collective-permute-done.refs_4_.refs_5_.refs_6_.refs_7_) | copy-start | bytes 9830404
  21.5 14.0 %copy-start.3 = (bf16[640,256]{1,0:T(8,128)(2,1)}, bf16[640,256]{1,0:T(8,128)(2,1)S(1)}, u32[]{:S(2)}) copy-start(bf16[640,256]{1,0:T(8,128)(2,1)S(1)} %collective-permute-done.1.refs_2_) | copy-start | bytes 983044
  21.5 13.9 %collective-permute-start.2 = (bf16[640,256]{1,0:T(8,128)(2,1)S(1)}, bf16[640,256]{1,0:T(8,128)(2,1)S(1)}, u32[]{:S(2)}, u32[]{:S(2)}) collective-permute-start(bf16[640,256]{1,0:T(8,128)(2,1)S(1)} %collective-permute-done.1.refs_2_), channel_id=1, source_target_pairs={{0,16},{16,0},{1,17},{17,1},{2,18},{18,2},{3,19},{19,3},{4,20},{20... | collective-permute-start | bytes 983048 | tf_op jit(solution)/shard_map/ppermute | solution.py:396
  23.5 11.9 %collective-permute-start.3 = (bf16[640,256]{1,0:T(8,128)(2,1)S(1)}, bf16[640,256]{1,0:T(8,128)(2,1)S(1)}, u32[]{:S(2)}, u32[]{:S(2)}) collective-permute-start(bf16[640,256]{1,0:T(8,128)(2,1)S(1)} %collective-permute-done.1.refs_2_), channel_id=1, source_target_pairs={{0,4},{4,0},{8,12},{12,8},{1,5},{5,1},{9,13},{13,9},{2,6},{6,2},{1... | collective-permute-start | bytes 983048 | tf_op jit(solution)/shard_map/ppermute | solution.py:397
  29.0 6.5 %copy-start.1 = (bf16[640,256]{1,0:T(8,128)(2,1)}, bf16[640,256]{1,0:T(8,128)(2,1)S(1)}, u32[]{:S(2)}) copy-start(bf16[640,256]{1,0:T(8,128)(2,1)S(1)} %collective-permute-done.5.refs_10_.refs_2_) | copy-start | bytes 983044
  29.0 17.5 %collective-permute-start.6 = (bf16[640,256]{1,0:T(8,128)(2,1)S(1)}, bf16[640,256]{1,0:T(8,128)(2,1)S(1)}, u32[]{:S(2)}, u32[]{:S(2)}) collective-permute-start(bf16[640,256]{1,0:T(8,128)(2,1)S(1)} %collective-permute-done.5.refs_10_.refs_2_), channel_id=1, source_target_pairs={{0,16},{16,0},{1,17},{17,1},{2,18},{18,2},{3,19},{19,3},{4,20},{20... | collective-permute-start | bytes 983048 | tf_op jit(solution)/shard_map/ppermute | solution.py:396
  33.8 1.7 %copy-start.4 = (bf16[640,256]{1,0:T(8,128)(2,1)}, bf16[640,256]{1,0:T(8,128)(2,1)S(1)}, u32[]{:S(2)}) copy-start(bf16[640,256]{1,0:T(8,128)(2,1)S(1)} %collective-permute-done.4.refs_5_) | copy-start | bytes 983044
  33.8 12.8 %collective-permute-start.7 = (bf16[640,256]{1,0:T(8,128)(2,1)S(1)}, bf16[640,256]{1,0:T(8,128)(2,1)S(1)}, u32[]{:S(2)}, u32[]{:S(2)}) collective-permute-start(bf16[640,256]{1,0:T(8,128)(2,1)S(1)} %collective-permute-done.5.refs_10_.refs_2_), channel_id=1, source_target_pairs={{0,4},{4,0},{8,12},{12,8},{1,5},{5,1},{9,13},{13,9},{2,6},{6,2},{1... | collective-permute-start | bytes 983048 | tf_op jit(solution)/shard_map/ppermute | solution.py:397
  35.4 0.7 copy-start.6
  35.4 0.9 %copy-start.7 = (bf16[640,256]{1,0:T(8,128)(2,1)}, bf16[640,256]{1,0:T(8,128)(2,1)S(1)}, u32[]{:S(2)}) copy-start(bf16[640,256]{1,0:T(8,128)(2,1)S(1)} %collective-permute-done.3.refs_4_) | copy-start | bytes 983044
  41.7 16.7 %all-to-all-start = ((bf16[8,112,256]{2,1,0:T(8,128)(2,1)}), bf16[8,112,256]{2,1,0:T(8,128)(2,1)S(1)}, u32[]{:S(2)}, u32[]{:S(2)}) async-start(bf16[8,112,256]{2,1,0:T(8,128)(2,1)} %far_part.2.refs_7_), calls=%async_computation | async-start | bytes 917504 | tf_op jit(solution)/shard_map/all_to_all | solution.py:365
  46.5 0.7 copy-start.2
  46.5 0.8 %copy-start.5 = (bf16[640,256]{1,0:T(8,128)(2,1)}, bf16[640,256]{1,0:T(8,128)(2,1)S(1)}, u32[]{:S(2)}) copy-start(bf16[640,256]{1,0:T(8,128)(2,1)S(1)} %collective-permute-done.6.refs_3_) | copy-start | bytes 983044
  47.4 0.7 copy-start.8
  58.5 14.7 %all-to-all-start.1 = ((bf16[8,96,256]{2,1,0:T(8,128)(2,1)}), bf16[8,96,256]{2,1,0:T(8,128)(2,1)S(1)}, u32[]{:S(2)}, u32[]{:S(2)}) async-start(bf16[8,96,256]{2,1,0:T(8,128)(2,1)} %bitcast.5), calls=%async_computation.1 | async-start | bytes 786432 | tf_op jit(solution)/shard_map/all_to_all | solution.py:365

commit v3 on v2

v3 whole, which is shorter than its diff:
```python
import functools

import jax
import jax.numpy as jnp
from jax import lax
from jax.experimental import pallas as pl
from jax.experimental.pallas import tpu as pltpu
from jax.sharding import PartitionSpec as P

HEAD_DIM = 128
BLOCK = 128
HOT_BLOCKS = 5
OWN_DEV = 256


epsilon = 1e-05
rope_base = 1000000.0
VMEM_BYTES = 62 * 1024 * 1024
NEAR_STEP = 128
NEAR_COST = 20_000_000_000
FAR_COST = 20_000_000_000


def ordered(*values):
    return lax.optimization_barrier(values)


def group_index():
    return lax.axis_index("rep") * lax.axis_size("fsdp") + lax.axis_index("fsdp")


def quarter_numbers():
    group = lax.axis_index("groups")
    odd = lax.rem(lax.axis_index("rep"), 2)
    return (2 * group + odd, 2 * (1 - group) + odd, 2 * group + 1 - odd, 3 - 2 * group - odd)


def far_places(relayed, depth):
    shards = lax.axis_size("fsdp")
    shard = lax.axis_index("fsdp")
    if relayed:
        return [(1 - shard) * depth + number * (depth // 4) for number in quarter_numbers()]
    return [lax.rem(shard + shards - k, shards) * depth for k in range(1, shards)]


def rotary_angles(positions):
    half_rot = HEAD_DIM // 4
    freq_index = jnp.arange(half_rot, dtype=jnp.float32)
    inverse = rope_base ** (-freq_index / half_rot)
    angles = inverse[:, None] * positions.astype(jnp.float32)[None, :]
    return jnp.cos(angles), jnp.sin(angles)


def cut_kernel(key_ref, value_ref, *refs):
    outs, sems = refs[:4], refs[4]
    quarter = outs[0].shape[0]
    mine = 2 * lax.axis_index("groups") + lax.rem(lax.axis_index("rep"), 2)
    copies = []
    for index, (source, which) in enumerate(
        ((key_ref, mine), (value_ref, mine), (key_ref, 3 - mine), (value_ref, 3 - mine))
    ):
        start = pl.multiple_of(which * quarter, quarter)
        copy = pltpu.make_async_copy(
            source.at[pl.ds(start, quarter), :], outs[index], sems.at[index]
        )
        copy.start()
        copies.append(copy)
    for copy in copies:
        copy.wait()


def cut_quarters(key_weight, value_weight):
    depth, columns = key_weight.shape
    piece = jax.ShapeDtypeStruct((depth // 4, columns), key_weight.dtype)
    return pl.pallas_call(
        cut_kernel,
        out_shape=(piece,) * 4,
        in_specs=[pl.BlockSpec(memory_space=pl.ANY)] * 2,
        out_specs=(pl.BlockSpec(memory_space=pltpu.VMEM),) * 4,
        scratch_shapes=[pltpu.SemaphoreType.DMA((4,))],
        compiler_params=pltpu.CompilerParams(vmem_limit_bytes=VMEM_BYTES),
        name="cut_quarters",
    )(key_weight, value_weight)


def near_kernel(
    own_ref,
    got_ref,
    key_ref,
    value_ref,
    gain_ref,
    key_bias_ref,
    value_bias_ref,
    keys_ref,
    values_ref,
    scale_ref,
    own_buf,
    got_buf,
    key_buf,
    value_buf,
    normed_ref,
    key_sum,
    value_sum,
    scale_buf,
    sems,
):
    rows, width = own_ref.shape
    depth = key_ref.shape[0]
    size = NEAR_STEP
    blocks = rows // size

    def read(index):
        if index == blocks:
            pairs = ((key_ref, key_buf), (value_ref, value_buf))
        else:
            here = pl.ds(index * size, size)
            pairs = (
                (own_ref.at[here, :], own_buf.at[here, :]),
                (got_ref.at[here, :], got_buf.at[here, :]),
            )
        return [
            pltpu.make_async_copy(source, buf, sems.at[side, index])
            for side, (source, buf) in enumerate(pairs)
        ]

    def start(index):
        if index <= blocks:
            for copy in read(index):
                copy.start()

    start(0)
    start(1)
    lanes = 128
    near_first = lax.axis_index("fsdp") * depth
    side = near_first // width
    gain = gain_ref[pl.ds(pl.multiple_of(side * width, width), width)]
    gain = gain.astype(jnp.float32).reshape(1, width)
    writes = []
    for index in range(blocks):
        for copy in read(index):
            copy.wait()
        start(index + 2)
        here = pl.ds(index * size, size)
        squares = jnp.zeros((size, lanes), jnp.float32)
        for source in (own_buf, got_buf):
            for first in range(0, width, lanes):
                part = source[here, first : first + lanes].astype(jnp.float32)
                squares += part * part
        total = jnp.sum(squares, axis=1, keepdims=True)
        scale = jnp.broadcast_to(lax.rsqrt(total / (2 * width) + epsilon), (size, lanes))
        scale_buf[here, :] = scale
        for source, is_near in (
            (own_buf, side == lax.axis_index("tp")),
            (got_buf, side != lax.axis_index("tp")),
        ):

            @pl.when(is_near)
            def _(source=source, here=here, scale=scale):
                for first in range(0, width, lanes):
                    part = source[here, first : first + lanes].astype(jnp.float32)
                    normed_ref[here, first : first + lanes] = (
                        part * scale * gain[:, first : first + lanes]
                    ).astype(jnp.bfloat16)

    write = pltpu.make_async_copy(scale_buf, scale_ref, sems.at[2, 0])
    write.start()
    writes.append(write)
    for copy in read(blocks):
        copy.wait()
    for weight, bias_ref, sum_ref, out_ref in (
        (key_buf, key_bias_ref, key_sum, keys_ref),
        (value_buf, value_bias_ref, value_sum, values_ref),
    ):
        bias = bias_ref[...].astype(jnp.float32).reshape(1, sum_ref.shape[1])
        near = normed_ref[:, pl.ds(pl.multiple_of(near_first % width, depth), depth)]
        sum_ref[...] = jnp.dot(near, weight[...], preferred_element_type=jnp.float32) + bias
        write = pltpu.make_async_copy(sum_ref, out_ref, sems.at[2, len(writes)])
        write.start()
        writes.append(write)
    for write in writes:
        write.wait()


def near_part(own, got, norm_gain, key_weight, value_weight, key_bias, value_bias):
    rows, width = own.shape
    depth, columns = key_weight.shape
    sums = jax.ShapeDtypeStruct((rows, columns), jnp.float32)
    vmem = pl.BlockSpec(memory_space=pltpu.VMEM)
    anywhere = pl.BlockSpec(memory_space=pl.ANY)
    return pl.pallas_call(
        near_kernel,
        out_shape=(sums, sums, jax.ShapeDtypeStruct((rows, 128), jnp.float32)),
        in_specs=[anywhere] * 4 + [vmem] * 3,
        out_specs=(anywhere,) * 3,
        scratch_shapes=[
            pltpu.VMEM((rows, width), jnp.bfloat16),
            pltpu.VMEM((rows, width), jnp.bfloat16),
            pltpu.VMEM((depth, columns), jnp.bfloat16),
            pltpu.VMEM((depth, columns), jnp.bfloat16),
            pltpu.VMEM((rows, width), jnp.bfloat16),
            pltpu.VMEM((rows, columns), jnp.float32),
            pltpu.VMEM((rows, columns), jnp.float32),
            pltpu.VMEM((rows, 128), jnp.float32),
            pltpu.SemaphoreType.DMA((3, rows // NEAR_STEP + 1)),
        ],
        compiler_params=pltpu.CompilerParams(vmem_limit_bytes=VMEM_BYTES),
        cost_estimate=pl.CostEstimate(
            flops=NEAR_COST,
            bytes_accessed=6 * rows * width + 4 * depth * columns,
            transcendentals=0,
        ),
        name="near_part",
    )(own, got, key_weight, value_weight, norm_gain, key_bias, value_bias)


def turned(total, cosine, sine):
    half_rot, rows = cosine.shape
    rest = jnp.zeros((HEAD_DIM - 2 * half_rot, rows), jnp.float32)
    straight = jnp.concatenate([cosine, cosine, rest + 1.0], axis=0).T
    crossed = jnp.concatenate([-sine, sine, rest], axis=0).T
    lane = lax.broadcasted_iota(jnp.int32, straight.shape, 1)
    heads = []
    for head in range(total.shape[1] // HEAD_DIM):
        part = total[:, head * HEAD_DIM : (head + 1) * HEAD_DIM]
        partner = jnp.where(
            lane < half_rot,
            pltpu.roll(part, HEAD_DIM - half_rot, 1),
            pltpu.roll(part, half_rot, 1),
        )
        heads.append(part * straight + partner * crossed)
    return jnp.concatenate(heads, axis=1)


def picked(target_ref, first, size, rows):
    target = target_ref[0:1, :]
    line = lax.broadcasted_iota(jnp.int32, (size, target.shape[1]), 0) + first
    pick = jnp.where(line == target, 1.0, 0.0).astype(jnp.bfloat16)
    return jnp.dot(pick, rows, preferred_element_type=jnp.float32).astype(jnp.bfloat16)


def far_kernel(relayed, turn, extra, count, outs, *refs):
    own_ref, got_ref, near_ref, scale_ref = refs[:4]
    pieces = refs[4 : 4 + count]
    scratch = refs[-2 * count - 5 :]
    part_bufs, piece_bufs = scratch[:count], scratch[count : 2 * count]
    near_buf, scale_buf, gain_buf, normed_buf, sems = scratch[2 * count :]
    rest = list(refs[4 + count : -outs - 1 - len(scratch)])
    out_refs = refs[-outs - len(scratch) : -len(scratch)]
    depth = pieces[0].shape[0]
    width = own_ref.shape[1]
    places = far_places(relayed, depth * 4 if relayed else depth)
    lanes = 128
    near_copies = (
        pltpu.make_async_copy(near_ref, near_buf, sems.at[0, count]),
        pltpu.make_async_copy(scale_ref, scale_buf, sems.at[1, count]),
    )

    def part_copy(source, index):
        first = pl.multiple_of(places[index] % width, lanes)
        return pltpu.make_async_copy(
            source.at[:, pl.ds(first, depth)], part_bufs[index], sems.at[0, index]
        )

    def piece_copy(index):
        return pltpu.make_async_copy(pieces[index], piece_bufs[index], sems.at[1, index])

    for copy in near_copies:
        copy.start()
    for index in range(count):
        is_own = places[index] // width == lax.axis_index("tp")

        @pl.when(is_own)
        def _(index=index):
            part_copy(own_ref, index).start()

        @pl.when(jnp.logical_not(is_own))
        def _(index=index):
            part_copy(got_ref, index).start()

        piece_copy(index).start()
    gain_ref = rest.pop(0)
    gain_buf[...] = gain_ref[...].astype(jnp.float32).reshape(1, 2 * width)
    for copy in near_copies:
        copy.wait()
    total = near_buf[...]
    for index in range(count):
        part_copy(own_ref, index).wait()
        for first in range(0, depth, lanes):
            here = slice(first, first + lanes)
            gain = gain_buf[:, pl.ds(pl.multiple_of(places[index] + first, lanes), lanes)]
            part = part_bufs[index][:, here].astype(jnp.float32)
            normed_buf[:, here] = (part * scale_buf[...] * gain).astype(jnp.bfloat16)
        piece_copy(index).wait()
        total += jnp.dot(
            normed_buf[...], piece_bufs[index][...], preferred_element_type=jnp.float32
        )
    if turn:
        total = turned(total, rest.pop(0)[...], rest.pop(0)[...])
    target_ref = rest.pop(0)
    total = total.astype(jnp.bfloat16)
    if outs > 1:
        me = group_index()
        for other, out_ref in enumerate(out_refs):
            size = out_ref.shape[0]
            out_ref[...] = picked(target_ref, lax.bitwise_xor(me, other) * size, size, total)
    elif extra:
        extra_ref = rest.pop(0)
        owners, tall, columns = out_refs[0].shape
        most_rows = tall - extra
        laid = picked(target_ref, 0, owners * most_rows, total)
        out_refs[0][:, :most_rows, :] = laid.reshape(owners, most_rows, columns)
        out_refs[0][:, most_rows:, :] = extra_ref[...]
    else:
        out_refs[0][...] = picked(target_ref, 0, out_refs[0].shape[0], total)


def far_part(
    relayed, rows_of, norm_gain, near, scale, pieces, angles, target, capacity, extra, outs, after
):
    rows, columns = near.shape
    depth = pieces[0].shape[0]
    count = len(pieces)
    operands = [norm_gain, *angles, target]
    tall = 0
    if extra is None:
        shape = (capacity // outs, columns)
    else:
        owners, tall, _ = extra.shape
        shape = (owners, capacity // owners + tall, columns)
        operands.append(extra)
    vmem = pl.BlockSpec(memory_space=pltpu.VMEM)
    anywhere = pl.BlockSpec(memory_space=pl.ANY)
    return pl.pallas_call(
        functools.partial(far_kernel, relayed, bool(angles), tall, count, outs),
        out_shape=(jax.ShapeDtypeStruct(shape, jnp.bfloat16),) * outs,
        in_specs=[anywhere] * (4 + count) + [vmem] * len(operands) + [anywhere],
        out_specs=(vmem,) * outs,
        scratch_shapes=[
            *[pltpu.VMEM((rows, depth), jnp.bfloat16) for _ in pieces],
            *[pltpu.VMEM((depth, columns), jnp.bfloat16) for _ in pieces],
            pltpu.VMEM((rows, columns), jnp.float32),
            pltpu.VMEM(scale.shape, jnp.float32),
            pltpu.VMEM((1, norm_gain.shape[0]), jnp.float32),
            pltpu.VMEM((rows, depth), jnp.bfloat16),
            pltpu.SemaphoreType.DMA((2, count + 1)),
        ],
        compiler_params=pltpu.CompilerParams(vmem_limit_bytes=VMEM_BYTES),
        cost_estimate=pl.CostEstimate(
            flops=FAR_COST,
            bytes_accessed=12 * rows * columns,
            transcendentals=0,
        ),
        name="far_part",
    )(*rows_of, near, scale, *pieces, *operands, after)


def route_kernel(most_rows, counts_ref, dest_ref, after_ref, target_ref, marks_ref):
    me = group_index()
    devices = marks_ref.shape[0]
    rows = dest_ref.shape[0]
    dest = dest_ref[...].reshape(1, rows)
    row = lax.broadcasted_iota(jnp.int32, (1, rows), 1)
    valid = (row < BLOCK * counts_ref[me]) & (dest >= 0)
    owner = jnp.where(valid, lax.div(dest, OWN_DEV), -1)
    slot = jnp.where(valid, lax.rem(dest, OWN_DEV), -1)
    tall = -(-devices // 16) * 16
    to_owner = lax.broadcasted_iota(jnp.int32, (tall, rows), 0) == owner
    ones = jnp.where(to_owner, 1.0, 0.0)
    earlier = jnp.where(
        lax.broadcasted_iota(jnp.int32, (rows, rows), 0)
        < lax.broadcasted_iota(jnp.int32, (rows, rows), 1),
        1.0,
        0.0,
    ).astype(jnp.bfloat16)
    before = jnp.dot(ones.astype(jnp.bfloat16), earlier, preferred_element_type=jnp.float32)
    rank = jnp.sum(ones * before, axis=0, keepdims=True).astype(jnp.int32)
    target = jnp.where(valid, owner * most_rows + rank, devices * most_rows)
    target_ref[...] = jnp.broadcast_to(target, target_ref.shape)
    at_rank = jnp.where(
        (lax.broadcasted_iota(jnp.int32, (marks_ref.shape[2], rows), 0) == rank) & valid, 1.0, 0.0
    ).astype(jnp.bfloat16)
    slots = jnp.where(to_owner, (slot + 1).astype(jnp.float32), 0.0).astype(jnp.bfloat16)
    marks = lax.dot_general(
        slots, at_rank, (((1,), (1,)), ((), ())), preferred_element_type=jnp.float32
    )
    marks = marks[:devices] - 1.0
    marks_ref[...] = jnp.broadcast_to(marks[:, None, :], marks_ref.shape).astype(jnp.bfloat16)


def route(block_counts, dest_slots, devices, most_rows, columns, after):
    rows = dest_slots.shape[0]
    vmem = pl.BlockSpec(memory_space=pltpu.VMEM)
    return pl.pallas_call(
        functools.partial(route_kernel, most_rows),
        out_shape=(
            jax.ShapeDtypeStruct((8, rows), jnp.int32),
            jax.ShapeDtypeStruct((devices, 16, columns), jnp.bfloat16),
        ),
        in_specs=[
            pl.BlockSpec(memory_space=pltpu.SMEM),
            vmem,
            pl.BlockSpec(memory_space=pl.ANY),
        ],
        out_specs=(vmem,) * 2,
        compiler_params=pltpu.CompilerParams(vmem_limit_bytes=VMEM_BYTES),
        name="route",
    )(block_counts, dest_slots, after)


def place_kernel(came_ref, put_ref, out_ref):
    devices, tall, columns = came_ref.shape
    most_rows = tall - 16
    owned = out_ref.shape[0]
    total = jnp.zeros(out_ref.shape, jnp.float32)
    slot = lax.broadcasted_iota(jnp.int32, (owned, most_rows), 0)
    me = group_index()
    for other in range(devices):
        source = lax.bitwise_xor(me, other)
        marks = came_ref[source, most_rows:, :].astype(jnp.float32)[0:1, :most_rows]
        put = jnp.where(slot == marks.astype(jnp.int32), 1.0, 0.0).astype(jnp.bfloat16)
        put_ref[other, :, :most_rows] = put
        total += jnp.dot(put, came_ref[source, :most_rows, :], preferred_element_type=jnp.float32)
    out_ref[...] = total.astype(jnp.bfloat16)


def place_keys(came):
    devices, tall, columns = came.shape
    vmem = pl.BlockSpec(memory_space=pltpu.VMEM)
    return pl.pallas_call(
        place_kernel,
        out_shape=(
            jax.ShapeDtypeStruct((devices, OWN_DEV, 128), jnp.bfloat16),
            jax.ShapeDtypeStruct((OWN_DEV, columns), jnp.bfloat16),
        ),
        in_specs=[vmem],
        out_specs=(vmem,) * 2,
        compiler_params=pltpu.CompilerParams(vmem_limit_bytes=VMEM_BYTES),
        name="place_keys",
    )(came)


def place_values_kernel(put_ref, *refs):
    out_ref = refs[-1]
    most_rows = refs[0].shape[0]
    total = jnp.zeros(out_ref.shape, jnp.float32)
    for other, rows_ref in enumerate(refs[:-1]):
        total += jnp.dot(
            put_ref[other, :, :most_rows], rows_ref[...], preferred_element_type=jnp.float32
        )
    out_ref[...] = total.astype(jnp.bfloat16)


def place_values(put, came):
    vmem = pl.BlockSpec(memory_space=pltpu.VMEM)
    return pl.pallas_call(
        place_values_kernel,
        out_shape=jax.ShapeDtypeStruct((OWN_DEV, came[0].shape[1]), jnp.bfloat16),
        in_specs=[vmem] * (1 + len(came)),
        out_specs=vmem,
        compiler_params=pltpu.CompilerParams(vmem_limit_bytes=VMEM_BYTES),
        name="place_values",
    )(put, *came)


def local(
    tokens,
    norm_gain,
    key_weight,
    value_weight,
    key_bias,
    value_bias,
    block_counts,
    positions,
    dest_slots,
):
    axes = ("rep", "fsdp")
    devices = lax.axis_size(axes)
    most_rows = (HOT_BLOCKS + 1) * (BLOCK // devices)
    capacity = devices * most_rows
    rows, width = tokens.shape
    depth = key_weight.shape[0]
    shards = lax.axis_size("fsdp")

    def exchange(rows_by_owner):
        return lax.all_to_all(rows_by_owner, axes, split_axis=0, concat_axis=0, tiled=True)

    got = lax.ppermute(tokens, "tp", [(0, 1), (1, 0)])
    quarter = depth // 4
    relayed = (
        shards == 2
        and lax.axis_size("groups") == 2
        and lax.axis_size("rep") % 2 == 0
        and depth % 4 == 0
        and quarter % 128 == 0
    )
    swap = [(0, 1), (1, 0)]
    if relayed:
        key_own, value_own, key_last, value_last = cut_quarters(key_weight, value_weight)
        key_own = lax.ppermute(key_own, "fsdp", swap)
        value_own = lax.ppermute(value_own, "fsdp", swap)
        got, key_last, value_last = ordered(got, key_last, value_last)
        key_last = lax.ppermute(key_last, "fsdp", swap)
        value_last = lax.ppermute(value_last, "fsdp", swap)

    near_keys, near_values, scale = near_part(
        tokens,
        got,
        norm_gain,
        key_weight,
        value_weight,
        key_bias,
        value_bias,
    )
    if relayed:
        across = [(i, i ^ 1) for i in range(lax.axis_size("rep"))]
        key_own, near_values = ordered(key_own, near_values)

        def pieces_of(own, opposite):
            by_group = lax.ppermute(own, "groups", swap)
            by_rep = lax.ppermute(own, "rep", across)
            return own, by_group, by_rep, opposite

        key_pieces = pieces_of(key_own, key_last)
        value_pieces = pieces_of(value_own, value_last)
    else:
        steps = range(1, shards)

        def pieces_of(weight):
            return tuple(
                lax.ppermute(weight, "fsdp", [(i, (i + k) % shards) for i in range(shards)])
                for k in steps
            )

        key_pieces = pieces_of(key_weight)
        value_pieces = pieces_of(value_weight)

    columns = key_weight.shape[1]
    inline = most_rows % 16 == 0 and most_rows <= columns
    target, marks = route(block_counts, dest_slots, devices, most_rows, columns, near_values)
    positions, near_values = ordered(positions, near_values)
    angles = rotary_angles(positions)
    if not inline:
        got_marks = exchange(marks[:, 0, :most_rows].reshape(capacity))
    (send_keys,) = far_part(
        relayed,
        (tokens, got),
        norm_gain,
        near_keys,
        scale,
        key_pieces,
        angles,
        target,
        capacity,
        marks if inline else None,
        1,
        value_pieces[0],
    )
    came_keys = exchange(send_keys)
    paired = inline and devices & (devices - 1) == 0 and most_rows <= 128
    send_values = far_part(
        relayed,
        (tokens, got),
        norm_gain,
        near_values,
        scale,
        value_pieces,
        (),
        target,
        capacity,
        None,
        devices if paired else 1,
        send_keys,
    )
    if paired:
        came_values = list(send_values)
        for other in sorted(range(1, devices), key=lambda k: -(k ^ 2)):
            came_values[other] = lax.ppermute(
                send_values[other], axes, [(i, i ^ other) for i in range(devices)]
            )
        put, cache_keys = place_keys(came_keys)
        return cache_keys, place_values(put, came_values)
    came_values = exchange(send_values[0])
    if inline:
        got_marks = came_keys[:, most_rows, :most_rows].reshape(capacity)
        came_keys = came_keys[:, :most_rows].reshape(capacity, columns)
    put = (
        jnp.arange(OWN_DEV, dtype=jnp.int32)[:, None] == got_marks.astype(jnp.int32)[None, :]
    ).astype(jnp.bfloat16)
    return tuple(
        jnp.dot(put, came, preferred_element_type=jnp.float32).astype(jnp.bfloat16)
        for came in (came_keys, came_values)
    )


def solution(mesh):
    return jax.shard_map(
        local,
        mesh=mesh,
        in_specs=(
            P(("groups", "rep", "fsdp"), "tp"),
            P(),
            P("fsdp", "tp"),
            P("fsdp", "tp"),
            P("tp"),
            P("tp"),
            P("groups"),
            P(("groups", "rep", "fsdp")),
            P(("groups", "rep", "fsdp")),
        ),
        out_specs=(P(("groups", "rep", "fsdp"), "tp"), P(("groups", "rep", "fsdp"), "tp")),
        check_vma=False,
    )
```

time: 74.6 us -> 70.1 us (0.940)
  waiting for transfers between devices: 18.4 us -> 3.31 us
  starting transfers between devices: 20.9 us -> 31.1 us
  Pallas kernels: 26.1 us -> 31.1 us
  local copies, waits for them, and re-layouts: 4.24 us -> 2.13 us
  matrix products: 1.86 us -> 0 us
    all_to_all x2 -> x1, waiting for transfers between devices: 15.6 us -> 0.01 us  [exchange(): lax.all_to_all(rows_by_owner, axes, split_axis=0, concat_axis=0, tiled=True)]
    ppermute x4 -> x11, starting transfers between devices: 4.69 us -> 16.9 us  [the longest x7 11.3 us: local(): lax.ppermute(send_values[other], axes, [(i, i ^ other) for i in range(dev...]
    pallas_call x3 -> x5, Pallas kernels: 20.9 us -> 27 us  [the longest x2 13.8 us: far_part(): pl.pallas_call(functools.partial(far_kernel, relayed, bool(angles), tall,...]
    all_to_all x2 -> x1, starting transfers between devices: 8.48 us -> 5.61 us  [exchange(): lax.all_to_all(rows_by_owner, axes, split_axis=0, concat_axis=0, tiled=True)]
    unnamed x18 -> x28, local copies, waits for them, and re-layouts: 4.14 us -> 2.13 us
    dot_general x2 -> x0, matrix products: 1.86 us -> none  [local(): jnp.dot(put, came, preferred_element_type=jnp.float32).astype(jnp.bfloat16)]
    pallas_call x1, Pallas kernels: 2.8 us -> 1.73 us  [route(): pl.pallas_call(functools.partial(route_kernel, most_rows), out_shape=(jax...]
    ppermute x2, starting transfers between devices: 4.02 us -> 4.8 us  [pieces_of(): by_group = lax.ppermute(own, 'groups', swap)]
  transfers between devices with their start and end apart: 11 -> 17, of which waited for: 3 -> 2; matrix products, arithmetic and copies ran while one was open for 4% -> 2% of each run, Pallas kernels for 35% -> 42%
where the time goes in v3:
time: 70.1 us; the launch traced here: 69.5 us
  starting transfers between devices  31.1 us (44%)
  Pallas kernels  31.1 us (44%)
  waiting for transfers between devices  3.31 us (5%)
  local copies, waits for them, and re-layouts  2.13 us (3%)
  other arithmetic  1.04 us (1%)
  between operations  0.81 us (1%)
    pallas_call x2, Pallas kernels, far_part(): pl.pallas_call(functools.partial(far_kernel, relayed, bool(angles), tall,...  13.8 us
    ppermute x7, starting transfers between devices, local(): lax.ppermute(send_values[other], axes, [(i, i ^ other) for i in range(dev...  11.3 us
    pallas_call x1, Pallas kernels, near_part(): pl.pallas_call(near_kernel, out_shape=(sums, sums, jax.ShapeDtypeStruct((...  8.88 us
    all_to_all x1, starting transfers between devices, exchange(): lax.all_to_all(rows_by_owner, axes, split_axis=0, concat_axis=0, tiled=True)  5.61 us
    ppermute x2, starting transfers between devices, pieces_of(): by_group = lax.ppermute(own, 'groups', swap)  4.8 us
    ppermute x2, starting transfers between devices, pieces_of(): by_rep = lax.ppermute(own, 'rep', across)  3.27 us
    ppermute x1, starting transfers between devices, local(): key_own = lax.ppermute(key_own, 'fsdp', swap)  2.59 us
    ppermute x7, waiting for transfers between devices, local(): lax.ppermute(send_values[other], axes, [(i, i ^ other) for i in range(dev...  2.52 us
  transfers between devices with their start and end apart: 17, of which 2 were waited for; matrix products, arithmetic and copies ran while one was open for 2% of the time, Pallas kernels for 42%

profile of v3, /device:TPU:0, one launch (start us, length us, event | category | flops | bytes accessed | tf_op | source)
XLA Modules:
  0.0 69.5 jit_solution(6513451331244913712)
XLA Ops:
  0.6 0.5 collective-permute-start
  1.1 2.4 %cut_quarters.1 = (bf16[640,256]{1,0:T(8,128)(2,1)}, bf16[640,256]{1,0:T(8,128)(2,1)}, bf16[640,256]{1,0:T(8,128)(2,1)}, bf16[640,256]{1,0:T(8,128)(2,1)}) custom-call(bf16[2560,256]{1,0:T(8,128)(2,1)} %key_ref.3, bf16[2560,256]{1,0:T(8,128)(2,1)} %value_ref.3), custom_call_target="tpu_custom_call" | custom-call | tf_op jit(solution)/shard_map/cut_quarters/pallas_call | solution.py:75
  3.5 2.6 %collective-permute-start.1 = (bf16[640,256]{1,0:T(8,128)(2,1)}, bf16[640,256]{1,0:T(8,128)(2,1)S(1)}, u32[]{:S(2)}, u32[]{:S(2)}) collective-permute-start(bf16[640,256]{1,0:T(8,128)(2,1)} %get-tuple-element.33), channel_id=1, source_target_pairs={{0,2},{2,0},{1,3},{3,1},{4,6},{6,4},{5,7},{7,5},{8,10},{10,8},{9,1... | collective-permute-start | bytes 983048 | tf_op jit(solution)/shard_map/ppermute | solution.py:499
  6.1 0.1 collective-permute-start.5
  6.2 0.8 %collective-permute-done.got_ref.refs_1_ = bf16[640,2560]{1,0:T(8,128)(2,1)} collective-permute-done((bf16[640,2560]{1,0:T(8,128)(2,1)}, bf16[640,2560]{1,0:T(8,128)(2,1)}, u32[]{:S(2)}, u32[]{:S(2)}) %collective-permute-start) | collective-permute-done | bytes 3276832 | tf_op jit(solution)/shard_map/ppermute | solution.py:487
  7.0 0.0 copy-start.13
  7.0 0.0 copy-start.8
  7.0 0.0 copy-start.10
  7.0 8.9 %near_part.1 = (f32[640,256]{1,0:T(8,128)}, f32[640,256]{1,0:T(8,128)}, f32[640,128]{1,0:T(8,128)}) custom-call(bf16[640,2560]{1,0:T(8,128)(2,1)} %refs_0_.3, bf16[640,2560]{1,0:T(8,128)(2,1)} %collective-permute-done.got_ref.refs_1_, bf16[2560,256]{1,0:T(8,128)(2,1)} %key_ref.3, bf16[2560,256]{1,0:T(8,128)(2,1)} %value_ref.3, bf16[5120]{0:T(1024)(128)(2,1)} %refs_8_.3, ...), custom_call_target="tpu_custom_call" | custom-call | flops 20000000000 | bytes 12451840 | tf_op jit(solution)/shard_map/near_part/pallas_call | solution.py:190
  15.9 0.0 collective-permute-done.1.refs_4_
  15.9 0.0 copy-start.11
  15.9 3.0 %collective-permute-start.2 = (bf16[640,256]{1,0:T(8,128)(2,1)S(1)}, bf16[640,256]{1,0:T(8,128)(2,1)}, u32[]{:S(2)}, u32[]{:S(2)}) collective-permute-start(bf16[640,256]{1,0:T(8,128)(2,1)S(1)} %collective-permute-done.1.refs_4_), channel_id=1, source_target_pairs={{0,16},{16,0},{1,17},{17,1},{2,18},{18,2},{3,19},{19,3},{4,20},{20... | collective-permute-start | bytes 983048 | tf_op jit(solution)/shard_map/ppermute | solution.py:519
  18.8 1.6 %collective-permute-start.3 = (bf16[640,256]{1,0:T(8,128)(2,1)S(1)}, bf16[640,256]{1,0:T(8,128)(2,1)}, u32[]{:S(2)}, u32[]{:S(2)}) collective-permute-start(bf16[640,256]{1,0:T(8,128)(2,1)S(1)} %collective-permute-done.1.refs_4_), channel_id=1, source_target_pairs={{0,4},{4,0},{8,12},{12,8},{1,5},{5,1},{9,13},{13,9},{2,6},{6,2},{1... | collective-permute-start | bytes 983048 | tf_op jit(solution)/shard_map/ppermute | solution.py:520
  20.4 0.0 copy-done.13
  20.4 1.5 %collective-permute-start.4 = (bf16[640,256]{1,0:T(8,128)(2,1)S(1)}, bf16[640,256]{1,0:T(8,128)(2,1)}, u32[]{:S(2)}, u32[]{:S(2)}) collective-permute-start(bf16[640,256]{1,0:T(8,128)(2,1)S(1)} %copy-done.13), channel_id=1, source_target_pairs={{0,2},{2,0},{1,3},{3,1},{4,6},{6,4},{5,7},{7,5},{8,10},{10,8},{9,1... | collective-permute-start | bytes 983048 | tf_op jit(solution)/shard_map/ppermute | solution.py:502
  21.9 0.0 collective-permute-done.5.refs_13_.refs_4_
  21.9 0.0 copy-start.9
  21.9 1.8 %collective-permute-start.6 = (bf16[640,256]{1,0:T(8,128)(2,1)S(1)}, bf16[640,256]{1,0:T(8,128)(2,1)S(1)}, u32[]{:S(2)}, u32[]{:S(2)}) collective-permute-start(bf16[640,256]{1,0:T(8,128)(2,1)S(1)} %collective-permute-done.5.refs_13_.refs_4_), channel_id=1, source_target_pairs={{0,16},{16,0},{1,17},{17,1},{2,18},{18,2},{3,19},{19,3},{4,20},{20... | collective-permute-start | bytes 983048 | tf_op jit(solution)/shard_map/ppermute | solution.py:519
  23.8 1.7 %collective-permute-start.7 = (bf16[640,256]{1,0:T(8,128)(2,1)S(1)}, bf16[640,256]{1,0:T(8,128)(2,1)}, u32[]{:S(2)}, u32[]{:S(2)}) collective-permute-start(bf16[640,256]{1,0:T(8,128)(2,1)S(1)} %collective-permute-done.5.refs_13_.refs_4_), channel_id=1, source_target_pairs={{0,4},{4,0},{8,12},{12,8},{1,5},{5,1},{9,13},{13,9},{2,6},{6,2},{1... | collective-permute-start | bytes 983048 | tf_op jit(solution)/shard_map/ppermute | solution.py:520
  25.5 0.0 copy-done.8
  25.5 1.7 %route.1 = (s32[8,640]{1,0:T(8,128)}, bf16[8,16,256]{2,1,0:T(8,128)(2,1)}) custom-call(s32[8]{0:T(128)} %counts_ref.1, s32[640]{0:T(1024)} %dest_ref.1, f32[640,256]{1,0:T(8,128)} %get-tuple-element.44.after_ref.refs_2_), custom_call_target="tpu_custom_call" | custom-call | tf_op jit(solution)/shard_map/route/pallas_call | solution.py:393
  27.2 1.0 %multiply_sine_fusion = (f32[32,640]{1,0:T(8,128)}, f32[32,640]{1,0:T(8,128)}) fusion(f32[640]{0:T(1024)S(1)} %convert_element_type.3, f32[32]{0:T(128)S(1)} %multiply_power_fusion), kind=kLoop, calls=%fused_computation | loop fusion | flops 20480 | bytes 166528 | tf_op jit(solution)/shard_map/sin | solution.py:51
  28.2 0.0 collective-permute-done.2.refs_5_
  28.2 0.0 copy-done.10
  28.2 1.5 %collective-permute-start.8 = (bf16[640,256]{1,0:T(8,128)(2,1)S(1)}, bf16[640,256]{1,0:T(8,128)(2,1)}, u32[]{:S(2)}, u32[]{:S(2)}) collective-permute-start(bf16[640,256]{1,0:T(8,128)(2,1)S(1)} %copy-done.10), channel_id=1, source_target_pairs={{0,2},{2,0},{1,3},{3,1},{4,6},{6,4},{5,7},{7,5},{8,10},{10,8},{9,1... | collective-permute-start | bytes 983048 | tf_op jit(solution)/shard_map/ppermute | solution.py:503
  29.7 0.0 collective-permute-done.3.refs_6_
  29.7 0.0 collective-permute-done.4.refs_7_
  29.7 0.0 copy-done.11
  29.8 0.0 copy-done.9
  29.8 7.1 %far_part.2.refs_10_ = bf16[8,112,256]{2,1,0:T(8,128)(2,1)} custom-call(bf16[640,2560]{1,0:T(8,128)(2,1)} %refs_0_.3, bf16[640,2560]{1,0:T(8,128)(2,1)} %collective-permute-done.got_ref.refs_1_, f32[640,256]{1,0:T(8,128)} %get-tuple-element.31.refs_2_, f32[640,128]{1,0:T(8,128)} %get-tuple-element.32.refs_3_, bf16[640,256]{1,0:T(8,128)(2,1)} %copy-done.11, ...), custom_call_target="tpu_custom_call" | custom-call | flops 20000000000 | bytes 1966080 | tf_op jit(solution)/shard_map/far_part/pallas_call | solution.py:333
  36.9 5.6 %all-to-all-start = ((bf16[8,112,256]{2,1,0:T(8,128)(2,1)}), bf16[8,112,256]{2,1,0:T(8,128)(2,1)S(1)}, u32[]{:S(2)}, u32[]{:S(2)}) async-start(bf16[8,112,256]{2,1,0:T(8,128)(2,1)} %far_part.2.refs_10_), calls=%async_computation | async-start | bytes 917504 | tf_op jit(solution)/shard_map/all_to_all | solution.py:485
  42.5 0.0 collective-permute-done.6.refs_5_
  42.5 0.0 copy-start.12
  42.5 0.0 collective-permute-done.7.refs_6_
  42.5 0.0 collective-permute-done.8.refs_7_
  42.5 0.7 %copy-done.12 = bf16[640,256]{1,0:T(8,128)(2,1)} copy-done((bf16[640,256]{1,0:T(8,128)(2,1)}, bf16[640,256]{1,0:T(8,128)(2,1)S(1)}, u32[]{:S(2)}) %copy-start.12) | copy-done | bytes 327704
  43.3 6.7 %far_part.3 = (bf16[96,256]{1,0:T(8,128)(2,1)}, bf16[96,256]{1,0:T(8,128)(2,1)}, bf16[96,256]{1,0:T(8,128)(2,1)}, bf16[96,256]{1,0:T(8,128)(2,1)}, bf16[96,256]{...) custom-call(bf16[640,2560]{1,0:T(8,128)(2,1)} %refs_0_.3, ...), custom_call_target="tpu_custom_call" | custom-call | flops 20000000000 | bytes 1966080 | tf_op jit(solution)/shard_map/far_part/pallas_call | solution.py:333
  49.9 2.1 %collective-permute-start.10 = (bf16[96,256]{1,0:T(8,128)(2,1)}, bf16[96,256]{1,0:T(8,128)(2,1)S(1)}, u32[]{:S(2)}, u32[]{:S(2)}) collective-permute-start(bf16[96,256]{1,0:T(8,128)(2,1)} %get-tuple-element.48), channel_id=1, source_target_pairs={{0,4},{2,6},{4,0},{6,2},{8,12},{10,14},{12,8},{14,10},{1,5},{3,7},... | collective-permute-start | bytes 147464 | tf_op jit(solution)/shard_map/ppermute | solution.py:577
  52.0 1.5 %collective-permute-start.11 = (bf16[96,256]{1,0:T(8,128)(2,1)}, bf16[96,256]{1,0:T(8,128)(2,1)S(1)}, u32[]{:S(2)}, u32[]{:S(2)}) collective-permute-start(bf16[96,256]{1,0:T(8,128)(2,1)} %get-tuple-element.49), channel_id=1, source_target_pairs={{0,6},{2,4},{4,2},{6,0},{8,14},{10,12},{12,10},{14,8},{1,7},{3,5},... | collective-permute-start | bytes 147464 | tf_op jit(solution)/shard_map/ppermute | solution.py:577
  53.5 2.4 %collective-permute-start.12 = (bf16[96,256]{1,0:T(8,128)(2,1)}, bf16[96,256]{1,0:T(8,128)(2,1)S(1)}, u32[]{:S(2)}, u32[]{:S(2)}) collective-permute-start(bf16[96,256]{1,0:T(8,128)(2,1)} %get-tuple-element.50), channel_id=1, source_target_pairs={{0,8},{2,10},{4,12},{6,14},{8,0},{10,2},{12,4},{14,6},{1,9},{3,11}... | collective-permute-start | bytes 147464 | tf_op jit(solution)/shard_map/ppermute | solution.py:577
  55.8 0.1 collective-permute-start.13
  55.9 3.7 %collective-permute-start.14 = (bf16[96,256]{1,0:T(8,128)(2,1)}, bf16[96,256]{1,0:T(8,128)(2,1)S(1)}, u32[]{:S(2)}, u32[]{:S(2)}) collective-permute-start(bf16[96,256]{1,0:T(8,128)(2,1)} %get-tuple-element.52), channel_id=1, source_target_pairs={{0,12},{2,14},{4,8},{6,10},{8,4},{10,6},{12,0},{14,2},{1,13},{3,15... | collective-permute-start | bytes 147464 | tf_op jit(solution)/shard_map/ppermute | solution.py:577
  59.7 0.0 collective-permute-done.10.refs_2_
  59.7 1.5 %collective-permute-start.15 = (bf16[96,256]{1,0:T(8,128)(2,1)}, bf16[96,256]{1,0:T(8,128)(2,1)S(1)}, u32[]{:S(2)}, u32[]{:S(2)}) collective-permute-start(bf16[96,256]{1,0:T(8,128)(2,1)} %get-tuple-element.53), channel_id=1, source_target_pairs={{0,14},{2,12},{4,10},{6,8},{8,6},{10,4},{12,2},{14,0},{1,15},{3,13... | collective-permute-start | bytes 147464 | tf_op jit(solution)/shard_map/ppermute | solution.py:577
  61.1 0.0 collective-permute-done.11.refs_3_
  61.1 0.1 collective-permute-start.9
  61.2 0.0 all-to-all-done.came_ref
  61.2 0.8 %copy-done = bf16[8,112,256]{2,1,0:T(8,128)(2,1)} copy-done((bf16[8,112,256]{2,1,0:T(8,128)(2,1)}, bf16[8,112,256]{2,1,0:T(8,128)(2,1)S(1)}, u32[]{:S(2)}) %copy-start) | copy-done | bytes 458776
  62.0 2.1 %place_keys.1 = (bf16[8,256,128]{2,1,0:T(8,128)(2,1)}, bf16[256,256]{1,0:T(8,128)(2,1)}) custom-call(bf16[8,112,256]{2,1,0:T(8,128)(2,1)} %copy-done), custom_call_target="tpu_custom_call" | custom-call | tf_op jit(solution)/shard_map/place_keys/pallas_call | solution.py:429
  64.1 0.0 collective-permute-done.12.refs_4_
  64.1 0.0 collective-permute-done.13.refs_5_
  64.1 0.0 copy-start.4
  64.1 0.0 collective-permute-done.14.refs_6_
  64.1 0.0 copy-start.5
  64.2 2.5 %collective-permute-done.15.refs_7_ = bf16[96,256]{1,0:T(8,128)(2,1)S(1)} collective-permute-done((bf16[96,256]{1,0:T(8,128)(2,1)}, bf16[96,256]{1,0:T(8,128)(2,1)S(1)}, u32[]{:S(2)}, u32[]{:S(2)}) %collective-permute-start.15) | collective-permute-done | bytes 49184 | tf_op jit(solution)/shard_map/ppermute | solution.py:577
  66.7 0.0 collective-permute-done.9.refs_1_
  66.7 0.0 copy-done.1
  66.7 0.0 copy-done.2
  66.7 0.0 copy-done.3
  66.7 0.0 copy-done.4
  66.7 0.0 copy-done.5
  66.7 0.6 copy-done.6
  67.3 0.0 copy-done.7
  67.3 2.2 %place_values.1 = bf16[256,256]{1,0:T(8,128)(2,1)} custom-call(bf16[8,256,128]{2,1,0:T(8,128)(2,1)} %get-tuple-element.43.put_ref, bf16[96,256]{1,0:T(8,128)(2,1)} %get-tuple-element.46.refs_0_, bf16[96,256]{1,0:T(8,128)(2,1)} %copy-done.7, bf16[96,256]{1,0:T(8,128)(2,1)} %copy-done.1, bf16[96,256]{1,0:T(8,128)(2,1)} %copy-done.2, ...), custom_call_target="tpu_custom_call" | custom-call | tf_op jit(solution)/shard_map/place_values/pallas_call | solution.py:455
  (8 shorter events, 0.0 us)
Async XLA Ops:
  0.6 6.3 %collective-permute-start = (bf16[640,2560]{1,0:T(8,128)(2,1)}, bf16[640,2560]{1,0:T(8,128)(2,1)}, u32[]{:S(2)}, u32[]{:S(2)}) collective-permute-start(bf16[640,2560]{1,0:T(8,128)(2,1)} %refs_0_.3), channel_id=1, source_target_pairs={{0,1},{1,0},{2,3},{3,2},{4,5},{5,4},{6,7},{7,6},{8,9},{9,8},{10,11... | collective-permute-start | bytes 9830408 | tf_op jit(solution)/shard_map/ppermute | solution.py:487
  3.5 12.3 %collective-permute-start.1 = (bf16[640,256]{1,0:T(8,128)(2,1)}, bf16[640,256]{1,0:T(8,128)(2,1)S(1)}, u32[]{:S(2)}, u32[]{:S(2)}) collective-permute-start(bf16[640,256]{1,0:T(8,128)(2,1)} %get-tuple-element.33), channel_id=1, source_target_pairs={{0,2},{2,0},{1,3},{3,1},{4,6},{6,4},{5,7},{7,5},{8,10},{10,8},{9,1... | collective-permute-start | bytes 983048 | tf_op jit(solution)/shard_map/ppermute | solution.py:499
  6.1 15.8 %collective-permute-start.5 = (bf16[640,256]{1,0:T(8,128)(2,1)}, bf16[640,256]{1,0:T(8,128)(2,1)S(1)}, u32[]{:S(2)}, u32[]{:S(2)}) collective-permute-start(bf16[640,256]{1,0:T(8,128)(2,1)} %get-tuple-element.41), channel_id=1, source_target_pairs={{0,2},{2,0},{1,3},{3,1},{4,6},{6,4},{5,7},{7,5},{8,10},{10,8},{9,1... | collective-permute-start | bytes 983048 | tf_op jit(solution)/shard_map/ppermute | solution.py:500
  7.0 13.4 %copy-start.13 = (bf16[640,256]{1,0:T(8,128)(2,1)S(1)}, bf16[640,256]{1,0:T(8,128)(2,1)}, u32[]{:S(2)}) copy-start(bf16[640,256]{1,0:T(8,128)(2,1)} %get-tuple-element.36) | copy-start | bytes 983044
  7.0 18.5 %copy-start.8 = (s32[640]{0:T(1024)S(1)}, s32[640]{0:T(1024)}, u32[]{:S(2)}) copy-start(s32[640]{0:T(1024)} %param.16) | copy-start | bytes 7684
  7.0 21.3 %copy-start.10 = (bf16[640,256]{1,0:T(8,128)(2,1)S(1)}, bf16[640,256]{1,0:T(8,128)(2,1)}, u32[]{:S(2)}) copy-start(bf16[640,256]{1,0:T(8,128)(2,1)} %get-tuple-element.45) | copy-start | bytes 983044
  15.9 13.9 %copy-start.11 = (bf16[640,256]{1,0:T(8,128)(2,1)}, bf16[640,256]{1,0:T(8,128)(2,1)S(1)}, u32[]{:S(2)}) copy-start(bf16[640,256]{1,0:T(8,128)(2,1)S(1)} %collective-permute-done.1.refs_4_) | copy-start | bytes 983044
  15.9 12.4 %collective-permute-start.2 = (bf16[640,256]{1,0:T(8,128)(2,1)S(1)}, bf16[640,256]{1,0:T(8,128)(2,1)}, u32[]{:S(2)}, u32[]{:S(2)}) collective-permute-start(bf16[640,256]{1,0:T(8,128)(2,1)S(1)} %collective-permute-done.1.refs_4_), channel_id=1, source_target_pairs={{0,16},{16,0},{1,17},{17,1},{2,18},{18,2},{3,19},{19,3},{4,20},{20... | collective-permute-start | bytes 983048 | tf_op jit(solution)/shard_map/ppermute | solution.py:519
  18.8 10.9 %collective-permute-start.3 = (bf16[640,256]{1,0:T(8,128)(2,1)S(1)}, bf16[640,256]{1,0:T(8,128)(2,1)}, u32[]{:S(2)}, u32[]{:S(2)}) collective-permute-start(bf16[640,256]{1,0:T(8,128)(2,1)S(1)} %collective-permute-done.1.refs_4_), channel_id=1, source_target_pairs={{0,4},{4,0},{8,12},{12,8},{1,5},{5,1},{9,13},{13,9},{2,6},{6,2},{1... | collective-permute-start | bytes 983048 | tf_op jit(solution)/shard_map/ppermute | solution.py:520
  20.4 9.3 %collective-permute-start.4 = (bf16[640,256]{1,0:T(8,128)(2,1)S(1)}, bf16[640,256]{1,0:T(8,128)(2,1)}, u32[]{:S(2)}, u32[]{:S(2)}) collective-permute-start(bf16[640,256]{1,0:T(8,128)(2,1)S(1)} %copy-done.13), channel_id=1, source_target_pairs={{0,2},{2,0},{1,3},{3,1},{4,6},{6,4},{5,7},{7,5},{8,10},{10,8},{9,1... | collective-permute-start | bytes 983048 | tf_op jit(solution)/shard_map/ppermute | solution.py:502
  21.9 7.8 %copy-start.9 = (bf16[640,256]{1,0:T(8,128)(2,1)}, bf16[640,256]{1,0:T(8,128)(2,1)S(1)}, u32[]{:S(2)}) copy-start(bf16[640,256]{1,0:T(8,128)(2,1)S(1)} %collective-permute-done.5.refs_13_.refs_4_) | copy-start | bytes 983044
  21.9 20.6 %collective-permute-start.6 = (bf16[640,256]{1,0:T(8,128)(2,1)S(1)}, bf16[640,256]{1,0:T(8,128)(2,1)S(1)}, u32[]{:S(2)}, u32[]{:S(2)}) collective-permute-start(bf16[640,256]{1,0:T(8,128)(2,1)S(1)} %collective-permute-done.5.refs_13_.refs_4_), channel_id=1, source_target_pairs={{0,16},{16,0},{1,17},{17,1},{2,18},{18,2},{3,19},{19,3},{4,20},{20... | collective-permute-start | bytes 983048 | tf_op jit(solution)/shard_map/ppermute | solution.py:519
  23.8 18.7 %collective-permute-start.7 = (bf16[640,256]{1,0:T(8,128)(2,1)S(1)}, bf16[640,256]{1,0:T(8,128)(2,1)}, u32[]{:S(2)}, u32[]{:S(2)}) collective-permute-start(bf16[640,256]{1,0:T(8,128)(2,1)S(1)} %collective-permute-done.5.refs_13_.refs_4_), channel_id=1, source_target_pairs={{0,4},{4,0},{8,12},{12,8},{1,5},{5,1},{9,13},{13,9},{2,6},{6,2},{1... | collective-permute-start | bytes 983048 | tf_op jit(solution)/shard_map/ppermute | solution.py:520
  28.2 14.3 %collective-permute-start.8 = (bf16[640,256]{1,0:T(8,128)(2,1)S(1)}, bf16[640,256]{1,0:T(8,128)(2,1)}, u32[]{:S(2)}, u32[]{:S(2)}) collective-permute-start(bf16[640,256]{1,0:T(8,128)(2,1)S(1)} %copy-done.10), channel_id=1, source_target_pairs={{0,2},{2,0},{1,3},{3,1},{4,6},{6,4},{5,7},{7,5},{8,10},{10,8},{9,1... | collective-permute-start | bytes 983048 | tf_op jit(solution)/shard_map/ppermute | solution.py:503
  36.9 24.3 %all-to-all-start = ((bf16[8,112,256]{2,1,0:T(8,128)(2,1)}), bf16[8,112,256]{2,1,0:T(8,128)(2,1)S(1)}, u32[]{:S(2)}, u32[]{:S(2)}) async-start(bf16[8,112,256]{2,1,0:T(8,128)(2,1)} %far_part.2.refs_10_), calls=%async_computation | async-start | bytes 917504 | tf_op jit(solution)/shard_map/all_to_all | solution.py:485
  42.5 0.7 %copy-start.12 = (bf16[640,256]{1,0:T(8,128)(2,1)}, bf16[640,256]{1,0:T(8,128)(2,1)S(1)}, u32[]{:S(2)}) copy-start(bf16[640,256]{1,0:T(8,128)(2,1)S(1)} %collective-permute-done.6.refs_5_) | copy-start | bytes 983044
  49.9 9.7 %collective-permute-start.10 = (bf16[96,256]{1,0:T(8,128)(2,1)}, bf16[96,256]{1,0:T(8,128)(2,1)S(1)}, u32[]{:S(2)}, u32[]{:S(2)}) collective-permute-start(bf16[96,256]{1,0:T(8,128)(2,1)} %get-tuple-element.48), channel_id=1, source_target_pairs={{0,4},{2,6},{4,0},{6,2},{8,12},{10,14},{12,8},{14,10},{1,5},{3,7},... | collective-permute-start | bytes 147464 | tf_op jit(solution)/shard_map/ppermute | solution.py:577
  52.0 9.1 %collective-permute-start.11 = (bf16[96,256]{1,0:T(8,128)(2,1)}, bf16[96,256]{1,0:T(8,128)(2,1)S(1)}, u32[]{:S(2)}, u32[]{:S(2)}) collective-permute-start(bf16[96,256]{1,0:T(8,128)(2,1)} %get-tuple-element.49), channel_id=1, source_target_pairs={{0,6},{2,4},{4,2},{6,0},{8,14},{10,12},{12,10},{14,8},{1,7},{3,5},... | collective-permute-start | bytes 147464 | tf_op jit(solution)/shard_map/ppermute | solution.py:577
  53.5 10.7 %collective-permute-start.12 = (bf16[96,256]{1,0:T(8,128)(2,1)}, bf16[96,256]{1,0:T(8,128)(2,1)S(1)}, u32[]{:S(2)}, u32[]{:S(2)}) collective-permute-start(bf16[96,256]{1,0:T(8,128)(2,1)} %get-tuple-element.50), channel_id=1, source_target_pairs={{0,8},{2,10},{4,12},{6,14},{8,0},{10,2},{12,4},{14,6},{1,9},{3,11}... | collective-permute-start | bytes 147464 | tf_op jit(solution)/shard_map/ppermute | solution.py:577
  55.8 8.3 %collective-permute-start.13 = (bf16[96,256]{1,0:T(8,128)(2,1)}, bf16[96,256]{1,0:T(8,128)(2,1)S(1)}, u32[]{:S(2)}, u32[]{:S(2)}) collective-permute-start(bf16[96,256]{1,0:T(8,128)(2,1)} %get-tuple-element.51), channel_id=1, source_target_pairs={{0,10},{2,8},{4,14},{6,12},{8,2},{10,0},{12,6},{14,4},{1,11},{3,9}... | collective-permute-start | bytes 147464 | tf_op jit(solution)/shard_map/ppermute | solution.py:577
  55.9 8.2 %collective-permute-start.14 = (bf16[96,256]{1,0:T(8,128)(2,1)}, bf16[96,256]{1,0:T(8,128)(2,1)S(1)}, u32[]{:S(2)}, u32[]{:S(2)}) collective-permute-start(bf16[96,256]{1,0:T(8,128)(2,1)} %get-tuple-element.52), channel_id=1, source_target_pairs={{0,12},{2,14},{4,8},{6,10},{8,4},{10,6},{12,0},{14,2},{1,13},{3,15... | collective-permute-start | bytes 147464 | tf_op jit(solution)/shard_map/ppermute | solution.py:577
  59.7 7.0 %copy-start.1 = (bf16[96,256]{1,0:T(8,128)(2,1)}, bf16[96,256]{1,0:T(8,128)(2,1)S(1)}, u32[]{:S(2)}) copy-start(bf16[96,256]{1,0:T(8,128)(2,1)S(1)} %collective-permute-done.10.refs_2_) | copy-start | bytes 147460
  59.7 7.0 %collective-permute-start.15 = (bf16[96,256]{1,0:T(8,128)(2,1)}, bf16[96,256]{1,0:T(8,128)(2,1)S(1)}, u32[]{:S(2)}, u32[]{:S(2)}) collective-permute-start(bf16[96,256]{1,0:T(8,128)(2,1)} %get-tuple-element.53), channel_id=1, source_target_pairs={{0,14},{2,12},{4,10},{6,8},{8,6},{10,4},{12,2},{14,0},{1,15},{3,13... | collective-permute-start | bytes 147464 | tf_op jit(solution)/shard_map/ppermute | solution.py:577
  61.1 5.6 %copy-start.2 = (bf16[96,256]{1,0:T(8,128)(2,1)}, bf16[96,256]{1,0:T(8,128)(2,1)S(1)}, u32[]{:S(2)}) copy-start(bf16[96,256]{1,0:T(8,128)(2,1)S(1)} %collective-permute-done.11.refs_3_) | copy-start | bytes 147460
  61.1 5.5 %collective-permute-start.9 = (bf16[96,256]{1,0:T(8,128)(2,1)}, bf16[96,256]{1,0:T(8,128)(2,1)S(1)}, u32[]{:S(2)}, u32[]{:S(2)}) collective-permute-start(bf16[96,256]{1,0:T(8,128)(2,1)} %get-tuple-element.47), channel_id=1, source_target_pairs={{0,2},{2,0},{4,6},{6,4},{8,10},{10,8},{12,14},{14,12},{1,3},{3,1},... | collective-permute-start | bytes 147464 | tf_op jit(solution)/shard_map/ppermute | solution.py:577
  61.2 0.8 %copy-start = (bf16[8,112,256]{2,1,0:T(8,128)(2,1)}, bf16[8,112,256]{2,1,0:T(8,128)(2,1)S(1)}, u32[]{:S(2)}) copy-start(bf16[8,112,256]{2,1,0:T(8,128)(2,1)S(1)} %all-to-all-done.came_ref) | copy-start | bytes 1376260
  64.1 2.6 %copy-start.3 = (bf16[96,256]{1,0:T(8,128)(2,1)}, bf16[96,256]{1,0:T(8,128)(2,1)S(1)}, u32[]{:S(2)}) copy-start(bf16[96,256]{1,0:T(8,128)(2,1)S(1)} %collective-permute-done.12.refs_4_) | copy-start | bytes 147460
  64.1 2.6 %copy-start.4 = (bf16[96,256]{1,0:T(8,128)(2,1)}, bf16[96,256]{1,0:T(8,128)(2,1)S(1)}, u32[]{:S(2)}) copy-start(bf16[96,256]{1,0:T(8,128)(2,1)S(1)} %collective-permute-done.13.refs_5_) | copy-start | bytes 147460
  64.1 2.6 %copy-start.5 = (bf16[96,256]{1,0:T(8,128)(2,1)}, bf16[96,256]{1,0:T(8,128)(2,1)S(1)}, u32[]{:S(2)}) copy-start(bf16[96,256]{1,0:T(8,128)(2,1)S(1)} %collective-permute-done.14.refs_6_) | copy-start | bytes 147460
  66.7 0.6 copy-start.6
  66.7 0.6 copy-start.7

commit v4 on v3

--- a/solution.py
+++ b/solution.py
@@ -16,7 +16,9 @@
 epsilon = 1e-05
 rope_base = 1000000.0
 VMEM_BYTES = 62 * 1024 * 1024
+VMEM_PLACE = 16 * 1024 * 1024
 NEAR_STEP = 128
+NEAR_AHEAD = 4
 NEAR_COST = 20_000_000_000
 FAR_COST = 20_000_000_000
 
@@ -51,15 +53,14 @@
     return jnp.cos(angles), jnp.sin(angles)
 
 
-def cut_kernel(key_ref, value_ref, *refs):
-    outs, sems = refs[:4], refs[4]
+def cut_kernel(opposite, *refs):
+    count = len(opposite)
+    sources, outs, sems = refs[:count], refs[count : 2 * count], refs[-1]
     quarter = outs[0].shape[0]
-    mine = 2 * lax.axis_index("groups") + lax.rem(lax.axis_index("rep"), 2)
+    mine, last = quarter_numbers()[0], quarter_numbers()[3]
     copies = []
-    for index, (source, which) in enumerate(
-        ((key_ref, mine), (value_ref, mine), (key_ref, 3 - mine), (value_ref, 3 - mine))
-    ):
-        start = pl.multiple_of(which * quarter, quarter)
+    for index, source in enumerate(sources):
+        start = pl.multiple_of((last if opposite[index] else mine) * quarter, quarter)
         copy = pltpu.make_async_copy(
             source.at[pl.ds(start, quarter), :], outs[index], sems.at[index]
         )
@@ -69,18 +70,19 @@
         copy.wait()
 
 
-def cut_quarters(key_weight, value_weight):
-    depth, columns = key_weight.shape
-    piece = jax.ShapeDtypeStruct((depth // 4, columns), key_weight.dtype)
+def cut_quarters(weights, opposite):
+    count = len(weights)
+    depth, columns = weights[0].shape
+    piece = jax.ShapeDtypeStruct((depth // 4, columns), weights[0].dtype)
     return pl.pallas_call(
-        cut_kernel,
-        out_shape=(piece,) * 4,
-        in_specs=[pl.BlockSpec(memory_space=pl.ANY)] * 2,
-        out_specs=(pl.BlockSpec(memory_space=pltpu.VMEM),) * 4,
-        scratch_shapes=[pltpu.SemaphoreType.DMA((4,))],
+        functools.partial(cut_kernel, opposite),
+        out_shape=(piece,) * count,
+        in_specs=[pl.BlockSpec(memory_space=pl.ANY)] * count,
+        out_specs=(pl.BlockSpec(memory_space=pltpu.VMEM),) * count,
+        scratch_shapes=[pltpu.SemaphoreType.DMA((count,))],
         compiler_params=pltpu.CompilerParams(vmem_limit_bytes=VMEM_BYTES),
         name="cut_quarters",
-    )(key_weight, value_weight)
+    )(*weights)
 
 
 def near_kernel(
@@ -128,8 +130,8 @@
             for copy in read(index):
                 copy.start()
 
-    start(0)
-    start(1)
+    for index in range(NEAR_AHEAD):
+        start(index)
     lanes = 128
     near_first = lax.axis_index("fsdp") * depth
     side = near_first // width
@@ -139,7 +141,7 @@
     for index in range(blocks):
         for copy in read(index):
             copy.wait()
-        start(index + 2)
+        start(index + NEAR_AHEAD)
         here = pl.ds(index * size, size)
         squares = jnp.zeros((size, lanes), jnp.float32)
         for source in (own_buf, got_buf):
@@ -407,59 +409,64 @@
     )(block_counts, dest_slots, after)
 
 
-def place_kernel(came_ref, put_ref, out_ref):
+def put_rows(slots, rows_ref, owned):
+    slot = lax.broadcasted_iota(jnp.int32, (owned, slots.shape[1]), 0)
+    put = jnp.where(slot == slots, 1.0, 0.0).astype(jnp.bfloat16)
+    return jnp.dot(put, rows_ref[: slots.shape[1], :], preferred_element_type=jnp.float32)
+
+
+def place_kernel(came_ref, values_ref, slots_ref, started_ref, out_ref):
     devices, tall, columns = came_ref.shape
     most_rows = tall - 16
     owned = out_ref.shape[0]
     total = jnp.zeros(out_ref.shape, jnp.float32)
-    slot = lax.broadcasted_iota(jnp.int32, (owned, most_rows), 0)
     me = group_index()
     for other in range(devices):
         source = lax.bitwise_xor(me, other)
-        marks = came_ref[source, most_rows:, :].astype(jnp.float32)[0:1, :most_rows]
-        put = jnp.where(slot == marks.astype(jnp.int32), 1.0, 0.0).astype(jnp.bfloat16)
-        put_ref[other, :, :most_rows] = put
-        total += jnp.dot(put, came_ref[source, :most_rows, :], preferred_element_type=jnp.float32)
+        marks = came_ref[source, most_rows:, :].astype(jnp.float32)[0:8].astype(jnp.int32)
+        slots_ref[other] = marks[:, :128]
+        total += put_rows(marks[0:1, :most_rows], came_ref.at[source], owned)
+        if other == 0:
+            started_ref[...] = put_rows(marks[0:1, :most_rows], values_ref, owned)
     out_ref[...] = total.astype(jnp.bfloat16)
 
 
-def place_keys(came):
+def place_keys(came, own_values):
     devices, tall, columns = came.shape
     vmem = pl.BlockSpec(memory_space=pltpu.VMEM)
     return pl.pallas_call(
         place_kernel,
         out_shape=(
-            jax.ShapeDtypeStruct((devices, OWN_DEV, 128), jnp.bfloat16),
+            jax.ShapeDtypeStruct((devices, 8, 128), jnp.int32),
+            jax.ShapeDtypeStruct((OWN_DEV, columns), jnp.float32),
             jax.ShapeDtypeStruct((OWN_DEV, columns), jnp.bfloat16),
         ),
-        in_specs=[vmem],
-        out_specs=(vmem,) * 2,
-        compiler_params=pltpu.CompilerParams(vmem_limit_bytes=VMEM_BYTES),
+        in_specs=[vmem] * 2,
+        out_specs=(vmem,) * 3,
+        compiler_params=pltpu.CompilerParams(vmem_limit_bytes=VMEM_PLACE),
         name="place_keys",
-    )(came)
-
-
-def place_values_kernel(put_ref, *refs):
+    )(came, own_values)
+
+
+def place_values_kernel(slots_ref, started_ref, *refs):
     out_ref = refs[-1]
-    most_rows = refs[0].shape[0]
-    total = jnp.zeros(out_ref.shape, jnp.float32)
+    total = started_ref[...]
     for other, rows_ref in enumerate(refs[:-1]):
-        total += jnp.dot(
-            put_ref[other, :, :most_rows], rows_ref[...], preferred_element_type=jnp.float32
-        )
+        slots = slots_ref[other + 1, 0:1, : rows_ref.shape[0]]
+        total += put_rows(slots, rows_ref, out_ref.shape[0])
     out_ref[...] = total.astype(jnp.bfloat16)
 
 
-def place_values(put, came):
+def place_values(slots, started, came):
     vmem = pl.BlockSpec(memory_space=pltpu.VMEM)
     return pl.pallas_call(
         place_values_kernel,
-        out_shape=jax.ShapeDtypeStruct((OWN_DEV, came[0].shape[1]), jnp.bfloat16),
-        in_specs=[vmem] * (1 + len(came)),
+        out_shape=jax.ShapeDtypeStruct(started.shape, jnp.bfloat16),
+        in_specs=[vmem] * (2 + len(came)),
         out_specs=vmem,
-        compiler_params=pltpu.CompilerParams(vmem_limit_bytes=VMEM_BYTES),
+        compiler_params=pltpu.CompilerParams(vmem_limit_bytes=VMEM_PLACE),
         name="place_values",
-    )(put, *came)
+    )(slots, started, *came)
 
 
 def local(
@@ -495,7 +502,10 @@
     )
     swap = [(0, 1), (1, 0)]
     if relayed:
-        key_own, value_own, key_last, value_last = cut_quarters(key_weight, value_weight)
+        (key_own,) = cut_quarters((key_weight,), (False,))
+        value_own, key_last, value_last = cut_quarters(
+            (value_weight, key_weight, value_weight), (False, True, True)
+        )
         key_own = lax.ppermute(key_own, "fsdp", swap)
         value_own = lax.ppermute(value_own, "fsdp", swap)
         got, key_last, value_last = ordered(got, key_last, value_last)
@@ -577,8 +587,8 @@
             came_values[other] = lax.ppermute(
                 send_values[other], axes, [(i, i ^ other) for i in range(devices)]
             )
-        put, cache_keys = place_keys(came_keys)
-        return cache_keys, place_values(put, came_values)
+        slots, started, cache_keys = place_keys(came_keys, send_values[0])
+        return cache_keys, place_values(slots, started, came_values[1:])
     came_values = exchange(send_values[0])
     if inline:
         got_marks = came_keys[:, most_rows, :most_rows].reshape(capacity)

time: 70.1 us -> 67.5 us (0.963)
  Pallas kernels: 31.1 us -> 29.3 us
    pallas_call x1, Pallas kernels: 8.88 us -> 7.76 us  [near_part(): pl.pallas_call(near_kernel, out_shape=(sums, sums, jax.ShapeDtypeStruct((...]
    ppermute x7, waiting for transfers between devices: 2.52 us -> 3.54 us  [local(): lax.ppermute(send_values[other], axes, [(i, i ^ other) for i in range(dev...]
    ppermute x1, waiting for transfers between devices: 0.76 us -> 0.01 us  [local(): got = lax.ppermute(tokens, 'tp', [(0, 1), (1, 0)])]
    pallas_call x3 -> x4, Pallas kernels: 6.72 us -> 6.02 us  [the longest x2 3.86 us: cut_quarters(): pl.pallas_call(functools.partial(cut_kernel, opposite), out_shape=(piece,...]
    unnamed x28 -> x14, local copies, waits for them, and re-layouts: 2.13 us -> 1.62 us
where the time goes in v4:
time: 67.5 us; the launch traced here: 67 us
  starting transfers between devices  30.6 us (45%)
  Pallas kernels  29.3 us (43%)
  waiting for transfers between devices  3.76 us (6%)
  local copies, waits for them, and re-layouts  1.62 us (2%)
  other arithmetic  1.04 us (2%)
  between operations  0.76 us (1%)
    pallas_call x2, Pallas kernels, far_part(): pl.pallas_call(functools.partial(far_kernel, relayed, bool(angles), tall,...  13.8 us
    ppermute x7, starting transfers between devices, local(): lax.ppermute(send_values[other], axes, [(i, i ^ other) for i in range(dev...  11.3 us
    pallas_call x1, Pallas kernels, near_part(): pl.pallas_call(near_kernel, out_shape=(sums, sums, jax.ShapeDtypeStruct((...  7.76 us
    all_to_all x1, starting transfers between devices, exchange(): lax.all_to_all(rows_by_owner, axes, split_axis=0, concat_axis=0, tiled=True)  5.52 us
    ppermute x2, starting transfers between devices, pieces_of(): by_group = lax.ppermute(own, 'groups', swap)  4.38 us
    pallas_call x2, Pallas kernels, cut_quarters(): pl.pallas_call(functools.partial(cut_kernel, opposite), out_shape=(piece,...  3.86 us
    ppermute x7, waiting for transfers between devices, local(): lax.ppermute(send_values[other], axes, [(i, i ^ other) for i in range(dev...  3.54 us
    ppermute x2, starting transfers between devices, pieces_of(): by_rep = lax.ppermute(own, 'rep', across)  3.15 us
  transfers between devices with their start and end apart: 17, of which 2 were waited for; matrix products, arithmetic and copies ran while one was open for 2% of the time, Pallas kernels for 42%

profile of v4, /device:TPU:0, one launch (start us, length us, event | category | flops | bytes accessed | tf_op | source)
XLA Modules:
  0.0 67.0 jit_solution(17522557925119392931)
XLA Ops:
  0.6 0.5 collective-permute-start
  1.1 1.7 %cut_quarters.3 = bf16[640,256]{1,0:T(8,128)(2,1)} custom-call(bf16[2560,256]{1,0:T(8,128)(2,1)} %refs_0_.5), custom_call_target="tpu_custom_call" | custom-call | tf_op jit(solution)/shard_map/cut_quarters/pallas_call | solution.py:77
  2.9 2.6 %collective-permute-start.1 = (bf16[640,256]{1,0:T(8,128)(2,1)}, bf16[640,256]{1,0:T(8,128)(2,1)S(1)}, u32[]{:S(2)}, u32[]{:S(2)}) collective-permute-start(bf16[640,256]{1,0:T(8,128)(2,1)} %cut_quarters.3), channel_id=1, source_target_pairs={{0,2},{2,0},{1,3},{3,1},{4,6},{6,4},{5,7},{7,5},{8,10},{10,8},{9,1... | collective-permute-start | bytes 983048 | tf_op jit(solution)/shard_map/ppermute | solution.py:509
  5.5 2.1 %cut_quarters.2 = (bf16[640,256]{1,0:T(8,128)(2,1)}, bf16[640,256]{1,0:T(8,128)(2,1)}, bf16[640,256]{1,0:T(8,128)(2,1)}) custom-call(bf16[2560,256]{1,0:T(8,128)(2,1)} %value_ref.1, bf16[2560,256]{1,0:T(8,128)(2,1)} %refs_0_.5, bf16[2560,256]{1,0:T(8,128)(2,1)} %value_ref.1), custom_call_target="tpu_custom_call" | custom-call | tf_op jit(solution)/shard_map/cut_quarters/pallas_call | solution.py:77
  7.6 0.1 collective-permute-start.5
  7.7 0.0 collective-permute-done.got_ref.refs_1_
  7.7 0.0 copy-start.1
  7.7 0.0 copy-start.3
  7.7 7.8 %near_part.1 = (f32[640,256]{1,0:T(8,128)}, f32[640,256]{1,0:T(8,128)}, f32[640,128]{1,0:T(8,128)}) custom-call(bf16[640,2560]{1,0:T(8,128)(2,1)} %refs_0_.7, bf16[640,2560]{1,0:T(8,128)(2,1)} %collective-permute-done.got_ref.refs_1_, bf16[2560,256]{1,0:T(8,128)(2,1)} %refs_0_.5, bf16[2560,256]{1,0:T(8,128)(2,1)} %value_ref.1, bf16[5120]{0:T(1024)(128)(2,1)} %refs_8_.3, ...), custom_call_target="tpu_custom_call" | custom-call | flops 20000000000 | bytes 12451840 | tf_op jit(solution)/shard_map/near_part/pallas_call | solution.py:192
  15.5 0.0 collective-permute-done.1.refs_4_
  15.5 0.0 copy-start.4
  15.5 2.2 %collective-permute-start.2 = (bf16[640,256]{1,0:T(8,128)(2,1)S(1)}, bf16[640,256]{1,0:T(8,128)(2,1)}, u32[]{:S(2)}, u32[]{:S(2)}) collective-permute-start(bf16[640,256]{1,0:T(8,128)(2,1)S(1)} %collective-permute-done.1.refs_4_), channel_id=1, source_target_pairs={{0,16},{16,0},{1,17},{17,1},{2,18},{18,2},{3,19},{19,3},{4,20},{20... | collective-permute-start | bytes 983048 | tf_op jit(solution)/shard_map/ppermute | solution.py:529
  17.7 1.6 %collective-permute-start.3 = (bf16[640,256]{1,0:T(8,128)(2,1)S(1)}, bf16[640,256]{1,0:T(8,128)(2,1)}, u32[]{:S(2)}, u32[]{:S(2)}) collective-permute-start(bf16[640,256]{1,0:T(8,128)(2,1)S(1)} %collective-permute-done.1.refs_4_), channel_id=1, source_target_pairs={{0,4},{4,0},{8,12},{12,8},{1,5},{5,1},{9,13},{13,9},{2,6},{6,2},{1... | collective-permute-start | bytes 983048 | tf_op jit(solution)/shard_map/ppermute | solution.py:530
  19.3 1.5 %collective-permute-start.4 = (bf16[640,256]{1,0:T(8,128)(2,1)}, bf16[640,256]{1,0:T(8,128)(2,1)}, u32[]{:S(2)}, u32[]{:S(2)}) collective-permute-start(bf16[640,256]{1,0:T(8,128)(2,1)} %get-tuple-element.35), channel_id=1, source_target_pairs={{0,2},{2,0},{1,3},{3,1},{4,6},{6,4},{5,7},{7,5},{8,10},{10,8},{9,1... | collective-permute-start | bytes 983048 | tf_op jit(solution)/shard_map/ppermute | solution.py:512
  20.8 0.2 collective-permute-done.5.refs_13_.refs_4_
  21.0 0.0 copy-start.2
  21.0 2.2 %collective-permute-start.6 = (bf16[640,256]{1,0:T(8,128)(2,1)S(1)}, bf16[640,256]{1,0:T(8,128)(2,1)S(1)}, u32[]{:S(2)}, u32[]{:S(2)}) collective-permute-start(bf16[640,256]{1,0:T(8,128)(2,1)S(1)} %collective-permute-done.5.refs_13_.refs_4_), channel_id=1, source_target_pairs={{0,16},{16,0},{1,17},{17,1},{2,18},{18,2},{3,19},{19,3},{4,20},{20... | collective-permute-start | bytes 983048 | tf_op jit(solution)/shard_map/ppermute | solution.py:529
  23.2 1.6 %collective-permute-start.7 = (bf16[640,256]{1,0:T(8,128)(2,1)S(1)}, bf16[640,256]{1,0:T(8,128)(2,1)S(1)}, u32[]{:S(2)}, u32[]{:S(2)}) collective-permute-start(bf16[640,256]{1,0:T(8,128)(2,1)S(1)} %collective-permute-done.5.refs_13_.refs_4_), channel_id=1, source_target_pairs={{0,4},{4,0},{8,12},{12,8},{1,5},{5,1},{9,13},{13,9},{2,6},{6,2},{1... | collective-permute-start | bytes 983048 | tf_op jit(solution)/shard_map/ppermute | solution.py:530
  24.8 0.0 copy-done.1
  24.8 1.7 %route.1 = (s32[8,640]{1,0:T(8,128)}, bf16[8,16,256]{2,1,0:T(8,128)(2,1)}) custom-call(s32[8]{0:T(128)} %counts_ref.1, s32[640]{0:T(1024)} %dest_ref.1, f32[640,256]{1,0:T(8,128)} %get-tuple-element.41.after_ref.refs_2_), custom_call_target="tpu_custom_call" | custom-call | tf_op jit(solution)/shard_map/route/pallas_call | solution.py:395
  26.5 1.0 %multiply_sine_fusion = (f32[32,640]{1,0:T(8,128)}, f32[32,640]{1,0:T(8,128)}) fusion(f32[640]{0:T(1024)S(1)} %convert_element_type.3, f32[32]{0:T(128)S(1)} %multiply_power_fusion), kind=kLoop, calls=%fused_computation | loop fusion | flops 20480 | bytes 166528 | tf_op jit(solution)/shard_map/sin | solution.py:53
  27.6 0.0 collective-permute-done.2.refs_5_
  27.6 0.0 copy-done.3
  27.6 1.5 %collective-permute-start.8 = (bf16[640,256]{1,0:T(8,128)(2,1)S(1)}, bf16[640,256]{1,0:T(8,128)(2,1)}, u32[]{:S(2)}, u32[]{:S(2)}) collective-permute-start(bf16[640,256]{1,0:T(8,128)(2,1)S(1)} %copy-done.3), channel_id=1, source_target_pairs={{0,2},{2,0},{1,3},{3,1},{4,6},{6,4},{5,7},{7,5},{8,10},{10,8},{9,1... | collective-permute-start | bytes 983048 | tf_op jit(solution)/shard_map/ppermute | solution.py:513
  29.1 0.0 collective-permute-done.3.refs_6_
  29.1 0.0 collective-permute-done.4.refs_7_
  29.1 0.0 copy-done.4
  29.1 0.0 copy-done.2
  29.1 7.1 %far_part.2.refs_10_ = bf16[8,112,256]{2,1,0:T(8,128)(2,1)} custom-call(bf16[640,2560]{1,0:T(8,128)(2,1)} %refs_0_.7, bf16[640,2560]{1,0:T(8,128)(2,1)} %collective-permute-done.got_ref.refs_1_, f32[640,256]{1,0:T(8,128)} %get-tuple-element.31.refs_2_, f32[640,128]{1,0:T(8,128)} %get-tuple-element.32.refs_3_, bf16[640,256]{1,0:T(8,128)(2,1)} %copy-done.4, ...), custom_call_target="tpu_custom_call" | custom-call | flops 20000000000 | bytes 1966080 | tf_op jit(solution)/shard_map/far_part/pallas_call | solution.py:335
  36.2 5.5 %all-to-all-start = ((bf16[8,112,256]{2,1,0:T(8,128)(2,1)}), bf16[8,112,256]{2,1,0:T(8,128)(2,1)S(1)}, u32[]{:S(2)}, u32[]{:S(2)}) async-start(bf16[8,112,256]{2,1,0:T(8,128)(2,1)} %far_part.2.refs_10_), calls=%async_computation | async-start | bytes 917504 | tf_op jit(solution)/shard_map/all_to_all | solution.py:492
  41.7 0.0 collective-permute-done.6.refs_5_
  41.7 0.0 copy-start.5
  41.8 0.0 collective-permute-done.7.refs_6_
  41.8 0.0 copy-start.6
  41.8 0.0 collective-permute-done.8.refs_7_
  41.8 0.7 %copy-done.5 = bf16[640,256]{1,0:T(8,128)(2,1)} copy-done((bf16[640,256]{1,0:T(8,128)(2,1)}, bf16[640,256]{1,0:T(8,128)(2,1)S(1)}, u32[]{:S(2)}) %copy-start.5) | copy-done | bytes 327704
  42.5 0.1 copy-done.6
  42.6 6.6 %far_part.3 = (bf16[96,256]{1,0:T(8,128)(2,1)}, bf16[96,256]{1,0:T(8,128)(2,1)}, bf16[96,256]{1,0:T(8,128)(2,1)}, bf16[96,256]{1,0:T(8,128)(2,1)}, bf16[96,256]{...) custom-call(bf16[640,2560]{1,0:T(8,128)(2,1)} %refs_0_.7, ...), custom_call_target="tpu_custom_call" | custom-call | flops 20000000000 | bytes 1966080 | tf_op jit(solution)/shard_map/far_part/pallas_call | solution.py:335
  49.2 2.1 %collective-permute-start.10 = (bf16[96,256]{1,0:T(8,128)(2,1)}, bf16[96,256]{1,0:T(8,128)(2,1)S(1)}, u32[]{:S(2)}, u32[]{:S(2)}) collective-permute-start(bf16[96,256]{1,0:T(8,128)(2,1)} %get-tuple-element.48), channel_id=1, source_target_pairs={{0,4},{2,6},{4,0},{6,2},{8,12},{10,14},{12,8},{14,10},{1,5},{3,7},... | collective-permute-start | bytes 147464 | tf_op jit(solution)/shard_map/ppermute | solution.py:587
  51.3 1.5 %collective-permute-start.11 = (bf16[96,256]{1,0:T(8,128)(2,1)}, bf16[96,256]{1,0:T(8,128)(2,1)S(1)}, u32[]{:S(2)}, u32[]{:S(2)}) collective-permute-start(bf16[96,256]{1,0:T(8,128)(2,1)} %get-tuple-element.49), channel_id=1, source_target_pairs={{0,6},{2,4},{4,2},{6,0},{8,14},{10,12},{12,10},{14,8},{1,7},{3,5},... | collective-permute-start | bytes 147464 | tf_op jit(solution)/shard_map/ppermute | solution.py:587
  52.8 2.4 %collective-permute-start.12 = (bf16[96,256]{1,0:T(8,128)(2,1)}, bf16[96,256]{1,0:T(8,128)(2,1)S(1)}, u32[]{:S(2)}, u32[]{:S(2)}) collective-permute-start(bf16[96,256]{1,0:T(8,128)(2,1)} %get-tuple-element.50), channel_id=1, source_target_pairs={{0,8},{2,10},{4,12},{6,14},{8,0},{10,2},{12,4},{14,6},{1,9},{3,11}... | collective-permute-start | bytes 147464 | tf_op jit(solution)/shard_map/ppermute | solution.py:587
  55.2 0.1 collective-permute-start.13
  55.2 3.7 %collective-permute-start.14 = (bf16[96,256]{1,0:T(8,128)(2,1)}, bf16[96,256]{1,0:T(8,128)(2,1)S(1)}, u32[]{:S(2)}, u32[]{:S(2)}) collective-permute-start(bf16[96,256]{1,0:T(8,128)(2,1)} %get-tuple-element.52), channel_id=1, source_target_pairs={{0,12},{2,14},{4,8},{6,10},{8,4},{10,6},{12,0},{14,2},{1,13},{3,15... | collective-permute-start | bytes 147464 | tf_op jit(solution)/shard_map/ppermute | solution.py:587
  59.0 0.0 collective-permute-done.10.refs_1_
  59.0 1.5 %collective-permute-start.15 = (bf16[96,256]{1,0:T(8,128)(2,1)}, bf16[96,256]{1,0:T(8,128)(2,1)S(1)}, u32[]{:S(2)}, u32[]{:S(2)}) collective-permute-start(bf16[96,256]{1,0:T(8,128)(2,1)} %get-tuple-element.53), channel_id=1, source_target_pairs={{0,14},{2,12},{4,10},{6,8},{8,6},{10,4},{12,2},{14,0},{1,15},{3,13... | collective-permute-start | bytes 147464 | tf_op jit(solution)/shard_map/ppermute | solution.py:587
  60.4 0.0 collective-permute-done.11.refs_2_
  60.5 0.1 collective-permute-start.9
  60.5 0.0 all-to-all-done.came_ref
  60.5 0.0 copy-start
  60.5 0.8 %copy-done = bf16[96,256]{1,0:T(8,128)(2,1)S(1)} copy-done((bf16[96,256]{1,0:T(8,128)(2,1)S(1)}, bf16[96,256]{1,0:T(8,128)(2,1)}, u32[]{:S(2)}) %copy-start) | copy-done | bytes 49176
  61.3 1.1 %place_keys.1 = (s32[8,8,128]{2,1,0:T(8,128)S(1)}, f32[256,256]{1,0:T(8,128)S(1)}, bf16[256,256]{1,0:T(8,128)(2,1)}) custom-call(bf16[8,112,256]{2,1,0:T(8,128)(2,1)S(1)} %all-to-all-done.came_ref, bf16[96,256]{1,0:T(8,128)(2,1)S(1)} %copy-done), custom_call_target="tpu_custom_call" | custom-call | tf_op jit(solution)/shard_map/place_keys/pallas_call | solution.py:437
  62.4 0.0 collective-permute-done.12.refs_3_
  62.5 0.0 collective-permute-done.13.refs_4_
  62.5 0.0 collective-permute-done.14.refs_5_
  62.5 3.5 %collective-permute-done.15.refs_6_ = bf16[96,256]{1,0:T(8,128)(2,1)S(1)} collective-permute-done((bf16[96,256]{1,0:T(8,128)(2,1)}, bf16[96,256]{1,0:T(8,128)(2,1)S(1)}, u32[]{:S(2)}, u32[]{:S(2)}) %collective-permute-start.15) | collective-permute-done | bytes 49184 | tf_op jit(solution)/shard_map/ppermute | solution.py:587
  66.0 0.0 collective-permute-done.9.refs_0_
  66.0 1.0 %place_values.1 = bf16[256,256]{1,0:T(8,128)(2,1)} custom-call(s32[8,8,128]{2,1,0:T(8,128)S(1)} %get-tuple-element.45.slots_ref, f32[256,256]{1,0:T(8,128)S(1)} %get-tuple-element.46.started_ref, bf16[96,256]{1,0:T(8,128)(2,1)S(1)} %collective-permute-done.9.refs_0_, bf16[96,256]{1,0:T(8,128)(2,1)S(1)} %collective-permute-done.10.refs_1_, ...), custom_call_target="tpu_custom_call" | custom-call | tf_op jit(solution)/shard_map/place_values/pallas_call | solution.py:462
  (2 shorter events, 0.0 us)
Async XLA Ops:
  0.6 7.1 %collective-permute-start = (bf16[640,2560]{1,0:T(8,128)(2,1)}, bf16[640,2560]{1,0:T(8,128)(2,1)}, u32[]{:S(2)}, u32[]{:S(2)}) collective-permute-start(bf16[640,2560]{1,0:T(8,128)(2,1)} %refs_0_.7), channel_id=1, source_target_pairs={{0,1},{1,0},{2,3},{3,2},{4,5},{5,4},{6,7},{7,6},{8,9},{9,8},{10,11... | collective-permute-start | bytes 9830408 | tf_op jit(solution)/shard_map/ppermute | solution.py:494
  2.9 12.6 %collective-permute-start.1 = (bf16[640,256]{1,0:T(8,128)(2,1)}, bf16[640,256]{1,0:T(8,128)(2,1)S(1)}, u32[]{:S(2)}, u32[]{:S(2)}) collective-permute-start(bf16[640,256]{1,0:T(8,128)(2,1)} %cut_quarters.3), channel_id=1, source_target_pairs={{0,2},{2,0},{1,3},{3,1},{4,6},{6,4},{5,7},{7,5},{8,10},{10,8},{9,1... | collective-permute-start | bytes 983048 | tf_op jit(solution)/shard_map/ppermute | solution.py:509
  7.6 13.4 %collective-permute-start.5 = (bf16[640,256]{1,0:T(8,128)(2,1)}, bf16[640,256]{1,0:T(8,128)(2,1)S(1)}, u32[]{:S(2)}, u32[]{:S(2)}) collective-permute-start(bf16[640,256]{1,0:T(8,128)(2,1)} %get-tuple-element.40), channel_id=1, source_target_pairs={{0,2},{2,0},{1,3},{3,1},{4,6},{6,4},{5,7},{7,5},{8,10},{10,8},{9,1... | collective-permute-start | bytes 983048 | tf_op jit(solution)/shard_map/ppermute | solution.py:510
  7.7 17.1 %copy-start.1 = (s32[640]{0:T(1024)S(1)}, s32[640]{0:T(1024)}, u32[]{:S(2)}) copy-start(s32[640]{0:T(1024)} %param.16) | copy-start | bytes 7684
  7.7 19.8 %copy-start.3 = (bf16[640,256]{1,0:T(8,128)(2,1)S(1)}, bf16[640,256]{1,0:T(8,128)(2,1)}, u32[]{:S(2)}) copy-start(bf16[640,256]{1,0:T(8,128)(2,1)} %get-tuple-element.42) | copy-start | bytes 983044
  15.5 13.6 %copy-start.4 = (bf16[640,256]{1,0:T(8,128)(2,1)}, bf16[640,256]{1,0:T(8,128)(2,1)S(1)}, u32[]{:S(2)}) copy-start(bf16[640,256]{1,0:T(8,128)(2,1)S(1)} %collective-permute-done.1.refs_4_) | copy-start | bytes 983044
  15.5 12.1 %collective-permute-start.2 = (bf16[640,256]{1,0:T(8,128)(2,1)S(1)}, bf16[640,256]{1,0:T(8,128)(2,1)}, u32[]{:S(2)}, u32[]{:S(2)}) collective-permute-start(bf16[640,256]{1,0:T(8,128)(2,1)S(1)} %collective-permute-done.1.refs_4_), channel_id=1, source_target_pairs={{0,16},{16,0},{1,17},{17,1},{2,18},{18,2},{3,19},{19,3},{4,20},{20... | collective-permute-start | bytes 983048 | tf_op jit(solution)/shard_map/ppermute | solution.py:529
  17.7 11.4 %collective-permute-start.3 = (bf16[640,256]{1,0:T(8,128)(2,1)S(1)}, bf16[640,256]{1,0:T(8,128)(2,1)}, u32[]{:S(2)}, u32[]{:S(2)}) collective-permute-start(bf16[640,256]{1,0:T(8,128)(2,1)S(1)} %collective-permute-done.1.refs_4_), channel_id=1, source_target_pairs={{0,4},{4,0},{8,12},{12,8},{1,5},{5,1},{9,13},{13,9},{2,6},{6,2},{1... | collective-permute-start | bytes 983048 | tf_op jit(solution)/shard_map/ppermute | solution.py:530
  19.3 9.8 %collective-permute-start.4 = (bf16[640,256]{1,0:T(8,128)(2,1)}, bf16[640,256]{1,0:T(8,128)(2,1)}, u32[]{:S(2)}, u32[]{:S(2)}) collective-permute-start(bf16[640,256]{1,0:T(8,128)(2,1)} %get-tuple-element.35), channel_id=1, source_target_pairs={{0,2},{2,0},{1,3},{3,1},{4,6},{6,4},{5,7},{7,5},{8,10},{10,8},{9,1... | collective-permute-start | bytes 983048 | tf_op jit(solution)/shard_map/ppermute | solution.py:512
  21.0 8.0 %copy-start.2 = (bf16[640,256]{1,0:T(8,128)(2,1)}, bf16[640,256]{1,0:T(8,128)(2,1)S(1)}, u32[]{:S(2)}) copy-start(bf16[640,256]{1,0:T(8,128)(2,1)S(1)} %collective-permute-done.5.refs_13_.refs_4_) | copy-start | bytes 983044
  21.0 20.7 %collective-permute-start.6 = (bf16[640,256]{1,0:T(8,128)(2,1)S(1)}, bf16[640,256]{1,0:T(8,128)(2,1)S(1)}, u32[]{:S(2)}, u32[]{:S(2)}) collective-permute-start(bf16[640,256]{1,0:T(8,128)(2,1)S(1)} %collective-permute-done.5.refs_13_.refs_4_), channel_id=1, source_target_pairs={{0,16},{16,0},{1,17},{17,1},{2,18},{18,2},{3,19},{19,3},{4,20},{20... | collective-permute-start | bytes 983048 | tf_op jit(solution)/shard_map/ppermute | solution.py:529
  23.2 18.5 %collective-permute-start.7 = (bf16[640,256]{1,0:T(8,128)(2,1)S(1)}, bf16[640,256]{1,0:T(8,128)(2,1)S(1)}, u32[]{:S(2)}, u32[]{:S(2)}) collective-permute-start(bf16[640,256]{1,0:T(8,128)(2,1)S(1)} %collective-permute-done.5.refs_13_.refs_4_), channel_id=1, source_target_pairs={{0,4},{4,0},{8,12},{12,8},{1,5},{5,1},{9,13},{13,9},{2,6},{6,2},{1... | collective-permute-start | bytes 983048 | tf_op jit(solution)/shard_map/ppermute | solution.py:530
  27.6 14.2 %collective-permute-start.8 = (bf16[640,256]{1,0:T(8,128)(2,1)S(1)}, bf16[640,256]{1,0:T(8,128)(2,1)}, u32[]{:S(2)}, u32[]{:S(2)}) collective-permute-start(bf16[640,256]{1,0:T(8,128)(2,1)S(1)} %copy-done.3), channel_id=1, source_target_pairs={{0,2},{2,0},{1,3},{3,1},{4,6},{6,4},{5,7},{7,5},{8,10},{10,8},{9,1... | collective-permute-start | bytes 983048 | tf_op jit(solution)/shard_map/ppermute | solution.py:513
  36.2 24.3 %all-to-all-start = ((bf16[8,112,256]{2,1,0:T(8,128)(2,1)}), bf16[8,112,256]{2,1,0:T(8,128)(2,1)S(1)}, u32[]{:S(2)}, u32[]{:S(2)}) async-start(bf16[8,112,256]{2,1,0:T(8,128)(2,1)} %far_part.2.refs_10_), calls=%async_computation | async-start | bytes 917504 | tf_op jit(solution)/shard_map/all_to_all | solution.py:492
  41.7 0.7 %copy-start.5 = (bf16[640,256]{1,0:T(8,128)(2,1)}, bf16[640,256]{1,0:T(8,128)(2,1)S(1)}, u32[]{:S(2)}) copy-start(bf16[640,256]{1,0:T(8,128)(2,1)S(1)} %collective-permute-done.6.refs_5_) | copy-start | bytes 983044
  41.8 0.8 %copy-start.6 = (bf16[640,256]{1,0:T(8,128)(2,1)}, bf16[640,256]{1,0:T(8,128)(2,1)S(1)}, u32[]{:S(2)}) copy-start(bf16[640,256]{1,0:T(8,128)(2,1)S(1)} %collective-permute-done.7.refs_6_) | copy-start | bytes 983044
  49.2 9.7 %collective-permute-start.10 = (bf16[96,256]{1,0:T(8,128)(2,1)}, bf16[96,256]{1,0:T(8,128)(2,1)S(1)}, u32[]{:S(2)}, u32[]{:S(2)}) collective-permute-start(bf16[96,256]{1,0:T(8,128)(2,1)} %get-tuple-element.48), channel_id=1, source_target_pairs={{0,4},{2,6},{4,0},{6,2},{8,12},{10,14},{12,8},{14,10},{1,5},{3,7},... | collective-permute-start | bytes 147464 | tf_op jit(solution)/shard_map/ppermute | solution.py:587
  51.3 9.1 %collective-permute-start.11 = (bf16[96,256]{1,0:T(8,128)(2,1)}, bf16[96,256]{1,0:T(8,128)(2,1)S(1)}, u32[]{:S(2)}, u32[]{:S(2)}) collective-permute-start(bf16[96,256]{1,0:T(8,128)(2,1)} %get-tuple-element.49), channel_id=1, source_target_pairs={{0,6},{2,4},{4,2},{6,0},{8,14},{10,12},{12,10},{14,8},{1,7},{3,5},... | collective-permute-start | bytes 147464 | tf_op jit(solution)/shard_map/ppermute | solution.py:587
  52.8 9.7 %collective-permute-start.12 = (bf16[96,256]{1,0:T(8,128)(2,1)}, bf16[96,256]{1,0:T(8,128)(2,1)S(1)}, u32[]{:S(2)}, u32[]{:S(2)}) collective-permute-start(bf16[96,256]{1,0:T(8,128)(2,1)} %get-tuple-element.50), channel_id=1, source_target_pairs={{0,8},{2,10},{4,12},{6,14},{8,0},{10,2},{12,4},{14,6},{1,9},{3,11}... | collective-permute-start | bytes 147464 | tf_op jit(solution)/shard_map/ppermute | solution.py:587
  55.2 7.3 %collective-permute-start.13 = (bf16[96,256]{1,0:T(8,128)(2,1)}, bf16[96,256]{1,0:T(8,128)(2,1)S(1)}, u32[]{:S(2)}, u32[]{:S(2)}) collective-permute-start(bf16[96,256]{1,0:T(8,128)(2,1)} %get-tuple-element.51), channel_id=1, source_target_pairs={{0,10},{2,8},{4,14},{6,12},{8,2},{10,0},{12,6},{14,4},{1,11},{3,9}... | collective-permute-start | bytes 147464 | tf_op jit(solution)/shard_map/ppermute | solution.py:587
  55.2 7.2 %collective-permute-start.14 = (bf16[96,256]{1,0:T(8,128)(2,1)}, bf16[96,256]{1,0:T(8,128)(2,1)S(1)}, u32[]{:S(2)}, u32[]{:S(2)}) collective-permute-start(bf16[96,256]{1,0:T(8,128)(2,1)} %get-tuple-element.52), channel_id=1, source_target_pairs={{0,12},{2,14},{4,8},{6,10},{8,4},{10,6},{12,0},{14,2},{1,13},{3,15... | collective-permute-start | bytes 147464 | tf_op jit(solution)/shard_map/ppermute | solution.py:587
  59.0 7.0 %collective-permute-start.15 = (bf16[96,256]{1,0:T(8,128)(2,1)}, bf16[96,256]{1,0:T(8,128)(2,1)S(1)}, u32[]{:S(2)}, u32[]{:S(2)}) collective-permute-start(bf16[96,256]{1,0:T(8,128)(2,1)} %get-tuple-element.53), channel_id=1, source_target_pairs={{0,14},{2,12},{4,10},{6,8},{8,6},{10,4},{12,2},{14,0},{1,15},{3,13... | collective-permute-start | bytes 147464 | tf_op jit(solution)/shard_map/ppermute | solution.py:587
  60.5 5.5 %collective-permute-start.9 = (bf16[96,256]{1,0:T(8,128)(2,1)}, bf16[96,256]{1,0:T(8,128)(2,1)S(1)}, u32[]{:S(2)}, u32[]{:S(2)}) collective-permute-start(bf16[96,256]{1,0:T(8,128)(2,1)} %get-tuple-element.47), channel_id=1, source_target_pairs={{0,2},{2,0},{4,6},{6,4},{8,10},{10,8},{12,14},{14,12},{1,3},{3,1},... | collective-permute-start | bytes 147464 | tf_op jit(solution)/shard_map/ppermute | solution.py:587
  60.5 0.8 %copy-start = (bf16[96,256]{1,0:T(8,128)(2,1)S(1)}, bf16[96,256]{1,0:T(8,128)(2,1)}, u32[]{:S(2)}) copy-start(bf16[96,256]{1,0:T(8,128)(2,1)} %get-tuple-element.43.values_ref) | copy-start | bytes 147460

commit v5 on v4

--- a/solution.py
+++ b/solution.py
@@ -15,7 +15,7 @@
 
 epsilon = 1e-05
 rope_base = 1000000.0
-VMEM_BYTES = 62 * 1024 * 1024
+VMEM_BYTES = 63 * 1024 * 1024
 VMEM_PLACE = 16 * 1024 * 1024
 NEAR_STEP = 128
 NEAR_AHEAD = 4

time: 67.5 us -> 66.5 us (0.985)
  local copies, waits for them, and re-layouts: 1.62 us -> 0.81 us
    unnamed x14 -> x8, local copies, waits for them, and re-layouts: 1.62 us -> 0.81 us
  transfers between devices with their start and end apart: 17 -> 17, of which waited for: 2 -> 2; matrix products, arithmetic and copies ran while one was open for 2% -> 2% of each run, Pallas kernels for 42% -> 43%
where the time goes in v5:
time: 66.5 us; the launch traced here: 66 us
  starting transfers between devices  30.4 us (46%)
  Pallas kernels  29.2 us (44%)
  waiting for transfers between devices  3.82 us (6%)
  other arithmetic  1.04 us (2%)
  local copies, waits for them, and re-layouts  0.81 us (1%)
  between operations  0.74 us (1%)
    pallas_call x2, Pallas kernels, far_part(): pl.pallas_call(functools.partial(far_kernel, relayed, bool(angles), tall,...  13.8 us
    ppermute x7, starting transfers between devices, local(): lax.ppermute(send_values[other], axes, [(i, i ^ other) for i in range(dev...  11.3 us
    pallas_call x1, Pallas kernels, near_part(): pl.pallas_call(near_kernel, out_shape=(sums, sums, jax.ShapeDtypeStruct((...  7.69 us
    all_to_all x1, starting transfers between devices, exchange(): lax.all_to_all(rows_by_owner, axes, split_axis=0, concat_axis=0, tiled=True)  5.34 us
    ppermute x2, starting transfers between devices, pieces_of(): by_group = lax.ppermute(own, 'groups', swap)  4.39 us
    pallas_call x2, Pallas kernels, cut_quarters(): pl.pallas_call(functools.partial(cut_kernel, opposite), out_shape=(piece,...  3.86 us
    ppermute x7, waiting for transfers between devices, local(): lax.ppermute(send_values[other], axes, [(i, i ^ other) for i in range(dev...  3.54 us
    ppermute x2, starting transfers between devices, pieces_of(): by_rep = lax.ppermute(own, 'rep', across)  3.15 us
  transfers between devices with their start and end apart: 17, of which 2 were waited for; matrix products, arithmetic and copies ran while one was open for 2% of the time, Pallas kernels for 43%

profile of v5, /device:TPU:0, one launch (start us, length us, event | category | flops | bytes accessed | tf_op | source)
XLA Modules:
  0.0 66.0 jit_solution(4314435659560116060)
XLA Ops:
  0.6 0.5 collective-permute-start
  1.1 1.7 %cut_quarters.3 = bf16[640,256]{1,0:T(8,128)(2,1)} custom-call(bf16[2560,256]{1,0:T(8,128)(2,1)} %refs_0_.5), custom_call_target="tpu_custom_call" | custom-call | tf_op jit(solution)/shard_map/cut_quarters/pallas_call | solution.py:77
  2.9 2.6 %collective-permute-start.1 = (bf16[640,256]{1,0:T(8,128)(2,1)}, bf16[640,256]{1,0:T(8,128)(2,1)S(1)}, u32[]{:S(2)}, u32[]{:S(2)}) collective-permute-start(bf16[640,256]{1,0:T(8,128)(2,1)} %cut_quarters.3), channel_id=1, source_target_pairs={{0,2},{2,0},{1,3},{3,1},{4,6},{6,4},{5,7},{7,5},{8,10},{10,8},{9,1... | collective-permute-start | bytes 983048 | tf_op jit(solution)/shard_map/ppermute | solution.py:509
  5.4 2.2 %cut_quarters.2 = (bf16[640,256]{1,0:T(8,128)(2,1)}, bf16[640,256]{1,0:T(8,128)(2,1)}, bf16[640,256]{1,0:T(8,128)(2,1)}) custom-call(bf16[2560,256]{1,0:T(8,128)(2,1)} %value_ref.1, bf16[2560,256]{1,0:T(8,128)(2,1)} %refs_0_.5, bf16[2560,256]{1,0:T(8,128)(2,1)} %value_ref.1), custom_call_target="tpu_custom_call" | custom-call | tf_op jit(solution)/shard_map/cut_quarters/pallas_call | solution.py:77
  7.6 0.1 collective-permute-start.5
  7.7 0.0 collective-permute-done.got_ref.refs_1_
  7.7 0.0 copy-start.1
  7.7 7.7 %near_part.1 = (f32[640,256]{1,0:T(8,128)}, f32[640,256]{1,0:T(8,128)}, f32[640,128]{1,0:T(8,128)}) custom-call(bf16[640,2560]{1,0:T(8,128)(2,1)} %refs_0_.7, bf16[640,2560]{1,0:T(8,128)(2,1)} %collective-permute-done.got_ref.refs_1_, bf16[2560,256]{1,0:T(8,128)(2,1)} %refs_0_.5, bf16[2560,256]{1,0:T(8,128)(2,1)} %value_ref.1, bf16[5120]{0:T(1024)(128)(2,1)} %refs_8_.3, ...), custom_call_target="tpu_custom_call" | custom-call | flops 20000000000 | bytes 12451840 | tf_op jit(solution)/shard_map/near_part/pallas_call | solution.py:192
  15.4 0.0 collective-permute-done.1.refs_4_
  15.4 0.0 copy-start.3
  15.4 2.2 %collective-permute-start.2 = (bf16[640,256]{1,0:T(8,128)(2,1)S(1)}, bf16[640,256]{1,0:T(8,128)(2,1)}, u32[]{:S(2)}, u32[]{:S(2)}) collective-permute-start(bf16[640,256]{1,0:T(8,128)(2,1)S(1)} %collective-permute-done.1.refs_4_), channel_id=1, source_target_pairs={{0,16},{16,0},{1,17},{17,1},{2,18},{18,2},{3,19},{19,3},{4,20},{20... | collective-permute-start | bytes 983048 | tf_op jit(solution)/shard_map/ppermute | solution.py:529
  17.6 1.6 %collective-permute-start.3 = (bf16[640,256]{1,0:T(8,128)(2,1)S(1)}, bf16[640,256]{1,0:T(8,128)(2,1)}, u32[]{:S(2)}, u32[]{:S(2)}) collective-permute-start(bf16[640,256]{1,0:T(8,128)(2,1)S(1)} %collective-permute-done.1.refs_4_), channel_id=1, source_target_pairs={{0,4},{4,0},{8,12},{12,8},{1,5},{5,1},{9,13},{13,9},{2,6},{6,2},{1... | collective-permute-start | bytes 983048 | tf_op jit(solution)/shard_map/ppermute | solution.py:530
  19.2 1.5 %collective-permute-start.4 = (bf16[640,256]{1,0:T(8,128)(2,1)}, bf16[640,256]{1,0:T(8,128)(2,1)}, u32[]{:S(2)}, u32[]{:S(2)}) collective-permute-start(bf16[640,256]{1,0:T(8,128)(2,1)} %get-tuple-element.35), channel_id=1, source_target_pairs={{0,2},{2,0},{1,3},{3,1},{4,6},{6,4},{5,7},{7,5},{8,10},{10,8},{9,1... | collective-permute-start | bytes 983048 | tf_op jit(solution)/shard_map/ppermute | solution.py:512
  20.8 0.3 collective-permute-done.5.refs_13_.refs_4_
  21.0 0.0 copy-start.2
  21.0 2.2 %collective-permute-start.6 = (bf16[640,256]{1,0:T(8,128)(2,1)S(1)}, bf16[640,256]{1,0:T(8,128)(2,1)}, u32[]{:S(2)}, u32[]{:S(2)}) collective-permute-start(bf16[640,256]{1,0:T(8,128)(2,1)S(1)} %collective-permute-done.5.refs_13_.refs_4_), channel_id=1, source_target_pairs={{0,16},{16,0},{1,17},{17,1},{2,18},{18,2},{3,19},{19,3},{4,20},{20... | collective-permute-start | bytes 983048 | tf_op jit(solution)/shard_map/ppermute | solution.py:529
  23.2 1.6 %collective-permute-start.7 = (bf16[640,256]{1,0:T(8,128)(2,1)S(1)}, bf16[640,256]{1,0:T(8,128)(2,1)}, u32[]{:S(2)}, u32[]{:S(2)}) collective-permute-start(bf16[640,256]{1,0:T(8,128)(2,1)S(1)} %collective-permute-done.5.refs_13_.refs_4_), channel_id=1, source_target_pairs={{0,4},{4,0},{8,12},{12,8},{1,5},{5,1},{9,13},{13,9},{2,6},{6,2},{1... | collective-permute-start | bytes 983048 | tf_op jit(solution)/shard_map/ppermute | solution.py:530
  24.8 0.0 copy-done.1
  24.8 1.7 %route.1 = (s32[8,640]{1,0:T(8,128)}, bf16[8,16,256]{2,1,0:T(8,128)(2,1)}) custom-call(s32[8]{0:T(128)} %counts_ref.1, s32[640]{0:T(1024)} %dest_ref.1, f32[640,256]{1,0:T(8,128)} %get-tuple-element.41.after_ref.refs_2_), custom_call_target="tpu_custom_call" | custom-call | tf_op jit(solution)/shard_map/route/pallas_call | solution.py:395
  26.5 1.0 %multiply_sine_fusion = (f32[32,640]{1,0:T(8,128)}, f32[32,640]{1,0:T(8,128)}) fusion(f32[640]{0:T(1024)S(1)} %convert_element_type.3, f32[32]{0:T(128)S(1)} %multiply_power_fusion), kind=kLoop, calls=%fused_computation | loop fusion | flops 20480 | bytes 166528 | tf_op jit(solution)/shard_map/sin | solution.py:53
  27.5 0.0 collective-permute-done.2.refs_5_
  27.5 1.5 %collective-permute-start.8 = (bf16[640,256]{1,0:T(8,128)(2,1)}, bf16[640,256]{1,0:T(8,128)(2,1)}, u32[]{:S(2)}, u32[]{:S(2)}) collective-permute-start(bf16[640,256]{1,0:T(8,128)(2,1)} %get-tuple-element.42), channel_id=1, source_target_pairs={{0,2},{2,0},{1,3},{3,1},{4,6},{6,4},{5,7},{7,5},{8,10},{10,8},{9,1... | collective-permute-start | bytes 983048 | tf_op jit(solution)/shard_map/ppermute | solution.py:513
  29.0 0.0 collective-permute-done.3.refs_6_
  29.0 0.0 collective-permute-done.4.refs_7_
  29.0 0.0 copy-done.3
  29.1 0.0 copy-done.2
  29.1 7.1 %far_part.2.refs_10_ = bf16[8,112,256]{2,1,0:T(8,128)(2,1)} custom-call(bf16[640,2560]{1,0:T(8,128)(2,1)} %refs_0_.7, bf16[640,2560]{1,0:T(8,128)(2,1)} %collective-permute-done.got_ref.refs_1_, f32[640,256]{1,0:T(8,128)} %get-tuple-element.31.refs_2_, f32[640,128]{1,0:T(8,128)} %get-tuple-element.32.refs_3_, bf16[640,256]{1,0:T(8,128)(2,1)} %copy-done.3, ...), custom_call_target="tpu_custom_call" | custom-call | flops 20000000000 | bytes 1966080 | tf_op jit(solution)/shard_map/far_part/pallas_call | solution.py:335
  36.2 5.3 %all-to-all-start = ((bf16[8,112,256]{2,1,0:T(8,128)(2,1)}), bf16[8,112,256]{2,1,0:T(8,128)(2,1)S(1)}, u32[]{:S(2)}, u32[]{:S(2)}) async-start(bf16[8,112,256]{2,1,0:T(8,128)(2,1)} %far_part.2.refs_10_), calls=%async_computation | async-start | bytes 917504 | tf_op jit(solution)/shard_map/all_to_all | solution.py:492
  41.5 0.0 collective-permute-done.6.refs_5_
  41.5 0.0 collective-permute-done.7.refs_6_
  41.6 0.0 collective-permute-done.8.refs_7_
  41.6 6.7 %far_part.3 = (bf16[96,256]{1,0:T(8,128)(2,1)}, bf16[96,256]{1,0:T(8,128)(2,1)}, bf16[96,256]{1,0:T(8,128)(2,1)}, bf16[96,256]{1,0:T(8,128)(2,1)}, bf16[96,256]{...) custom-call(bf16[640,2560]{1,0:T(8,128)(2,1)} %refs_0_.7, ...), custom_call_target="tpu_custom_call" | custom-call | flops 20000000000 | bytes 1966080 | tf_op jit(solution)/shard_map/far_part/pallas_call | solution.py:335
  48.2 2.1 %collective-permute-start.10 = (bf16[96,256]{1,0:T(8,128)(2,1)}, bf16[96,256]{1,0:T(8,128)(2,1)S(1)}, u32[]{:S(2)}, u32[]{:S(2)}) collective-permute-start(bf16[96,256]{1,0:T(8,128)(2,1)} %get-tuple-element.48), channel_id=1, source_target_pairs={{0,4},{2,6},{4,0},{6,2},{8,12},{10,14},{12,8},{14,10},{1,5},{3,7},... | collective-permute-start | bytes 147464 | tf_op jit(solution)/shard_map/ppermute | solution.py:587
  50.3 1.5 %collective-permute-start.11 = (bf16[96,256]{1,0:T(8,128)(2,1)}, bf16[96,256]{1,0:T(8,128)(2,1)S(1)}, u32[]{:S(2)}, u32[]{:S(2)}) collective-permute-start(bf16[96,256]{1,0:T(8,128)(2,1)} %get-tuple-element.49), channel_id=1, source_target_pairs={{0,6},{2,4},{4,2},{6,0},{8,14},{10,12},{12,10},{14,8},{1,7},{3,5},... | collective-permute-start | bytes 147464 | tf_op jit(solution)/shard_map/ppermute | solution.py:587
  51.8 2.4 %collective-permute-start.12 = (bf16[96,256]{1,0:T(8,128)(2,1)}, bf16[96,256]{1,0:T(8,128)(2,1)S(1)}, u32[]{:S(2)}, u32[]{:S(2)}) collective-permute-start(bf16[96,256]{1,0:T(8,128)(2,1)} %get-tuple-element.50), channel_id=1, source_target_pairs={{0,8},{2,10},{4,12},{6,14},{8,0},{10,2},{12,4},{14,6},{1,9},{3,11}... | collective-permute-start | bytes 147464 | tf_op jit(solution)/shard_map/ppermute | solution.py:587
  54.2 0.1 collective-permute-start.13
  54.2 3.7 %collective-permute-start.14 = (bf16[96,256]{1,0:T(8,128)(2,1)}, bf16[96,256]{1,0:T(8,128)(2,1)S(1)}, u32[]{:S(2)}, u32[]{:S(2)}) collective-permute-start(bf16[96,256]{1,0:T(8,128)(2,1)} %get-tuple-element.52), channel_id=1, source_target_pairs={{0,12},{2,14},{4,8},{6,10},{8,4},{10,6},{12,0},{14,2},{1,13},{3,15... | collective-permute-start | bytes 147464 | tf_op jit(solution)/shard_map/ppermute | solution.py:587
  58.0 0.0 collective-permute-done.10.refs_1_
  58.0 1.5 %collective-permute-start.15 = (bf16[96,256]{1,0:T(8,128)(2,1)}, bf16[96,256]{1,0:T(8,128)(2,1)S(1)}, u32[]{:S(2)}, u32[]{:S(2)}) collective-permute-start(bf16[96,256]{1,0:T(8,128)(2,1)} %get-tuple-element.53), channel_id=1, source_target_pairs={{0,14},{2,12},{4,10},{6,8},{8,6},{10,4},{12,2},{14,0},{1,15},{3,13... | collective-permute-start | bytes 147464 | tf_op jit(solution)/shard_map/ppermute | solution.py:587
  59.4 0.0 collective-permute-done.11.refs_2_
  59.4 0.1 collective-permute-start.9
  59.5 0.0 all-to-all-done.came_ref
  59.5 0.0 copy-start
  59.5 0.8 %copy-done = bf16[96,256]{1,0:T(8,128)(2,1)S(1)} copy-done((bf16[96,256]{1,0:T(8,128)(2,1)S(1)}, bf16[96,256]{1,0:T(8,128)(2,1)}, u32[]{:S(2)}) %copy-start) | copy-done | bytes 49176
  60.3 1.1 %place_keys.1 = (s32[8,8,128]{2,1,0:T(8,128)S(1)}, f32[256,256]{1,0:T(8,128)S(1)}, bf16[256,256]{1,0:T(8,128)(2,1)}) custom-call(bf16[8,112,256]{2,1,0:T(8,128)(2,1)S(1)} %all-to-all-done.came_ref, bf16[96,256]{1,0:T(8,128)(2,1)S(1)} %copy-done), custom_call_target="tpu_custom_call" | custom-call | tf_op jit(solution)/shard_map/place_keys/pallas_call | solution.py:437
  61.4 0.0 collective-permute-done.12.refs_3_
  61.4 0.0 collective-permute-done.13.refs_4_
  61.4 0.0 collective-permute-done.14.refs_5_
  61.5 3.5 %collective-permute-done.15.refs_6_ = bf16[96,256]{1,0:T(8,128)(2,1)S(1)} collective-permute-done((bf16[96,256]{1,0:T(8,128)(2,1)}, bf16[96,256]{1,0:T(8,128)(2,1)S(1)}, u32[]{:S(2)}, u32[]{:S(2)}) %collective-permute-start.15) | collective-permute-done | bytes 49184 | tf_op jit(solution)/shard_map/ppermute | solution.py:587
  65.0 0.0 collective-permute-done.9.refs_0_
  65.0 1.0 %place_values.1 = bf16[256,256]{1,0:T(8,128)(2,1)} custom-call(s32[8,8,128]{2,1,0:T(8,128)S(1)} %get-tuple-element.45.slots_ref, f32[256,256]{1,0:T(8,128)S(1)} %get-tuple-element.46.started_ref, bf16[96,256]{1,0:T(8,128)(2,1)S(1)} %collective-permute-done.9.refs_0_, bf16[96,256]{1,0:T(8,128)(2,1)S(1)} %collective-permute-done.10.refs_1_, ...), custom_call_target="tpu_custom_call" | custom-call | tf_op jit(solution)/shard_map/place_values/pallas_call | solution.py:462
  (2 shorter events, 0.0 us)
Async XLA Ops:
  0.6 7.1 %collective-permute-start = (bf16[640,2560]{1,0:T(8,128)(2,1)}, bf16[640,2560]{1,0:T(8,128)(2,1)}, u32[]{:S(2)}, u32[]{:S(2)}) collective-permute-start(bf16[640,2560]{1,0:T(8,128)(2,1)} %refs_0_.7), channel_id=1, source_target_pairs={{0,1},{1,0},{2,3},{3,2},{4,5},{5,4},{6,7},{7,6},{8,9},{9,8},{10,11... | collective-permute-start | bytes 9830408 | tf_op jit(solution)/shard_map/ppermute | solution.py:494
  2.9 12.6 %collective-permute-start.1 = (bf16[640,256]{1,0:T(8,128)(2,1)}, bf16[640,256]{1,0:T(8,128)(2,1)S(1)}, u32[]{:S(2)}, u32[]{:S(2)}) collective-permute-start(bf16[640,256]{1,0:T(8,128)(2,1)} %cut_quarters.3), channel_id=1, source_target_pairs={{0,2},{2,0},{1,3},{3,1},{4,6},{6,4},{5,7},{7,5},{8,10},{10,8},{9,1... | collective-permute-start | bytes 983048 | tf_op jit(solution)/shard_map/ppermute | solution.py:509
  7.6 13.4 %collective-permute-start.5 = (bf16[640,256]{1,0:T(8,128)(2,1)}, bf16[640,256]{1,0:T(8,128)(2,1)S(1)}, u32[]{:S(2)}, u32[]{:S(2)}) collective-permute-start(bf16[640,256]{1,0:T(8,128)(2,1)} %get-tuple-element.40), channel_id=1, source_target_pairs={{0,2},{2,0},{1,3},{3,1},{4,6},{6,4},{5,7},{7,5},{8,10},{10,8},{9,1... | collective-permute-start | bytes 983048 | tf_op jit(solution)/shard_map/ppermute | solution.py:510
  7.7 17.1 %copy-start.1 = (s32[640]{0:T(1024)S(1)}, s32[640]{0:T(1024)}, u32[]{:S(2)}) copy-start(s32[640]{0:T(1024)} %param.16) | copy-start | bytes 7684
  15.4 13.6 %copy-start.3 = (bf16[640,256]{1,0:T(8,128)(2,1)}, bf16[640,256]{1,0:T(8,128)(2,1)S(1)}, u32[]{:S(2)}) copy-start(bf16[640,256]{1,0:T(8,128)(2,1)S(1)} %collective-permute-done.1.refs_4_) | copy-start | bytes 983044
  15.4 12.1 %collective-permute-start.2 = (bf16[640,256]{1,0:T(8,128)(2,1)S(1)}, bf16[640,256]{1,0:T(8,128)(2,1)}, u32[]{:S(2)}, u32[]{:S(2)}) collective-permute-start(bf16[640,256]{1,0:T(8,128)(2,1)S(1)} %collective-permute-done.1.refs_4_), channel_id=1, source_target_pairs={{0,16},{16,0},{1,17},{17,1},{2,18},{18,2},{3,19},{19,3},{4,20},{20... | collective-permute-start | bytes 983048 | tf_op jit(solution)/shard_map/ppermute | solution.py:529
  17.6 11.4 %collective-permute-start.3 = (bf16[640,256]{1,0:T(8,128)(2,1)S(1)}, bf16[640,256]{1,0:T(8,128)(2,1)}, u32[]{:S(2)}, u32[]{:S(2)}) collective-permute-start(bf16[640,256]{1,0:T(8,128)(2,1)S(1)} %collective-permute-done.1.refs_4_), channel_id=1, source_target_pairs={{0,4},{4,0},{8,12},{12,8},{1,5},{5,1},{9,13},{13,9},{2,6},{6,2},{1... | collective-permute-start | bytes 983048 | tf_op jit(solution)/shard_map/ppermute | solution.py:530
  19.2 9.8 %collective-permute-start.4 = (bf16[640,256]{1,0:T(8,128)(2,1)}, bf16[640,256]{1,0:T(8,128)(2,1)}, u32[]{:S(2)}, u32[]{:S(2)}) collective-permute-start(bf16[640,256]{1,0:T(8,128)(2,1)} %get-tuple-element.35), channel_id=1, source_target_pairs={{0,2},{2,0},{1,3},{3,1},{4,6},{6,4},{5,7},{7,5},{8,10},{10,8},{9,1... | collective-permute-start | bytes 983048 | tf_op jit(solution)/shard_map/ppermute | solution.py:512
  21.0 8.0 %copy-start.2 = (bf16[640,256]{1,0:T(8,128)(2,1)}, bf16[640,256]{1,0:T(8,128)(2,1)S(1)}, u32[]{:S(2)}) copy-start(bf16[640,256]{1,0:T(8,128)(2,1)S(1)} %collective-permute-done.5.refs_13_.refs_4_) | copy-start | bytes 983044
  21.0 20.5 %collective-permute-start.6 = (bf16[640,256]{1,0:T(8,128)(2,1)S(1)}, bf16[640,256]{1,0:T(8,128)(2,1)}, u32[]{:S(2)}, u32[]{:S(2)}) collective-permute-start(bf16[640,256]{1,0:T(8,128)(2,1)S(1)} %collective-permute-done.5.refs_13_.refs_4_), channel_id=1, source_target_pairs={{0,16},{16,0},{1,17},{17,1},{2,18},{18,2},{3,19},{19,3},{4,20},{20... | collective-permute-start | bytes 983048 | tf_op jit(solution)/shard_map/ppermute | solution.py:529
  23.2 18.3 %collective-permute-start.7 = (bf16[640,256]{1,0:T(8,128)(2,1)S(1)}, bf16[640,256]{1,0:T(8,128)(2,1)}, u32[]{:S(2)}, u32[]{:S(2)}) collective-permute-start(bf16[640,256]{1,0:T(8,128)(2,1)S(1)} %collective-permute-done.5.refs_13_.refs_4_), channel_id=1, source_target_pairs={{0,4},{4,0},{8,12},{12,8},{1,5},{5,1},{9,13},{13,9},{2,6},{6,2},{1... | collective-permute-start | bytes 983048 | tf_op jit(solution)/shard_map/ppermute | solution.py:530
  27.5 14.0 %collective-permute-start.8 = (bf16[640,256]{1,0:T(8,128)(2,1)}, bf16[640,256]{1,0:T(8,128)(2,1)}, u32[]{:S(2)}, u32[]{:S(2)}) collective-permute-start(bf16[640,256]{1,0:T(8,128)(2,1)} %get-tuple-element.42), channel_id=1, source_target_pairs={{0,2},{2,0},{1,3},{3,1},{4,6},{6,4},{5,7},{7,5},{8,10},{10,8},{9,1... | collective-permute-start | bytes 983048 | tf_op jit(solution)/shard_map/ppermute | solution.py:513
  36.2 23.3 %all-to-all-start = ((bf16[8,112,256]{2,1,0:T(8,128)(2,1)}), bf16[8,112,256]{2,1,0:T(8,128)(2,1)S(1)}, u32[]{:S(2)}, u32[]{:S(2)}) async-start(bf16[8,112,256]{2,1,0:T(8,128)(2,1)} %far_part.2.refs_10_), calls=%async_computation | async-start | bytes 917504 | tf_op jit(solution)/shard_map/all_to_all | solution.py:492
  48.2 9.7 %collective-permute-start.10 = (bf16[96,256]{1,0:T(8,128)(2,1)}, bf16[96,256]{1,0:T(8,128)(2,1)S(1)}, u32[]{:S(2)}, u32[]{:S(2)}) collective-permute-start(bf16[96,256]{1,0:T(8,128)(2,1)} %get-tuple-element.48), channel_id=1, source_target_pairs={{0,4},{2,6},{4,0},{6,2},{8,12},{10,14},{12,8},{14,10},{1,5},{3,7},... | collective-permute-start | bytes 147464 | tf_op jit(solution)/shard_map/ppermute | solution.py:587
  50.3 9.1 %collective-permute-start.11 = (bf16[96,256]{1,0:T(8,128)(2,1)}, bf16[96,256]{1,0:T(8,128)(2,1)S(1)}, u32[]{:S(2)}, u32[]{:S(2)}) collective-permute-start(bf16[96,256]{1,0:T(8,128)(2,1)} %get-tuple-element.49), channel_id=1, source_target_pairs={{0,6},{2,4},{4,2},{6,0},{8,14},{10,12},{12,10},{14,8},{1,7},{3,5},... | collective-permute-start | bytes 147464 | tf_op jit(solution)/shard_map/ppermute | solution.py:587
  51.8 9.7 %collective-permute-start.12 = (bf16[96,256]{1,0:T(8,128)(2,1)}, bf16[96,256]{1,0:T(8,128)(2,1)S(1)}, u32[]{:S(2)}, u32[]{:S(2)}) collective-permute-start(bf16[96,256]{1,0:T(8,128)(2,1)} %get-tuple-element.50), channel_id=1, source_target_pairs={{0,8},{2,10},{4,12},{6,14},{8,0},{10,2},{12,4},{14,6},{1,9},{3,11}... | collective-permute-start | bytes 147464 | tf_op jit(solution)/shard_map/ppermute | solution.py:587
  54.2 7.3 %collective-permute-start.13 = (bf16[96,256]{1,0:T(8,128)(2,1)}, bf16[96,256]{1,0:T(8,128)(2,1)S(1)}, u32[]{:S(2)}, u32[]{:S(2)}) collective-permute-start(bf16[96,256]{1,0:T(8,128)(2,1)} %get-tuple-element.51), channel_id=1, source_target_pairs={{0,10},{2,8},{4,14},{6,12},{8,2},{10,0},{12,6},{14,4},{1,11},{3,9}... | collective-permute-start | bytes 147464 | tf_op jit(solution)/shard_map/ppermute | solution.py:587
  54.2 7.2 %collective-permute-start.14 = (bf16[96,256]{1,0:T(8,128)(2,1)}, bf16[96,256]{1,0:T(8,128)(2,1)S(1)}, u32[]{:S(2)}, u32[]{:S(2)}) collective-permute-start(bf16[96,256]{1,0:T(8,128)(2,1)} %get-tuple-element.52), channel_id=1, source_target_pairs={{0,12},{2,14},{4,8},{6,10},{8,4},{10,6},{12,0},{14,2},{1,13},{3,15... | collective-permute-start | bytes 147464 | tf_op jit(solution)/shard_map/ppermute | solution.py:587
  58.0 7.0 %collective-permute-start.15 = (bf16[96,256]{1,0:T(8,128)(2,1)}, bf16[96,256]{1,0:T(8,128)(2,1)S(1)}, u32[]{:S(2)}, u32[]{:S(2)}) collective-permute-start(bf16[96,256]{1,0:T(8,128)(2,1)} %get-tuple-element.53), channel_id=1, source_target_pairs={{0,14},{2,12},{4,10},{6,8},{8,6},{10,4},{12,2},{14,0},{1,15},{3,13... | collective-permute-start | bytes 147464 | tf_op jit(solution)/shard_map/ppermute | solution.py:587
  59.4 5.5 %collective-permute-start.9 = (bf16[96,256]{1,0:T(8,128)(2,1)}, bf16[96,256]{1,0:T(8,128)(2,1)S(1)}, u32[]{:S(2)}, u32[]{:S(2)}) collective-permute-start(bf16[96,256]{1,0:T(8,128)(2,1)} %get-tuple-element.47), channel_id=1, source_target_pairs={{0,2},{2,0},{4,6},{6,4},{8,10},{10,8},{12,14},{14,12},{1,3},{3,1},... | collective-permute-start | bytes 147464 | tf_op jit(solution)/shard_map/ppermute | solution.py:587
  59.5 0.8 %copy-start = (bf16[96,256]{1,0:T(8,128)(2,1)S(1)}, bf16[96,256]{1,0:T(8,128)(2,1)}, u32[]{:S(2)}) copy-start(bf16[96,256]{1,0:T(8,128)(2,1)} %get-tuple-element.43.values_ref) | copy-start | bytes 147460
